TPU v7x, 32 devices: a whole 2x2x4 slice. The times are simulated.
32 devices in a mesh: groups: 2 (over y), seq: 4 (over z), rep: 2 (over x), tp: 2 (over core).
Axes of the slice: x: 2, y: 2, z: 4, core: 2. Of those that a mesh axis runs over, the one named last changes fastest.
Arguments:
- node_features: bfloat16 [4, 1024, 768], P(('groups', 'rep'), 'seq'), parts along dimension 0, may hold values from -20 to 20
- result_cotangent: bfloat16 [4, 1024, 768], P(('groups', 'rep'), 'seq', 'tp'), parts along dimension 0, may hold values from -6 to 6
- proj_weights: bfloat16 [768, 3, 768], P(None, None, 'tp'), may hold values from -2 to 2
- cluster_pairs: int32 [4, 8, 2], P(('groups', 'rep'), 'seq'), parts along dimension 0, may hold values from 0 to 7, as said below
- cluster_fill: int32 [4, 8], P(('groups', 'rep')), parts along dimension 0, may hold values from 64 to 128, as said below
- global_nodes: int32 [4, 256], P(('groups', 'rep')), parts along dimension 0, may hold values from 0 to 1023, as said below
Outputs:
- mixed_result: bfloat16 [4, 1024, 768], P(('groups', 'rep'), 'seq', 'tp'), parts along dimension 0
- grad_x: bfloat16 [4, 1024, 768], P(('groups', 'rep'), 'seq'), parts along dimension 0
- grad_w: float32 [1536, 3, 768], P(('groups', 'seq', 'rep'), None, 'tp'), parts along dimension 0
There are 2 independent parts, one for each index of `groups`. A program takes and returns all parts, laid end to end along the dimension named above; an argument that names none is the same for every part. Nothing has to cross between parts.
Inputs may be any that keep to these rules, and one draw needn't show every extreme that they name: `cluster_pairs`: cluster c holds node slots c * 128 to c * 128 + 127 and lies on shard c // 2. Entry [c, 0] is c itself and the entries of a row differ. Over the query clusters of one shard, at most one cluster of each other shard is named, and only by one of those query clusters. `cluster_fill`: some cluster of every subgraph is full. `global_nodes`: distinct real nodes.
All inputs are finite; a program needn't handle non-finite values.
Results may differ from a plain program's by a relative error of at most 0.0045.
The roundings to bfloat16 on the way count: a program that leaves them out, or rounds other values in their place, can miss the bound.
Values may be sent and summed in bfloat16 or wider, within the bound.
No kernel may reach another device: no remote copies, remote signals or barrier semaphores. Data moves between devices by JAX's collectives and lax.ppermute only.
A program may use at most 64 MiB of HBM per device.

v0:
```python
import jax
import jax.numpy as jnp
from jax import lax
from jax.sharding import PartitionSpec as P

HDIM = 64
GROUP_VERTICES = 128


NORM_EPS = 1e-06


def local(node_features, result_cotangent, proj_weights, cluster_pairs, cluster_fill, global_nodes):
    f32 = jnp.float32
    bf16 = jnp.bfloat16
    score_scale = HDIM ** (-0.5)
    features = node_features[0]
    cotangent = result_cotangent[0]
    pair_list = cluster_pairs[0]
    fill_all = cluster_fill[0]
    global_ids = global_nodes[0]
    nodes_here, feature_width = features.shape
    half_width = cotangent.shape[1]
    heads_here = half_width // HDIM
    clusters_here = nodes_here // GROUP_VERTICES
    partition_tally = lax.axis_size("seq")
    my_shard = lax.axis_index("seq")
    feats32 = features.astype(f32)
    inverse = lax.rsqrt(jnp.mean(feats32 * feats32, -1, keepdims=True) + NORM_EPS)
    normed32 = feats32 * inverse
    normed = normed32.astype(bf16)
    projected = jnp.einsum("nd,dif->nif", normed, proj_weights, preferred_element_type=f32).astype(
        bf16
    )
    quad_shape = (clusters_here, GROUP_VERTICES, heads_here, HDIM)
    queries = projected[:, 0].reshape(quad_shape)
    keys_here = projected[:, 1].reshape(quad_shape)
    values_here = projected[:, 2].reshape(quad_shape)
    cell_span = jnp.arange(GROUP_VERTICES, dtype=jnp.int32)
    fill_here = lax.dynamic_slice_in_dim(fill_all, my_shard * clusters_here, clusters_here)
    row_real = cell_span[None, :] < fill_here[:, None]
    dout = jnp.where(
        row_real[:, :, None],
        cotangent.reshape(clusters_here, GROUP_VERTICES, half_width),
        jnp.zeros((), bf16),
    ).reshape(quad_shape)
    owner_global = global_ids // nodes_here
    row_global = global_ids % nodes_here
    mine_global = owner_global == my_shard
    key_terms = jnp.where(
        mine_global[:, None], jnp.take(projected[:, 1], row_global, axis=0).astype(f32), 0.0
    )
    value_terms = jnp.where(
        mine_global[:, None], jnp.take(projected[:, 2], row_global, axis=0).astype(f32), 0.0
    )
    global_keys, global_values = (
        lax.psum(key_terms.astype(jnp.bfloat16), "seq").astype(jnp.float32),
        lax.psum(value_terms.astype(jnp.bfloat16), "seq").astype(jnp.float32),
    )
    global_keys = global_keys.astype(bf16).reshape(-1, heads_here, HDIM)
    global_values = global_values.astype(bf16).reshape(-1, heads_here, HDIM)
    owner_pair = pair_list // clusters_here
    local_pair = pair_list % clusters_here
    remote_pair = owner_pair != my_shard
    peer_ids = jnp.arange(partition_tally, dtype=jnp.int32)
    peer_match = remote_pair[None] & (owner_pair[None] == peer_ids[:, None, None])
    wanted = jnp.max(jnp.where(peer_match, local_pair[None], -1), axis=(1, 2))
    asked = lax.all_to_all(wanted[:, None], "seq", split_axis=0, concat_axis=0, tiled=True)[:, 0]
    give_mask = asked >= 0
    pick_index = jnp.maximum(asked, 0)
    key_send = jnp.take(keys_here, pick_index, axis=0).reshape(
        partition_tally, GROUP_VERTICES, half_width
    )
    value_send = jnp.take(values_here, pick_index, axis=0).reshape(
        partition_tally, GROUP_VERTICES, half_width
    )
    key_fetched, value_fetched = (
        lax.all_to_all(key_send, "seq", split_axis=0, concat_axis=0, tiled=True),
        lax.all_to_all(value_send, "seq", split_axis=0, concat_axis=0, tiled=True),
    )
    combined_keys = jnp.concatenate(
        [keys_here, key_fetched.reshape(partition_tally, GROUP_VERTICES, heads_here, HDIM)], 0
    )
    combined_values = jnp.concatenate(
        [values_here, value_fetched.reshape(partition_tally, GROUP_VERTICES, heads_here, HDIM)], 0
    )
    slot_ids = jnp.where(remote_pair, clusters_here + owner_pair, local_pair)
    cluster_ids = jnp.arange(fill_all.shape[0], dtype=jnp.int32)
    fill_pair = jnp.sum(jnp.where(pair_list[..., None] == cluster_ids, fill_all, 0), -1)
    block_real = (cell_span[None, None, :] < fill_pair[..., None]).reshape(clusters_here, -1)
    key_real = jnp.concatenate(
        [block_real, jnp.ones((clusters_here, global_keys.shape[0]), bool)], 1
    )
    keep_mask = jnp.ones(slot_ids.shape, f32)
    block_rows = slot_ids.shape[1] * GROUP_VERTICES

    def cluster_step(step_carry, step_items):
        key_acc, value_acc, gkey_acc, gvalue_acc = step_carry
        cluster, query_block, dout_block, slot_block, real_keys, real_queries, keep_block = (
            step_items
        )
        block_keys = jnp.take(combined_keys, slot_block, axis=0).reshape(-1, heads_here, HDIM)
        block_values = jnp.take(combined_values, slot_block, axis=0).reshape(-1, heads_here, HDIM)
        all_keys = jnp.concatenate([block_keys, global_keys], 0)
        all_values = jnp.concatenate([block_values, global_values], 0)
        scores = (
            jnp.einsum("qhd,khd->hqk", query_block, all_keys, preferred_element_type=f32)
            * score_scale
        )
        masked = jnp.where(real_keys[None, None, :], scores, -1e30)
        row_max = jnp.max(masked, -1, keepdims=True)
        exp_terms = jnp.where(real_keys[None, None, :], jnp.exp(masked - row_max), 0.0)
        row_total = jnp.sum(exp_terms, -1, keepdims=True)
        attn_prob = exp_terms / row_total
        prob_rounded = attn_prob.astype(bf16)
        output = jnp.einsum(
            "hqk,khd->qhd", prob_rounded, all_values, preferred_element_type=f32
        ).reshape(GROUP_VERTICES, half_width)
        output = jnp.where(real_queries[:, None], output, 0.0).astype(bf16)
        dprob = jnp.einsum("qhd,khd->hqk", dout_block, all_values, preferred_element_type=f32)
        row_delta = jnp.sum(attn_prob * dprob, -1, keepdims=True)
        dscore = (attn_prob * (dprob - row_delta)).astype(bf16)
        probe_derivative = (
            (jnp.einsum("hqk,khd->qhd", dscore, all_keys, preferred_element_type=f32) * score_scale)
            .reshape(GROUP_VERTICES, half_width)
            .astype(bf16)
        )
        key_part = (
            jnp.einsum("hqk,qhd->khd", dscore, query_block, preferred_element_type=f32)
            * score_scale
        )
        value_part = jnp.einsum(
            "hqk,qhd->khd", prob_rounded, dout_block, preferred_element_type=f32
        )
        weight_block = keep_block[:, None, None, None]
        key_acc = key_acc.at[slot_block].add(
            key_part[:block_rows].reshape(-1, GROUP_VERTICES, heads_here, HDIM) * weight_block
        )
        value_acc = value_acc.at[slot_block].add(
            value_part[:block_rows].reshape(-1, GROUP_VERTICES, heads_here, HDIM) * weight_block
        )
        gkey_acc = gkey_acc + key_part[block_rows:]
        gvalue_acc = gvalue_acc + value_part[block_rows:]
        stat_rows = ()
        return ((key_acc, value_acc, gkey_acc, gvalue_acc), (output, probe_derivative) + stat_rows)

    slot_zeros = jnp.zeros((clusters_here + partition_tally, GROUP_VERTICES, heads_here, HDIM), f32)
    global_zeros = jnp.zeros(global_keys.shape, f32)
    step_inputs = (
        jnp.arange(clusters_here, dtype=jnp.int32),
        queries,
        dout,
        slot_ids,
        key_real,
        row_real,
        keep_mask,
    )
    final_carry, step_outputs = lax.scan(
        cluster_step, (slot_zeros, slot_zeros, global_zeros, global_zeros), step_inputs
    )
    key_acc, value_acc, gkey_acc, gvalue_acc = final_carry
    mixed_result = step_outputs[0].reshape(nodes_here, half_width)
    probe_derivative = step_outputs[1].reshape(nodes_here, half_width)
    key_local = key_acc[:clusters_here]
    value_local = value_acc[:clusters_here]
    give_float = give_mask.astype(f32)
    back_keys, back_values = (
        lax.all_to_all(
            key_acc[clusters_here:].reshape(partition_tally, GROUP_VERTICES, half_width),
            "seq",
            split_axis=0,
            concat_axis=0,
            tiled=True,
        ),
        lax.all_to_all(
            value_acc[clusters_here:].reshape(partition_tally, GROUP_VERTICES, half_width),
            "seq",
            split_axis=0,
            concat_axis=0,
            tiled=True,
        ),
    )
    gate = give_float[:, None, None, None]
    key_local = key_local.at[pick_index].add(
        back_keys.reshape(partition_tally, GROUP_VERTICES, heads_here, HDIM) * gate
    )
    value_local = value_local.at[pick_index].add(
        back_values.reshape(partition_tally, GROUP_VERTICES, heads_here, HDIM) * gate
    )
    global_key_grad, global_value_grad = lax.psum(
        (gkey_acc.reshape(-1, half_width), gvalue_acc.reshape(-1, half_width)), "seq"
    )
    key_flat = (
        key_local.reshape(nodes_here, half_width)
        .at[row_global]
        .add(jnp.where(mine_global[:, None], global_key_grad, 0.0))
    )
    value_flat = (
        value_local.reshape(nodes_here, half_width)
        .at[row_global]
        .add(jnp.where(mine_global[:, None], global_value_grad, 0.0))
    )
    stacked = jnp.stack([probe_derivative, key_flat.astype(bf16), value_flat.astype(bf16)], 1)
    node_grad = jnp.einsum("nif,dif->nd", stacked, proj_weights, preferred_element_type=f32)
    feature_part = inverse * (
        node_grad - normed32 * jnp.mean(normed32 * node_grad, -1, keepdims=True)
    )
    grad_x = lax.psum(feature_part, "tp").astype(bf16)
    grad_w = lax.psum_scatter(
        jnp.einsum("nd,nif->dif", normed, stacked, preferred_element_type=f32),
        ("seq", "rep"),
        scatter_dimension=0,
        tiled=True,
    )
    return (mixed_result[None], grad_x[None], grad_w)


def solution(mesh):
    placed = (
        P(("groups", "rep"), "seq", None),
        P(("groups", "rep"), "seq", "tp"),
        P(None, None, "tp"),
        P(("groups", "rep"), "seq", None),
        P(("groups", "rep"), None),
        P(("groups", "rep"), None),
    )
    return jax.shard_map(
        local,
        mesh=mesh,
        in_specs=placed,
        out_specs=(
            P(("groups", "rep"), "seq", "tp"),
            P(("groups", "rep"), "seq", None),
            P(("groups", "seq", "rep"), None, "tp"),
        ),
        check_vma=False,
    )
```

profile of v0, /device:TPU:0, one launch (start us, length us, event | category | flops | bytes accessed | tf_op | source)
XLA Modules:
  0.0 305.5 jit_solution(277648281339315983)
XLA Ops:
  9.5 6.3 %all-to-all-start = ((s32[4,1,1]{2,1,0:T(1,128)}), s32[4,1,1]{2,1,0:T(1,128)S(1)}, u32[]{:S(2)}, u32[]{:S(2)}) async-start(s32[4,1,1]{2,1,0:T(1,128)} %copy.139), calls=%async_computation | async-start | bytes 4096 | tf_op jit(solution)/shard_map/all_to_all | solution.py:68
  27.2 5.1 %all-to-all-start.1 = ((bf16[4,128,384]{1,2,0:T(8,128)(2,1)}), bf16[4,128,384]{1,2,0:T(8,128)(2,1)S(1)}, u32[]{:S(2)}, u32[]{:S(2)}) async-start(bf16[4,128,384]{1,2,0:T(8,128)(2,1)} %bitcast.10), calls=%async_computation.1 | async-start | bytes 786432 | tf_op jit(solution)/shard_map/all_to_all | solution.py:78
  33.7 14.5 %all-to-all-done.1 = bf16[4,128,384]{1,2,0:T(8,128)(2,1)S(1)} async-done(((bf16[4,128,384]{1,2,0:T(8,128)(2,1)}), bf16[4,128,384]{1,2,0:T(8,128)(2,1)S(1)}, u32[]{:S(2)}, u32[]{:S(2)}) %all-to-all-start.1) | async-done | bytes 393248 | tf_op jit(solution)/shard_map/all_to_all | solution.py:78
  48.2 4.1 %all-to-all-start.2 = ((bf16[4,128,384]{1,2,0:T(8,128)(2,1)}), bf16[4,128,384]{1,2,0:T(8,128)(2,1)}, u32[]{:S(2)}, u32[]{:S(2)}) async-start(bf16[4,128,384]{1,2,0:T(8,128)(2,1)} %bitcast.16), calls=%async_computation.2 | async-start | bytes 786432 | tf_op jit(solution)/shard_map/all_to_all | solution.py:79
  55.2 15.2 %all-to-all-done.2 = bf16[4,128,384]{1,2,0:T(8,128)(2,1)} async-done(((bf16[4,128,384]{1,2,0:T(8,128)(2,1)}), bf16[4,128,384]{1,2,0:T(8,128)(2,1)}, u32[]{:S(2)}, u32[]{:S(2)}) %all-to-all-start.2) | async-done | bytes 393248 | tf_op jit(solution)/shard_map/all_to_all | solution.py:79
  75.6 52.2 %while.21 = (s32[]{:T(128)}, f32[6,128,6,64]{1,3,2,0:T(8,128)}, f32[6,128,6,64]{1,3,2,0:T(8,128)}, f32[256,6,64]{0,2,1:T(8,128)}, f32[256,6,64]{0,2,1:T(8,128)},...) while((s32[]{:T(128)}, f32[6,128,6,64]{1,3,2,0:T(8,128)}, ...), condition=%wide.region_11.15_spmd.clone, body=%wide.region_5.14_spmd.clone.sunk | while | flops 312558336 | bytes 64518736 | solution.py:158
  77.7 2.8 gather_fusion.1
  82.1 2.8 fusion.95
  95.6 2.4 scatter_fusion.1
  103.3 2.8 gather_fusion.1
  107.7 2.8 fusion.95
  122.3 2.5 scatter_fusion.1
  127.8 2.2 slice.39
  130.0 4.2 %all-to-all-start.3 = ((f32[4,128,384]{1,2,0:T(8,128)}), f32[4,128,384]{1,2,0:T(8,128)}, u32[]{:S(2)}, u32[]{:S(2)}) async-start(f32[4,128,384]{1,2,0:T(8,128)} %bitcast.181), calls=%async_computation.3 | async-start | bytes 1572864 | tf_op jit(solution)/shard_map/all_to_all | solution.py:168
  135.2 16.6 %all-to-all-done.3 = f32[4,128,384]{1,2,0:T(8,128)} async-done(((f32[4,128,384]{1,2,0:T(8,128)}), f32[4,128,384]{1,2,0:T(8,128)}, u32[]{:S(2)}, u32[]{:S(2)}) %all-to-all-start.3) | async-done | bytes 786464 | tf_op jit(solution)/shard_map/all_to_all | solution.py:168
  151.8 4.2 %all-to-all-start.4 = ((f32[4,128,384]{1,2,0:T(8,128)}), f32[4,128,384]{1,2,0:T(8,128)}, u32[]{:S(2)}, u32[]{:S(2)}) async-start(f32[4,128,384]{1,2,0:T(8,128)} %bitcast.180), calls=%async_computation.4 | async-start | bytes 1572864 | tf_op jit(solution)/shard_map/all_to_all | solution.py:175
  161.1 23.8 %all-to-all-done.4 = f32[4,128,384]{1,2,0:T(8,128)} async-done(((f32[4,128,384]{1,2,0:T(8,128)}), f32[4,128,384]{1,2,0:T(8,128)}, u32[]{:S(2)}, u32[]{:S(2)}) %all-to-all-start.4) | async-done | bytes 786464 | tf_op jit(solution)/shard_map/all_to_all | solution.py:175
  184.9 2.5 broadcast_multiply_fusion.1
  192.4 19.8 %all-reduce.7.cloned.1.call-done = (f32[256,384]{1,0:T(8,128)}, f32[256,384]{1,0:T(8,128)}) async-done(((f32[256,384]{1,0:T(8,128)}, f32[256,384]{1,0:T(8,128)}), (f32[256,384]{1,0:T(8,128)}, f32[256,384]{1,0:T(8,128)})) %all-reduce.7.cloned.1.call-update) | async-done | bytes 786448 | tf_op jit(solution)/shard_map/psum | solution.py:190
  212.2 2.8 scatter_custom_fusion.3
  215.0 2.8 scatter_custom_fusion.5
  217.9 2.6 fusion.51
  221.5 6.0 %all-reduce.10 = bf16[256,768]{1,0:T(8,128)(2,1)} all-reduce(f32[256,768]{1,0:T(8,128)S(1)} %fusion.44), channel_id=1, replica_groups=mesh['groups'=2,'seq'=4,'rep'=2,'tp'=2] {'tp'}, use_global_device_ids=true, to_apply=%region_19.23 | all-reduce | flops 196608 | bytes 1179648 | tf_op jit(solution)/shard_map/psum | solution.py:208
  227.5 71.5 %reduce-scatter.2.cloned.1.call-done = f32[96,3,384]{2,0,1:T(8,128)} async-done(((f32[768,3,384]{2,0,1:T(8,128)}), f32[96,3,384]{2,0,1:T(8,128)}) %reduce-scatter.2.cloned.1.call-update) | async-done | bytes 442384 | tf_op jit(solution)/shard_map/reduce_scatter | solution.py:209
  (228 shorter events, 70.1 us)
Async XLA Ops:
  7.2 10.3 %copy-start = (bf16[768,3,384]{2,0,1:T(8,128)(2,1)S(1)}, bf16[768,3,384]{2,0,1:T(8,128)(2,1)}, u32[]{:S(2)}) copy-start(bf16[768,3,384]{2,0,1:T(8,128)(2,1)} %param.16) | copy-start | bytes 5308420
  9.5 15.2 %all-to-all-start = ((s32[4,1,1]{2,1,0:T(1,128)}), s32[4,1,1]{2,1,0:T(1,128)S(1)}, u32[]{:S(2)}, u32[]{:S(2)}) async-start(s32[4,1,1]{2,1,0:T(1,128)} %copy.139), calls=%async_computation | async-start | bytes 4096 | tf_op jit(solution)/shard_map/all_to_all | solution.py:68
  15.8 57.4 %all-reduce.9.cloned.1.call-start = ((), (), s32[]{:S(2)}) async-start(), calls=%async_computation.8 | async-start | bytes 786432 | tf_op jit(solution)/shard_map/psum | solution.py:57
  26.1 6.9 %copy-start.19 = (bf16[1,256,384]{2,1,0:T(8,128)(2,1)S(1)}, bf16[1,256,384]{2,1,0:T(8,128)(2,1)}, u32[]{:S(2)}) copy-start(bf16[1,256,384]{2,1,0:T(8,128)(2,1)} %param.15) | copy-start | bytes 589828
  26.2 7.1 %copy-start.20 = (s32[1,2,2]{2,1,0:T(2,128)S(1)}, s32[1,2,2]{2,1,0:T(2,128)}, u32[]{:S(2)}) copy-start(s32[1,2,2]{2,1,0:T(2,128)} %param.17) | copy-start | bytes 52
  27.2 21.0 %all-to-all-start.1 = ((bf16[4,128,384]{1,2,0:T(8,128)(2,1)}), bf16[4,128,384]{1,2,0:T(8,128)(2,1)S(1)}, u32[]{:S(2)}, u32[]{:S(2)}) async-start(bf16[4,128,384]{1,2,0:T(8,128)(2,1)} %bitcast.10), calls=%async_computation.1 | async-start | bytes 786432 | tf_op jit(solution)/shard_map/all_to_all | solution.py:78
  33.0 20.3 %copy-start.29 = (pred[2,128]{1,0:T(4,128)(4,1)}, pred[2,128]{1,0:T(4,128)(4,1)S(1)}, u32[]{:S(2)}) copy-start(pred[2,128]{1,0:T(4,128)(4,1)S(1)} %iota_compare_fusion) | copy-start | bytes 772
  48.2 22.2 %all-to-all-start.2 = ((bf16[4,128,384]{1,2,0:T(8,128)(2,1)}), bf16[4,128,384]{1,2,0:T(8,128)(2,1)}, u32[]{:S(2)}, u32[]{:S(2)}) async-start(bf16[4,128,384]{1,2,0:T(8,128)(2,1)} %bitcast.16), calls=%async_computation.2 | async-start | bytes 786432 | tf_op jit(solution)/shard_map/all_to_all | solution.py:79
  75.6 6.5 %copy-start.13 = (bf16[2,128,6,64]{1,3,2,0:T(8,128)(2,1)}, bf16[2,128,6,64]{1,3,2,0:T(8,128)(2,1)S(1)}, u32[]{:S(2)}) copy-start(bf16[2,128,6,64]{1,3,2,0:T(8,128)(2,1)S(1)} %get-tuple-element.487) | copy-start | bytes 589828 | tf_op jit(solution)/shard_map/while
  95.6 3.5 %copy-start.1 = (f32[6,128,6,64]{1,3,2,0:T(8,128)S(1)}, f32[6,128,6,64]{1,3,2,0:T(8,128)}, u32[]{:S(2)}) copy-start(f32[6,128,6,64]{1,3,2,0:T(8,128)} %get-tuple-element.462) | copy-start | bytes 3538948 | tf_op jit(solution)/shard_map/while
  101.1 6.5 %copy-start.13 = (bf16[2,128,6,64]{1,3,2,0:T(8,128)(2,1)}, bf16[2,128,6,64]{1,3,2,0:T(8,128)(2,1)S(1)}, u32[]{:S(2)}) copy-start(bf16[2,128,6,64]{1,3,2,0:T(8,128)(2,1)S(1)} %get-tuple-element.487) | copy-start | bytes 589828 | tf_op jit(solution)/shard_map/while
  122.3 3.5 %copy-start.1 = (f32[6,128,6,64]{1,3,2,0:T(8,128)S(1)}, f32[6,128,6,64]{1,3,2,0:T(8,128)}, u32[]{:S(2)}) copy-start(f32[6,128,6,64]{1,3,2,0:T(8,128)} %get-tuple-element.462) | copy-start | bytes 3538948 | tf_op jit(solution)/shard_map/while
  127.8 6.4 %copy-start.3 = (f32[6,128,6,64]{1,3,2,0:T(8,128)S(1)}, f32[6,128,6,64]{1,3,2,0:T(8,128)}, u32[]{:S(2)}) copy-start(f32[6,128,6,64]{1,3,2,0:T(8,128)} %get-tuple-element.97) | copy-start | bytes 3538948
  130.0 21.8 %all-to-all-start.3 = ((f32[4,128,384]{1,2,0:T(8,128)}), f32[4,128,384]{1,2,0:T(8,128)}, u32[]{:S(2)}, u32[]{:S(2)}) async-start(f32[4,128,384]{1,2,0:T(8,128)} %bitcast.181), calls=%async_computation.3 | async-start | bytes 1572864 | tf_op jit(solution)/shard_map/all_to_all | solution.py:168
  134.2 21.8 %copy-start.8 = (f32[256,6,64]{0,2,1:T(8,128)S(1)}, f32[256,6,64]{0,2,1:T(8,128)}, u32[]{:S(2)}) copy-start(f32[256,6,64]{0,2,1:T(8,128)} %get-tuple-element.96) | copy-start | bytes 1179652
  151.8 33.1 %all-to-all-start.4 = ((f32[4,128,384]{1,2,0:T(8,128)}), f32[4,128,384]{1,2,0:T(8,128)}, u32[]{:S(2)}, u32[]{:S(2)}) async-start(f32[4,128,384]{1,2,0:T(8,128)} %bitcast.180), calls=%async_computation.4 | async-start | bytes 1572864 | tf_op jit(solution)/shard_map/all_to_all | solution.py:175
  156.0 3.2 %copy-start.28 = (s32[1,256]{1,0:T(1,128)S(1)}, s32[1,256]{1,0:T(1,128)}, u32[]{:S(2)}) copy-start(s32[1,256]{1,0:T(1,128)} %param.19) | copy-start | bytes 3076
  156.0 56.2 %all-reduce.7.cloned.1.call-start = ((), (), s32[]{:S(2)}) async-start(), calls=%async_computation.7 | async-start | bytes 1572864 | tf_op jit(solution)/shard_map/psum | solution.py:190
  158.9 140.0 %reduce-scatter.2.cloned.1.call-start = ((), (), s32[]{:S(2)}) async-start(), calls=%async_computation.6 | async-start | bytes 3981312 | tf_op jit(solution)/shard_map/reduce_scatter | solution.py:209
  191.8 20.4 %copy-start.15 = (f32[256,384]{1,0:T(8,128)S(1)}, f32[256,384]{1,0:T(8,128)}, u32[]{:S(2)}) copy-start(f32[256,384]{1,0:T(8,128)} %copy.156) | copy-start | bytes 1179652
  191.8 20.4 %copy-start.24 = (pred[256]{0:T(512)(128)(4,1)S(1)}, pred[256]{0:T(512)(128)(4,1)}, u32[]{:S(2)}) copy-start(pred[256]{0:T(512)(128)(4,1)} %copy-done.23) | copy-start | bytes 772
  192.3 25.5 %copy-start.12 = (bf16[1,256,768]{2,1,0:T(8,128)(2,1)S(1)}, bf16[1,256,768]{2,1,0:T(8,128)(2,1)}, u32[]{:S(2)}) copy-start(bf16[1,256,768]{2,1,0:T(8,128)(2,1)} %param.14) | copy-start | bytes 1179652
  192.4 25.5 %copy-start.18 = (bf16[2,128,384]{2,1,0:T(8,128)(2,1)S(1)}, bf16[2,128,384]{2,1,0:T(8,128)(2,1)}, u32[]{:S(2)}) copy-start(bf16[2,128,384]{2,1,0:T(8,128)(2,1)} %get-tuple-element.94) | copy-start | bytes 589828
  192.4 25.5 %copy-start.22 = (f32[256]{0:T(256)S(1)}, f32[256]{0:T(256)}, u32[]{:S(2)}) copy-start(f32[256]{0:T(256)} %copy-done.21) | copy-start | bytes 3076
  (35 other events, 55.7 us)
Sparse Core Ops, SparseCore 0:
  23.7 46.4 all-reduce.8
  159.9 52.1 all-reduce.6
  220.6 78.3 reduce-scatter.1
where the time goes:
time: 307 us; the launch traced here: 305 us
  waiting for transfers between devices  161 us (52%)
  local copies, waits for them, and re-layouts  44 us (14%)
  other arithmetic  31.1 us (10%)
  starting transfers between devices  24.2 us (8%)
  matrix products  23.9 us (8%)
  between operations  14.3 us (5%)
  blocking collectives  5.99 us (2%)
    reduce_scatter x1, waiting for transfers between devices, local(): lax.psum_scatter(jnp.einsum('nd,nif->dif', normed, stacked, preferred_ele...  71.5 us
    all_to_all x1, waiting for transfers between devices, local(): lax.all_to_all(value_acc[clusters_here:].reshape(partition_tally, GROUP_V...  23.8 us
    psum x1, waiting for transfers between devices, local(): lax.psum((gkey_acc.reshape(-1, half_width), gvalue_acc.reshape(-1, half_w...  19.8 us
    all_to_all x1, waiting for transfers between devices, local(): lax.all_to_all(key_acc[clusters_here:].reshape(partition_tally, GROUP_VER...  16.6 us
    all_to_all x1, waiting for transfers between devices, local(): lax.all_to_all(value_send, 'seq', split_axis=0, concat_axis=0, tiled=True)  15.2 us
    all_to_all x1, waiting for transfers between devices, local(): lax.all_to_all(key_send, 'seq', split_axis=0, concat_axis=0, tiled=True)  14.5 us
    all_to_all x1, starting transfers between devices, local(): lax.all_to_all(wanted[:, None], 'seq', split_axis=0, concat_axis=0, tiled...  6.32 us
  transfers between devices with their start and end apart: 8, of which 6 were waited for; matrix products, arithmetic and copies ran while one was open for 10% of the time, Pallas kernels for 0%

commit v1 on v0

v1 whole, which is shorter than its diff:
```python
import functools

import jax
import jax.numpy as jnp
from jax import lax
from jax.experimental import pallas as pl
from jax.experimental.pallas import tpu as pltpu
from jax.sharding import PartitionSpec as P

HDIM = 64
GROUP_VERTICES = 128
PAIR = 2 * HDIM
NORM_EPS = 1e-06
LOG2E = 1.4426950408889634
F32 = jnp.float32
BF16 = jnp.bfloat16
VMEM_LIMIT = 48 * 1024 * 1024
NT = (((1,), (1,)), ((), ()))
NN = (((1,), (0,)), ((), ()))
TN = (((0,), (0,)), ((), ()))

VMEM = pl.BlockSpec(memory_space=pltpu.VMEM)
SMEM = pl.BlockSpec(memory_space=pltpu.SMEM)


def dot(a, b, dims=NN):
    return lax.dot_general(a, b, dims, preferred_element_type=F32)


def params():
    return pltpu.CompilerParams(vmem_limit_bytes=VMEM_LIMIT)


def project_kernel(shards, core_ref, ids_ref, w_ref, x_ref, *refs):
    near = refs[: shards - 1]
    far = refs[shards - 1 : 2 * (shards - 1)]
    normed_ref, q_ref, k_ref, v_ref = refs[2 * (shards - 1) :]
    nodes = x_ref.shape[0]
    rows = nodes // 2
    core = core_ref[0]

    def norm(block):
        wide = block.astype(F32)
        inverse = lax.rsqrt(jnp.mean(wide * wide, -1, keepdims=True) + NORM_EPS)
        return (wide * inverse).astype(BF16)

    def project(start, count):
        normed = normed_ref[pl.ds(start, count), :]
        q_ref[pl.ds(start, count), :] = dot(normed, w_ref[0]).astype(BF16)
        k_ref[pl.ds(start, count), :] = dot(normed, w_ref[1]).astype(BF16)
        v_ref[pl.ds(start, count), :] = dot(normed, w_ref[2]).astype(BF16)

    normed_ref[pl.ds(0, nodes), :] = norm(x_ref[...])
    project(0, nodes)
    for shard in range(1, shards):
        mine = pl.multiple_of(shard * nodes + core * rows, rows)
        other = pl.multiple_of(shard * nodes + (1 - core) * rows, rows)
        normed_ref[pl.ds(mine, rows), :] = norm(near[shard - 1][...])
        normed_ref[pl.ds(other, rows), :] = norm(far[shard - 1][...])
        project(shard * nodes, nodes)
    total = shards * nodes
    count = ids_ref.shape[0]
    key_sum = jnp.zeros((count, k_ref.shape[1]), F32)
    value_sum = key_sum
    for shard in range(shards):
        places = lax.broadcasted_iota(jnp.int32, (count, nodes), 1) + shard * nodes
        pick = jnp.where(places == ids_ref[...], 1.0, 0.0).astype(BF16)
        key_sum += dot(pick, k_ref[shard * nodes : (shard + 1) * nodes, :])
        value_sum += dot(pick, v_ref[shard * nodes : (shard + 1) * nodes, :])
    k_ref[total : total + count, :] = key_sum.astype(BF16)
    v_ref[total : total + count, :] = value_sum.astype(BF16)


def attend_kernel(shard, total, lookups, first, meta_ref, fill_ref, q_ref, dout_ref, k_ref, v_ref, *refs):
    if first:
        dq_ref, dk_ref, dv_ref, out_ref = refs
        dk_ref[...] = jnp.zeros_like(dk_ref)
        dv_ref[...] = jnp.zeros_like(dv_ref)
    else:
        dk_in, dv_in, dq_ref, dk_ref, dv_ref = refs
        dk_ref[...] = dk_in[...]
        dv_ref[...] = dv_in[...]
    size = GROUP_VERTICES
    clusters = dout_ref.shape[0] // size
    width = dout_ref.shape[1]
    count = k_ref.shape[0] - total
    lanes = lax.broadcasted_iota(jnp.int32, (size, PAIR), 1)
    low = lanes < HDIM
    rows = lax.broadcasted_iota(jnp.int32, (size, 1), 0)
    slots = lax.broadcasted_iota(jnp.int32, (size, 2 * size), 0)
    zero = jnp.zeros((), BF16)

    def split(block):
        return jnp.concatenate([jnp.where(low, block, zero), jnp.where(low, zero, block)], 0)

    @pl.loop(0, clusters)
    def _(cluster):
        base = (shard * clusters + cluster) * lookups
        starts = [pl.multiple_of(meta_ref[base + i] * size, size) for i in range(lookups)]
        fills = [fill_ref[base + i] for i in range(lookups)]
        place = pl.multiple_of(cluster * size, size)
        real = rows < fills[0]
        for column in range(0, width, PAIR):
            cols = slice(column, column + PAIR)
            queries = split(q_ref[pl.ds(shard * clusters * size + place, size), cols])
            douts = split(jnp.where(real, dout_ref[pl.ds(place, size), cols], zero))
            keys = jnp.concatenate(
                [k_ref[pl.ds(s, size), cols] for s in starts] + [k_ref[total:, cols]], 0
            )
            values = jnp.concatenate(
                [v_ref[pl.ds(s, size), cols] for s in starts] + [v_ref[total:, cols]], 0
            )
            scores = dot(keys, queries, NT)
            parts = [
                jnp.where(slots < fills[i], scores[i * size : (i + 1) * size], -1e30)
                for i in range(lookups)
            ]
            scores = jnp.concatenate(parts + [scores[lookups * size :]], 0)
            peak = jnp.max(scores, 0, keepdims=True)
            terms = jnp.exp2((scores - peak) * (LOG2E * HDIM ** (-0.5)))
            prob = terms * (1.0 / jnp.sum(terms, 0, keepdims=True))
            rounded = prob.astype(BF16)
            dprob = dot(values, douts, NT)
            delta = jnp.sum(prob * dprob, 0, keepdims=True)
            dscore = (prob * (dprob - delta)).astype(BF16)
            dv_part = dot(rounded, douts)
            dk_part = dot(dscore, queries) * HDIM ** (-0.5)
            for i in range(lookups):
                span = pl.ds(starts[i], size)
                dk_ref[span, cols] += dk_part[i * size : (i + 1) * size]
                dv_ref[span, cols] += dv_part[i * size : (i + 1) * size]
            dk_ref[total:, cols] += dk_part[lookups * size :]
            dv_ref[total:, cols] += dv_part[lookups * size :]
            dq = dot(keys, dscore, TN) * HDIM ** (-0.5)
            dq = jnp.concatenate([dq[:HDIM, :size], dq[HDIM:, size:]], 0)
            dq_ref[pl.ds(place, size), cols] = dq.T.astype(BF16)
            if first:
                mixed = dot(values, rounded, TN)
                mixed = jnp.concatenate([mixed[:HDIM, :size], mixed[HDIM:, size:]], 0)
                out_ref[pl.ds(place, size), cols] = jnp.where(real, mixed.T, 0.0).astype(BF16)


def finish_kernel(shards, reps, rep_ref, ids_ref, slices_ref, w_ref, dk_ref, dv_ref, *refs):
    dq_refs = refs[:shards]
    mine_ref, other_ref, node_ref = refs[shards:]
    nodes = dq_refs[0].shape[0]
    total = shards * nodes
    count = ids_ref.shape[1]
    share = mine_ref.shape[1]
    dkg, dvg = dk_ref[total:, :], dv_ref[total:, :]
    dkg_hi, dvg_hi = dkg.astype(BF16), dvg.astype(BF16)
    dkg_lo, dvg_lo = (dkg - dkg_hi.astype(F32)).astype(BF16), (dvg - dvg_hi.astype(F32)).astype(BF16)
    sums = [None, None, None]
    for shard in range(shards):
        span = slice(shard * nodes, (shard + 1) * nodes)
        places = lax.broadcasted_iota(jnp.int32, (nodes, count), 0) + shard * nodes
        put = jnp.where(places == ids_ref[...], 1.0, 0.0).astype(BF16)
        dk = (dk_ref[span, :] + (dot(put, dkg_hi) + dot(put, dkg_lo))).astype(BF16)
        dv = (dv_ref[span, :] + (dot(put, dvg_hi) + dot(put, dvg_lo))).astype(BF16)
        grads = [dq_refs[shard][...], dk, dv]
        left = slices_ref[:, span]
        for i in range(3):
            term = dot(left, grads[i])
            sums[i] = term if shard == 0 else sums[i] + term
        if shard == 0:
            node_ref[...] = dot(grads[0], w_ref[0], NT) + (
                dot(grads[1], w_ref[1], NT) + dot(grads[2], w_ref[2], NT)
            )
    for i in range(3):
        mine_ref[i] = sums[i][:share]
        other_ref[i] = sums[i][share:]


def local(node_features, result_cotangent, proj_weights, cluster_pairs, cluster_fill, global_nodes):
    features = node_features[0]
    cotangent = result_cotangent[0]
    pairs_here = cluster_pairs[0]
    fill_all = cluster_fill[0]
    global_ids = global_nodes[0]
    weights = jnp.transpose(proj_weights, (1, 0, 2))
    nodes, width = features.shape
    half_width = cotangent.shape[1]
    clusters, lookups = pairs_here.shape
    shards = lax.axis_size("seq")
    reps = lax.axis_size("rep")
    me = lax.axis_index("seq")
    core = lax.axis_index("tp")
    rep = lax.axis_index("rep")
    total = shards * nodes
    count = global_ids.shape[0]
    rows = nodes // 2

    def shift(value, step):
        return lax.ppermute(value, "seq", [(j, (j + step) % shards) for j in range(shards)])

    def swap(value, axis):
        return lax.ppermute(value, axis, [(0, 1), (1, 0)])

    half = lax.dynamic_slice_in_dim(features, core * rows, rows)
    near = [shift(half, step) for step in range(1, shards)]
    far = [swap(block, "tp") for block in near]
    pair_blocks = [pairs_here] + [shift(pairs_here, step) for step in range(1, shards)]
    anchor = near[-1]
    douts = [cotangent]
    for step in range(1, shards):
        ready, _ = lax.optimization_barrier((cotangent, anchor))
        douts.append(shift(ready, step))

    pairs = jnp.stack(pair_blocks).reshape(-1)
    meta = ((me - pairs // clusters) % shards) * clusters + pairs % clusters
    fills = jnp.sum(
        jnp.where(
            pairs[:, None] == jnp.arange(fill_all.shape[0], dtype=jnp.int32)[None], fill_all[None], 0
        ),
        -1,
    )
    ids = ((me - global_ids // nodes) % shards) * nodes + global_ids % nodes

    normed, q, k, v = pl.pallas_call(
        functools.partial(project_kernel, shards),
        out_shape=(
            jax.ShapeDtypeStruct((total, width), BF16),
            jax.ShapeDtypeStruct((total, half_width), BF16),
            jax.ShapeDtypeStruct((total + count, half_width), BF16),
            jax.ShapeDtypeStruct((total + count, half_width), BF16),
        ),
        in_specs=[SMEM] + [VMEM] * (3 + 2 * (shards - 1)),
        out_specs=(VMEM,) * 4,
        compiler_params=params(),
        name="project",
    )(core.reshape(1), ids[:, None], weights, features, *near, *far)

    share = width // (shards * reps)
    block = lax.dynamic_slice_in_dim(normed, me * reps * share, reps * share, 1).T
    block = jnp.roll(block, -rep * share, 0)

    dqs = []
    dk = dv = mixed = None
    acc = jax.ShapeDtypeStruct((total + count, half_width), F32)
    flat = jax.ShapeDtypeStruct((nodes, half_width), BF16)
    for shard in range(shards):
        first = shard == 0
        got = pl.pallas_call(
            functools.partial(attend_kernel, shard, total, lookups, first),
            out_shape=(flat, acc, acc) + ((flat,) if first else ()),
            in_specs=[SMEM, SMEM] + [VMEM] * (4 if first else 6),
            out_specs=(VMEM,) * (4 if first else 3),
            compiler_params=params(),
            name="attend_%d" % shard,
        )(meta, fills, q, douts[shard], k, v, *(() if first else (dk, dv)))
        dqs.append(got[0])
        dk, dv = got[1:3]
        if first:
            mixed = got[3]

    part = jax.ShapeDtypeStruct((3, share, half_width), F32)
    rest = jax.ShapeDtypeStruct((3, (reps - 1) * share, half_width), F32)
    mine, other, node_part = pl.pallas_call(
        functools.partial(finish_kernel, shards, reps),
        out_shape=(part, rest, jax.ShapeDtypeStruct((nodes, width), F32)),
        in_specs=[SMEM] + [VMEM] * (5 + shards),
        out_specs=(VMEM,) * 3,
        compiler_params=params(),
        name="finish",
    )(rep.reshape(1), ids[None, :], block, weights, dk, dv, *dqs)

    if reps == 2:
        grad_w = mine + swap(other, "rep")
    else:
        whole = jnp.roll(jnp.concatenate([mine, other], 1), rep * share, 1)
        grad_w = lax.psum_scatter(whole, "rep", scatter_dimension=1, tiled=True)
    node_grad = node_part + swap(node_part, "tp")
    wide = features.astype(F32)
    inverse = lax.rsqrt(jnp.mean(wide * wide, -1, keepdims=True) + NORM_EPS)
    normed32 = wide * inverse
    grad_x = inverse * (node_grad - normed32 * jnp.mean(normed32 * node_grad, -1, keepdims=True))
    return mixed[None], grad_x.astype(BF16)[None], jnp.transpose(grad_w, (1, 0, 2))


def solution(mesh):
    placed = (
        P(("groups", "rep"), "seq", None),
        P(("groups", "rep"), "seq", "tp"),
        P(None, None, "tp"),
        P(("groups", "rep"), "seq", None),
        P(("groups", "rep"), None),
        P(("groups", "rep"), None),
    )
    return jax.shard_map(
        local,
        mesh=mesh,
        in_specs=placed,
        out_specs=(
            P(("groups", "rep"), "seq", "tp"),
            P(("groups", "rep"), "seq", None),
            P(("groups", "seq", "rep"), None, "tp"),
        ),
        check_vma=False,
    )
```

time: 307 us -> 109 us (0.36)
  waiting for transfers between devices: 161 us -> 14.7 us
  Pallas kernels: 0 us -> 39.7 us
  other arithmetic: 31.1 us -> 4.99 us
  local copies, waits for them, and re-layouts: 44 us -> 18.5 us
  matrix products: 23.9 us -> 0 us
  between operations: 14.3 us -> 0.79 us
  blocking collectives: 5.99 us -> 0 us
  starting transfers between devices: 24.2 us -> 29.6 us
    reduce_scatter x1 -> x0, waiting for transfers between devices: 71.5 us -> none  [local(): lax.psum_scatter(jnp.einsum('nd,nif->dif', normed, stacked, preferred_ele...]
    all_to_all x5 -> x0, waiting for transfers between devices: 70.2 us -> none  [the longest x1 23.8 us: local(): lax.all_to_all(value_acc[clusters_here:].reshape(partition_tally, GROUP_V...]
    pallas_call x0 -> x6, Pallas kernels: none -> 39.7 us  [the longest x4 29.8 us: local(): pl.pallas_call(functools.partial(attend_kernel, shard, total, lookups, fi...]
    ppermute x0 -> x14, starting transfers between devices: none -> 29.6 us  [the longest x9 27.1 us: shift(): lax.ppermute(value, 'seq', [(j, (j + step) % shards) for j in range(shard...]
    all_to_all x5 -> x0, starting transfers between devices: 23.9 us -> none  [the longest x1 6.32 us: local(): lax.all_to_all(wanted[:, None], 'seq', split_axis=0, concat_axis=0, tiled...]
    psum x2 -> x0, waiting for transfers between devices: 19.8 us -> none  [the longest x1 19.8 us: local(): lax.psum((gkey_acc.reshape(-1, half_width), gvalue_acc.reshape(-1, half_w...]
    dot_general x13 -> x0, matrix products: 18.2 us -> none  [the longest x2 4.17 us: cluster_step(): jnp.einsum('hqk,khd->qhd', prob_rounded, all_values, preferred_element_ty...]
    scatter-add x8 -> x0, other arithmetic: 15.4 us -> none  [the longest x2 4.9 us: cluster_step(): value_acc.at[slot_block]]
  transfers between devices with their start and end apart: 8 -> 14, of which waited for: 6 -> 4; matrix products, arithmetic and copies ran while one was open for 10% -> 8% of each run, Pallas kernels for 0% -> 25%
where the time goes in v1:
time: 109 us; the launch traced here: 108 us
  Pallas kernels  39.7 us (36%)
  starting transfers between devices  29.6 us (27%)
  local copies, waits for them, and re-layouts  18.5 us (17%)
  waiting for transfers between devices  14.7 us (13%)
  other arithmetic  4.99 us (5%)
    pallas_call x4, Pallas kernels, local(): pl.pallas_call(functools.partial(attend_kernel, shard, total, lookups, fi...  29.8 us
    ppermute x9, starting transfers between devices, shift(): lax.ppermute(value, 'seq', [(j, (j + step) % shards) for j in range(shard...  27.1 us
    unnamed x30, local copies, waits for them, and re-layouts  13 us
    ppermute x5, waiting for transfers between devices, swap(): return lax.ppermute(value, axis, [(0, 1), (1, 0)])  10.8 us
    pallas_call x1, Pallas kernels, local(): pl.pallas_call(functools.partial(project_kernel, shards), out_shape=(jax....  5.12 us
    pallas_call x1, Pallas kernels, local(): pl.pallas_call(functools.partial(finish_kernel, shards, reps), out_shape=...  4.82 us
    ppermute x9, waiting for transfers between devices, shift(): lax.ppermute(value, 'seq', [(j, (j + step) % shards) for j in range(shard...  3.89 us
    pallas_call x1, local copies, waits for them, and re-layouts, local(): pl.pallas_call(functools.partial(project_kernel, shards), out_shape=(jax....  2.57 us
  transfers between devices with their start and end apart: 14, of which 4 were waited for; matrix products, arithmetic and copies ran while one was open for 8% of the time, Pallas kernels for 25%

profile of v1, /device:TPU:0, one launch (start us, length us, event | category | flops | bytes accessed | tf_op | source)
XLA Modules:
  0.0 108.2 jit_solution(11881970071074220269)
XLA Ops:
  0.6 5.1 %collective-permute-start.2 = (s32[2,2]{1,0:T(2,128)}, s32[2,2]{1,0:T(2,128)S(1)}, u32[]{:S(2)}, u32[]{:S(2)}) collective-permute-start(s32[2,2]{1,0:T(2,128)} %bitcast.31), channel_id=1, source_target_pairs={{0,12},{4,0},{8,4},{12,8},{1,13},{5,1},{9,5},{13,9},{2,14},{6,2},{... | collective-permute-start | bytes 56 | tf_op jit(solution)/shard_map/ppermute | solution.py:194
  5.7 1.0 collective-permute-start
  6.7 0.9 dynamic-slice_bitcast_fusion.1
  7.7 2.9 %collective-permute-start.5 = (bf16[128,768]{1,0:T(8,128)(2,1)S(1)}, bf16[128,768]{1,0:T(8,128)(2,1)S(1)}, u32[]{:S(2)}, u32[]{:S(2)}) collective-permute-start(bf16[128,768]{1,0:T(8,128)(2,1)S(1)} %dynamic-slice_bitcast_fusion.1), channel_id=1, source_target_pairs={{0,12},{4,0},{8,4},{12,8},{1,13},{5,1},{9,5},{13,9},{2,14},{6,2},{... | collective-permute-start | bytes 589832 | tf_op jit(solution)/shard_map/ppermute | solution.py:194
  10.6 1.1 %collective-permute-start.4 = (bf16[128,768]{1,0:T(8,128)(2,1)S(1)}, bf16[128,768]{1,0:T(8,128)(2,1)S(1)}, u32[]{:S(2)}, u32[]{:S(2)}) collective-permute-start(bf16[128,768]{1,0:T(8,128)(2,1)S(1)} %dynamic-slice_bitcast_fusion.1), channel_id=1, source_target_pairs={{0,8},{4,12},{8,0},{12,4},{1,9},{5,13},{9,1},{13,5},{2,10},{6,14},... | collective-permute-start | bytes 589832 | tf_op jit(solution)/shard_map/ppermute | solution.py:194
  15.9 16.9 %collective-permute-start.11 = (bf16[256,384]{1,0:T(8,128)(2,1)}, bf16[256,384]{1,0:T(8,128)(2,1)S(1)}, u32[]{:S(2)}, u32[]{:S(2)}) collective-permute-start(bf16[256,384]{1,0:T(8,128)(2,1)} %bitcast.26), channel_id=1, source_target_pairs={{0,4},{4,8},{8,12},{12,0},{1,5},{5,9},{9,13},{13,1},{2,6},{6,10},{... | collective-permute-start | bytes 589832 | tf_op jit(solution)/shard_map/ppermute | solution.py:194
  33.5 3.0 %collective-permute-done.4.refs_1_ = bf16[128,768]{1,0:T(8,128)(2,1)S(1)} collective-permute-done((bf16[128,768]{1,0:T(8,128)(2,1)S(1)}, bf16[128,768]{1,0:T(8,128)(2,1)S(1)}, u32[]{:S(2)}, u32[]{:S(2)}) %collective-permute-start.4) | collective-permute-done | bytes 196640 | tf_op jit(solution)/shard_map/ppermute | solution.py:194
  38.7 1.0 copy-done
  42.5 5.1 %project.1 = (bf16[1024,768]{1,0:T(8,128)(2,1)S(1)}, bf16[1024,384]{1,0:T(8,128)(2,1)S(1)}, bf16[1280,384]{1,0:T(8,128)(2,1)S(1)}, bf16[1280,384]{1,0:T(8,128)(2,1)S(1)}) custom-call(s32[1]{0:T(128)} %bitcast.5.core_ref, s32[256,1]{1,0:T(8,128)S(1)} %fusion.12.ids_ref, bf16[3,768,384]{2,1,0:T(8,128)(2,1)} %bitcast.24, bf16[256,768]{1,0:T(8,128)(2,1)S(1)} %bitcast.23, ...), custom_call_target="tpu_custom_call" | custom-call | tf_op jit(solution)/shard_map/project/pallas_call | solution.py:219
  47.6 1.2 %copy-done.7 = bf16[1024,768]{1,0:T(8,128)(2,1)} copy-done((bf16[1024,768]{1,0:T(8,128)(2,1)}, bf16[1024,768]{1,0:T(8,128)(2,1)S(1)}, u32[]{:S(2)}) %copy-start.7) | copy-done | bytes 1572888
  48.8 2.6 %copy.19 = bf16[1024,768]{0,1:T(8,128)(2,1)} copy(bf16[1024,768]{1,0:T(8,128)(2,1)} %copy-done.7) | data formatting | bytes 3145728 | tf_op jit(solution)/shard_map/project/pallas_call | solution.py:219
  52.3 6.3 %attend_0.1 = (bf16[256,384]{1,0:T(8,128)(2,1)S(1)}, f32[1280,384]{1,0:T(8,128)S(1)}, f32[1280,384]{1,0:T(8,128)}, bf16[256,384]{1,0:T(8,128)(2,1)}) custom-call(s32[16]{0:T(128)S(1)} %fusion.17.meta_ref, s32[16]{0:T(128)S(1)} %select_reduce_fusion.fill_ref, bf16[1024,384]{1,0:T(8,128)(2,1)S(1)} %get-tuple-element.24.q_ref, bf16[256,384]{1,0:T(8,128)(2,1)S(1)} %bitcast.29, ...), custom_call_target="tpu_custom_call" | custom-call | tf_op jit(solution)/shard_map/attend_0/pallas_call | solution.py:243
  58.6 1.3 %copy-done.6 = f32[1280,384]{1,0:T(8,128)} copy-done((f32[1280,384]{1,0:T(8,128)}, f32[1280,384]{1,0:T(8,128)S(1)}, u32[]{:S(2)}) %copy-start.6) | copy-done | bytes 1966104
  59.9 7.8 %attend_1.1 = (bf16[256,384]{1,0:T(8,128)(2,1)S(1)}, f32[1280,384]{1,0:T(8,128)S(1)}, f32[1280,384]{1,0:T(8,128)}) custom-call(s32[16]{0:T(128)S(1)} %fusion.17.meta_ref, s32[16]{0:T(128)S(1)} %select_reduce_fusion.fill_ref, bf16[1024,384]{1,0:T(8,128)(2,1)S(1)} %get-tuple-element.24.q_ref, bf16[256,384]{1,0:T(8,128)(2,1)S(1)} %collective-permute-done.11.dout_ref, ...), custom_call_target="tpu_custom_call" | custom-call | tf_op jit(solution)/shard_map/attend_1/pallas_call | solution.py:243
  67.6 1.3 %copy-done.5 = f32[1280,384]{1,0:T(8,128)} copy-done((f32[1280,384]{1,0:T(8,128)}, f32[1280,384]{1,0:T(8,128)S(1)}, u32[]{:S(2)}) %copy-start.5) | copy-done | bytes 1966104
  68.9 7.8 %attend_2.1 = (bf16[256,384]{1,0:T(8,128)(2,1)S(1)}, f32[1280,384]{1,0:T(8,128)S(1)}, f32[1280,384]{1,0:T(8,128)}) custom-call(s32[16]{0:T(128)S(1)} %fusion.17.meta_ref, s32[16]{0:T(128)S(1)} %select_reduce_fusion.fill_ref, bf16[1024,384]{1,0:T(8,128)(2,1)S(1)} %get-tuple-element.24.q_ref, bf16[256,384]{1,0:T(8,128)(2,1)S(1)} %collective-permute-done.10.dout_ref, ...), custom_call_target="tpu_custom_call" | custom-call | tf_op jit(solution)/shard_map/attend_2/pallas_call | solution.py:243
  76.7 1.3 %copy-done.3 = f32[1280,384]{1,0:T(8,128)} copy-done((f32[1280,384]{1,0:T(8,128)}, f32[1280,384]{1,0:T(8,128)S(1)}, u32[]{:S(2)}) %copy-start.3) | copy-done | bytes 1966104
  78.0 1.0 dynamic-slice_bitcast_fusion
  79.5 7.9 %attend_3.1 = (bf16[256,384]{1,0:T(8,128)(2,1)S(1)}, f32[1280,384]{1,0:T(8,128)S(1)}, f32[1280,384]{1,0:T(8,128)}) custom-call(s32[16]{0:T(128)S(1)} %fusion.17.meta_ref, s32[16]{0:T(128)S(1)} %select_reduce_fusion.fill_ref, bf16[1024,384]{1,0:T(8,128)(2,1)S(1)} %get-tuple-element.24.q_ref, bf16[256,384]{1,0:T(8,128)(2,1)S(1)} %collective-permute-done.9.dout_ref, ...), custom_call_target="tpu_custom_call" | custom-call | tf_op jit(solution)/shard_map/attend_3/pallas_call | solution.py:243
  87.4 1.3 %copy-done.4 = f32[1280,384]{1,0:T(8,128)} copy-done((f32[1280,384]{1,0:T(8,128)}, f32[1280,384]{1,0:T(8,128)S(1)}, u32[]{:S(2)}) %copy-start.4) | copy-done | bytes 1966104
  88.7 4.8 %finish.1 = (f32[3,96,384]{2,1,0:T(8,128)S(1)}, f32[3,96,384]{2,1,0:T(8,128)S(1)}, f32[256,768]{1,0:T(8,128)S(1)}) custom-call(s32[1]{0:T(128)} %bitcast.12.rep_ref, s32[1,256]{1,0:T(1,128)S(1)} %fusion.14.ids_ref, bf16[192,1024]{1,0:T(8,128)(2,1)S(1)} %fusion.7.slices_ref, bf16[3,768,384]{2,1,0:T(8,128)(2,1)S(1)} %bitcast.25, f32[1280,384]{1,0:T(8,128)} %copy-done.4, ...), custom_call_target="tpu_custom_call" | custom-call | tf_op jit(solution)/shard_map/finish/pallas_call | solution.py:258
  94.0 1.5 %collective-permute-start.13 = (f32[3,96,384]{2,1,0:T(8,128)S(1)}, f32[3,96,384]{2,1,0:T(8,128)S(1)}, u32[]{:S(2)}, u32[]{:S(2)}) collective-permute-start(f32[3,96,384]{2,1,0:T(8,128)S(1)} %get-tuple-element.44), channel_id=1, source_target_pairs={{0,2},{2,0},{1,3},{3,1},{4,6},{6,4},{5,7},{7,5},{8,10},{10,8},{9,1... | collective-permute-start | bytes 1327112 | tf_op jit(solution)/shard_map/ppermute | solution.py:197
  95.6 10.5 %collective-permute-done.13 = f32[3,96,384]{2,1,0:T(8,128)S(1)} collective-permute-done((f32[3,96,384]{2,1,0:T(8,128)S(1)}, f32[3,96,384]{2,1,0:T(8,128)S(1)}, u32[]{:S(2)}, u32[]{:S(2)}) %collective-permute-start.13) | collective-permute-done | bytes 442400 | tf_op jit(solution)/shard_map/ppermute | solution.py:197
  107.3 1.0 fusion.8
  (57 shorter events, 13.0 us)
Async XLA Ops:
  0.6 12.8 %collective-permute-start.2 = (s32[2,2]{1,0:T(2,128)}, s32[2,2]{1,0:T(2,128)S(1)}, u32[]{:S(2)}, u32[]{:S(2)}) collective-permute-start(s32[2,2]{1,0:T(2,128)} %bitcast.31), channel_id=1, source_target_pairs={{0,12},{4,0},{8,4},{12,8},{1,13},{5,1},{9,5},{13,9},{2,14},{6,2},{... | collective-permute-start | bytes 56 | tf_op jit(solution)/shard_map/ppermute | solution.py:194
  5.7 7.7 %collective-permute-start.1 = (s32[2,2]{1,0:T(2,128)}, s32[2,2]{1,0:T(2,128)S(1)}, u32[]{:S(2)}, u32[]{:S(2)}) collective-permute-start(s32[2,2]{1,0:T(2,128)} %bitcast.32), channel_id=1, source_target_pairs={{0,8},{4,12},{8,0},{12,4},{1,9},{5,13},{9,1},{13,5},{2,10},{6,14},... | collective-permute-start | bytes 56 | tf_op jit(solution)/shard_map/ppermute | solution.py:194
  5.7 7.7 %collective-permute-start = (s32[2,2]{1,0:T(2,128)}, s32[2,2]{1,0:T(2,128)S(1)}, u32[]{:S(2)}, u32[]{:S(2)}) collective-permute-start(s32[2,2]{1,0:T(2,128)} %bitcast.33), channel_id=1, source_target_pairs={{0,4},{4,8},{8,12},{12,0},{1,5},{5,9},{9,13},{13,1},{2,6},{6,10},{... | collective-permute-start | bytes 56 | tf_op jit(solution)/shard_map/ppermute | solution.py:194
  7.7 8.2 %collective-permute-start.5 = (bf16[128,768]{1,0:T(8,128)(2,1)S(1)}, bf16[128,768]{1,0:T(8,128)(2,1)S(1)}, u32[]{:S(2)}, u32[]{:S(2)}) collective-permute-start(bf16[128,768]{1,0:T(8,128)(2,1)S(1)} %dynamic-slice_bitcast_fusion.1), channel_id=1, source_target_pairs={{0,12},{4,0},{8,4},{12,8},{1,13},{5,1},{9,5},{13,9},{2,14},{6,2},{... | collective-permute-start | bytes 589832 | tf_op jit(solution)/shard_map/ppermute | solution.py:194
  10.6 25.9 %collective-permute-start.4 = (bf16[128,768]{1,0:T(8,128)(2,1)S(1)}, bf16[128,768]{1,0:T(8,128)(2,1)S(1)}, u32[]{:S(2)}, u32[]{:S(2)}) collective-permute-start(bf16[128,768]{1,0:T(8,128)(2,1)S(1)} %dynamic-slice_bitcast_fusion.1), channel_id=1, source_target_pairs={{0,8},{4,12},{8,0},{12,4},{1,9},{5,13},{9,1},{13,5},{2,10},{6,14},... | collective-permute-start | bytes 589832 | tf_op jit(solution)/shard_map/ppermute | solution.py:194
  13.4 23.7 %collective-permute-start.3 = (bf16[128,768]{1,0:T(8,128)(2,1)S(1)}, bf16[128,768]{1,0:T(8,128)(2,1)S(1)}, u32[]{:S(2)}, u32[]{:S(2)}) collective-permute-start(bf16[128,768]{1,0:T(8,128)(2,1)S(1)} %dynamic-slice_bitcast_fusion.1), channel_id=1, source_target_pairs={{0,4},{4,8},{8,12},{12,0},{1,5},{5,9},{9,13},{13,1},{2,6},{6,10},{... | collective-permute-start | bytes 589832 | tf_op jit(solution)/shard_map/ppermute | solution.py:194
  15.9 44.0 %collective-permute-start.11 = (bf16[256,384]{1,0:T(8,128)(2,1)}, bf16[256,384]{1,0:T(8,128)(2,1)S(1)}, u32[]{:S(2)}, u32[]{:S(2)}) collective-permute-start(bf16[256,384]{1,0:T(8,128)(2,1)} %bitcast.26), channel_id=1, source_target_pairs={{0,4},{4,8},{8,12},{12,0},{1,5},{5,9},{9,13},{13,1},{2,6},{6,10},{... | collective-permute-start | bytes 589832 | tf_op jit(solution)/shard_map/ppermute | solution.py:194
  32.8 36.1 %collective-permute-start.10 = (bf16[256,384]{1,0:T(8,128)(2,1)}, bf16[256,384]{1,0:T(8,128)(2,1)S(1)}, u32[]{:S(2)}, u32[]{:S(2)}) collective-permute-start(bf16[256,384]{1,0:T(8,128)(2,1)} %bitcast.27), channel_id=1, source_target_pairs={{0,8},{4,12},{8,0},{12,4},{1,9},{5,13},{9,1},{13,5},{2,10},{6,14},... | collective-permute-start | bytes 589832 | tf_op jit(solution)/shard_map/ppermute | solution.py:194
  32.8 5.5 %collective-permute-start.8 = (bf16[128,768]{1,0:T(8,128)(2,1)S(1)}, bf16[128,768]{1,0:T(8,128)(2,1)S(1)}, u32[]{:S(2)}, u32[]{:S(2)}) collective-permute-start(bf16[128,768]{1,0:T(8,128)(2,1)S(1)} %collective-permute-done.5.refs_2_), channel_id=1, source_target_pairs={{0,1},{1,0},{2,3},{3,2},{4,5},{5,4},{6,7},{7,6},{8,9},{9,8},{10,11... | collective-permute-start | bytes 589832 | tf_op jit(solution)/shard_map/ppermute | solution.py:197
  36.5 2.0 %collective-permute-start.7 = (bf16[128,768]{1,0:T(8,128)(2,1)S(1)}, bf16[128,768]{1,0:T(8,128)(2,1)S(1)}, u32[]{:S(2)}, u32[]{:S(2)}) collective-permute-start(bf16[128,768]{1,0:T(8,128)(2,1)S(1)} %collective-permute-done.4.refs_1_), channel_id=1, source_target_pairs={{0,1},{1,0},{2,3},{3,2},{4,5},{5,4},{6,7},{7,6},{8,9},{9,8},{10,11... | collective-permute-start | bytes 589832 | tf_op jit(solution)/shard_map/ppermute | solution.py:197
  37.1 1.6 %collective-permute-start.6 = (bf16[128,768]{1,0:T(8,128)(2,1)S(1)}, bf16[128,768]{1,0:T(8,128)(2,1)S(1)}, u32[]{:S(2)}, u32[]{:S(2)}) collective-permute-start(bf16[128,768]{1,0:T(8,128)(2,1)S(1)} %collective-permute-done.3.refs_0_), channel_id=1, source_target_pairs={{0,1},{1,0},{2,3},{3,2},{4,5},{5,4},{6,7},{7,6},{8,9},{9,8},{10,11... | collective-permute-start | bytes 589832 | tf_op jit(solution)/shard_map/ppermute | solution.py:197
  38.4 41.1 %collective-permute-start.9 = (bf16[256,384]{1,0:T(8,128)(2,1)}, bf16[256,384]{1,0:T(8,128)(2,1)S(1)}, u32[]{:S(2)}, u32[]{:S(2)}) collective-permute-start(bf16[256,384]{1,0:T(8,128)(2,1)} %bitcast.28), channel_id=1, source_target_pairs={{0,12},{4,0},{8,4},{12,8},{1,13},{5,1},{9,5},{13,9},{2,14},{6,2},{... | collective-permute-start | bytes 589832 | tf_op jit(solution)/shard_map/ppermute | solution.py:194
  38.7 1.0 copy-start
  39.7 0.9 copy-start.9
  40.6 0.9 copy-start.11
  47.6 1.2 %copy-start.7 = (bf16[1024,768]{1,0:T(8,128)(2,1)}, bf16[1024,768]{1,0:T(8,128)(2,1)S(1)}, u32[]{:S(2)}) copy-start(bf16[1024,768]{1,0:T(8,128)(2,1)S(1)} %get-tuple-element.28) | copy-start | bytes 4718596
  58.6 1.3 %copy-start.6 = (f32[1280,384]{1,0:T(8,128)}, f32[1280,384]{1,0:T(8,128)S(1)}, u32[]{:S(2)}) copy-start(f32[1280,384]{1,0:T(8,128)S(1)} %get-tuple-element.30.refs_0_) | copy-start | bytes 5898244
  67.6 1.3 %copy-start.5 = (f32[1280,384]{1,0:T(8,128)}, f32[1280,384]{1,0:T(8,128)S(1)}, u32[]{:S(2)}) copy-start(f32[1280,384]{1,0:T(8,128)S(1)} %get-tuple-element.32.refs_0_) | copy-start | bytes 5898244
  76.7 1.3 %copy-start.3 = (f32[1280,384]{1,0:T(8,128)}, f32[1280,384]{1,0:T(8,128)S(1)}, u32[]{:S(2)}) copy-start(f32[1280,384]{1,0:T(8,128)S(1)} %get-tuple-element.34.refs_0_) | copy-start | bytes 5898244
  79.5 9.2 %copy-start.2 = (bf16[768,3,384]{2,0,1:T(8,128)(2,1)S(1)}, bf16[768,3,384]{2,0,1:T(8,128)(2,1)}, u32[]{:S(2)}) copy-start(bf16[768,3,384]{2,0,1:T(8,128)(2,1)} %param.8) | copy-start | bytes 5308420
  87.4 1.3 %copy-start.4 = (f32[1280,384]{1,0:T(8,128)}, f32[1280,384]{1,0:T(8,128)S(1)}, u32[]{:S(2)}) copy-start(f32[1280,384]{1,0:T(8,128)S(1)} %get-tuple-element.36.dk_ref) | copy-start | bytes 5898244
  88.7 6.8 %copy-start.1 = (bf16[1,256,768]{2,1,0:T(8,128)(2,1)S(1)}, bf16[1,256,768]{2,1,0:T(8,128)(2,1)}, u32[]{:S(2)}) copy-start(bf16[1,256,768]{2,1,0:T(8,128)(2,1)} %param.6) | copy-start | bytes 1179652
  93.5 13.5 %collective-permute-start.12 = (f32[256,768]{1,0:T(8,128)S(1)}, f32[256,768]{1,0:T(8,128)S(1)}, u32[]{:S(2)}, u32[]{:S(2)}) collective-permute-start(f32[256,768]{1,0:T(8,128)S(1)} %get-tuple-element.42), channel_id=1, source_target_pairs={{0,1},{1,0},{2,3},{3,2},{4,5},{5,4},{6,7},{7,6},{8,9},{9,8},{10,11... | collective-permute-start | bytes 2359304 | tf_op jit(solution)/shard_map/ppermute | solution.py:197
  94.0 12.2 %collective-permute-start.13 = (f32[3,96,384]{2,1,0:T(8,128)S(1)}, f32[3,96,384]{2,1,0:T(8,128)S(1)}, u32[]{:S(2)}, u32[]{:S(2)}) collective-permute-start(f32[3,96,384]{2,1,0:T(8,128)S(1)} %get-tuple-element.44), channel_id=1, source_target_pairs={{0,2},{2,0},{1,3},{3,1},{4,6},{6,4},{5,7},{7,5},{8,10},{10,8},{9,1... | collective-permute-start | bytes 1327112 | tf_op jit(solution)/shard_map/ppermute | solution.py:197
  (5 other events, 3.9 us)

commit v2 on v1

v2 whole, which is shorter than its diff:
```python
import functools

import jax
import jax.numpy as jnp
from jax import lax
from jax.experimental import pallas as pl
from jax.experimental.pallas import tpu as pltpu
from jax.sharding import PartitionSpec as P

HDIM = 64
GROUP_VERTICES = 128
PAIR = 2 * HDIM
TAIL = 16
CHUNK = 32
NORM_EPS = 1e-06
SCALE = HDIM ** (-0.5)
LOG2E = 1.4426950408889634
F32 = jnp.float32
BF16 = jnp.bfloat16
NT = (((1,), (1,)), ((), ()))
NN = (((1,), (0,)), ((), ()))
TN = (((0,), (0,)), ((), ()))

VMEM = pl.BlockSpec(memory_space=pltpu.VMEM)
SMEM = pl.BlockSpec(memory_space=pltpu.SMEM)
ANY = pl.BlockSpec(memory_space=pl.ANY)


def dot(a, b, dims=NN):
    return lax.dot_general(a, b, dims, preferred_element_type=F32)


def shape(dtype, *sizes):
    return jax.ShapeDtypeStruct(sizes, dtype)


def call(kernel, name, total, scalars, arrays, outs, scratch=(), micros=1, remote=()):
    spaces = [ANY if i in remote else VMEM for i in range(len(arrays))]
    return pl.pallas_call(
        kernel,
        out_shape=outs,
        in_specs=[SMEM] * len(scalars) + spaces,
        out_specs=(VMEM,) * len(outs),
        scratch_shapes=scratch,
        compiler_params=pltpu.CompilerParams(vmem_limit_bytes=(10 + 9 * total // 1024) << 20),
        cost_estimate=pl.CostEstimate(flops=micros * 10**9, bytes_accessed=0, transcendentals=0),
        name=name,
    )(*scalars, *arrays)


def prepare_kernel(place_ref, pairs_ref, x_ref, cotangent_ref, half_ref, dout_ref, sems):
    nodes, width = dout_ref.shape[0] - TAIL, dout_ref.shape[1]
    rows = half_ref.shape[0]
    start = pl.multiple_of(place_ref[1] * rows, rows)
    first = pltpu.make_async_copy(x_ref.at[pl.ds(start, rows), :], half_ref, sems.at[0])
    second = pltpu.make_async_copy(cotangent_ref, dout_ref.at[pl.ds(0, nodes), :], sems.at[1])
    first.start()
    second.start()
    lane = lax.broadcasted_iota(jnp.int32, (TAIL, width), 1)
    tail = jnp.zeros((TAIL, width), F32)
    clusters, lookups = pairs_ref.shape
    for index in range(clusters * lookups):
        entry = pairs_ref[index // lookups, index % lookups].astype(F32)
        tail = jnp.where(lane == index, entry, tail)
    dout_ref[nodes:, :] = tail.astype(BF16)
    first.wait()
    second.wait()


def norm(block):
    wide = block.astype(F32)
    inverse = lax.rsqrt(jnp.mean(wide * wide, -1, keepdims=True) + NORM_EPS)
    return (wide * inverse).astype(BF16)


def share_columns(place_ref, share, width):
    shift = place_ref[2] * place_ref[3]
    index = lax.broadcasted_iota(jnp.int32, (share, width), 0) + shift
    index = jnp.where(index >= share, index - share, index) + place_ref[0] * share
    columns = lax.broadcasted_iota(jnp.int32, (share, width), 1)
    return jnp.where(columns == index, 1.0, 0.0).astype(BF16)


def project_first_kernel(place_ref, row_ref, w_ref, x_ref, q_ref, k_ref, v_ref, left_ref, put_ref):
    normed = norm(x_ref[...])
    for i, ref in enumerate((q_ref, k_ref, v_ref)):
        ref[...] = dot(normed, w_ref[i]).astype(BF16)
    pick = share_columns(place_ref, left_ref.shape[0], normed.shape[1])
    left_ref[...] = dot(pick, normed, NT).astype(BF16)
    places = lax.broadcasted_iota(jnp.int32, put_ref.shape, 0)
    put_ref[...] = jnp.where(places == row_ref[...], 1.0, 0.0).astype(BF16)


def project_kernel(shards, place_ref, col_ref, w_ref, *refs):
    own, refs = refs[:4], refs[4:]
    near, refs = refs[: shards - 1], refs[shards - 1 :]
    far, refs = refs[: shards - 1], refs[shards - 1 :]
    q_ref, k_ref, v_ref, left_ref, normed_ref, sems = refs
    nodes = own[0].shape[0]
    rows = nodes // 2
    total = shards * nodes
    count = col_ref.shape[0]
    core = place_ref[1]
    copies = []
    for i, (ref, start) in enumerate(zip((q_ref, k_ref, v_ref), own)):
        copies.append(pltpu.make_async_copy(start, ref.at[pl.ds(0, nodes), :], sems.at[i]))
    copies.append(pltpu.make_async_copy(own[3], left_ref.at[:, pl.ds(0, nodes)], sems.at[3]))
    for copy in copies:
        copy.start()
    pick = share_columns(place_ref, left_ref.shape[0], normed_ref.shape[1])
    key_sum = jnp.zeros((count, k_ref.shape[1]), F32)
    value_sum = key_sum
    for shard in list(range(1, shards)) + [0]:
        span = slice(shard * nodes, (shard + 1) * nodes)
        if shard:
            mine = pl.multiple_of(core * rows, rows)
            other = pl.multiple_of((1 - core) * rows, rows)
            normed_ref[pl.ds(mine, rows), :] = norm(near[shard - 1][...])
            normed_ref[pl.ds(other, rows), :] = norm(far[shard - 1][...])
            normed = normed_ref[...]
            for i, ref in enumerate((q_ref, k_ref, v_ref)):
                ref[span, :] = dot(normed, w_ref[i]).astype(BF16)
            left_ref[:, span] = dot(pick, normed, NT).astype(BF16)
        else:
            for copy in copies:
                copy.wait()
        places = lax.broadcasted_iota(jnp.int32, (count, nodes), 1) + shard * nodes
        chosen = jnp.where(places == col_ref[...], 1.0, 0.0).astype(BF16)
        key_sum += dot(chosen, k_ref[span, :])
        value_sum += dot(chosen, v_ref[span, :])
    k_ref[total:, :] = key_sum.astype(BF16)
    v_ref[total:, :] = value_sum.astype(BF16)


def read_pairs(place_ref, fill_ref, dout_ref, nodes, clusters, lookups):
    tail = dout_ref[nodes:, :PAIR].astype(F32)
    lane = lax.broadcasted_iota(jnp.int32, tail.shape, 1)
    entries = []
    for index in range(clusters * lookups):
        cluster = jnp.max(jnp.where(lane == index, tail, 0.0)).astype(jnp.int32)
        block = (lax.div(cluster, clusters) ^ place_ref[0]) * clusters + lax.rem(cluster, clusters)
        entries.append((pl.multiple_of(block * GROUP_VERTICES, GROUP_VERTICES), fill_ref[cluster]))
    return [entries[i * lookups : (i + 1) * lookups] for i in range(clusters)]


def fold(block, op):
    result = block[:8]
    for start in range(8, block.shape[0], 8):
        result = op(result, block[start : start + 8])
    return result


def unit(slot, shard, total, entries, cluster, column, refs, accs, acc_cols, emit, scratch):
    q_ref, dout_ref, k_ref, v_ref = refs
    score_ref, dprob_ref, prob_ref, dscore_ref = (ref.at[slot] for ref in scratch)
    dk_ref, dv_ref = accs
    size = GROUP_VERTICES
    clusters = (dout_ref.shape[0] - TAIL) // size
    local_rows = len(entries) * size
    listed = local_rows + k_ref.shape[0] - total
    cols = slice(column, column + PAIR)
    state = {}
    places = [pl.ds(start, size) for start, _ in entries]
    places += [pl.ds(start, size) for start in range(total, k_ref.shape[0], size)]

    def split(block):
        low = lax.broadcasted_iota(jnp.int32, (size, PAIR), 1) < HDIM
        zero = jnp.zeros((), BF16)
        return jnp.concatenate([jnp.where(low, block, zero), jnp.where(low, zero, block)], 0)

    def load():
        start = (shard * clusters + cluster) * size
        real = lax.broadcasted_iota(jnp.int32, (size, 1), 0) < entries[0][1]
        douts = dout_ref[cluster * size : (cluster + 1) * size, cols]
        state["queries"] = split(q_ref[start : start + size, cols])
        state["douts"] = split(jnp.where(real, douts, jnp.zeros((), BF16)))

    def score_step(index):
        span = slice(index * size, (index + 1) * size)
        score_ref[span, :] = dot(k_ref[places[index], cols], state["queries"], NT)

    def dprob_step(index):
        span = slice(index * size, (index + 1) * size)
        dprob_ref[span, :] = dot(v_ref[places[index], cols], state["douts"], NT)

    def masked(start):
        block = score_ref[start : start + CHUNK, :]
        if start >= local_rows:
            return block
        slots = lax.broadcasted_iota(jnp.int32, (CHUNK, 2 * size), 0) + start % size
        return jnp.where(slots < entries[start // size][1], block, -1e30)

    def peak_step(start):
        part = fold(masked(start), jnp.maximum)
        state["peak"] = part if start == 0 else jnp.maximum(state["peak"], part)

    def term_step(start):
        if start == 0:
            state["peak"] = jnp.max(state["peak"], 0, keepdims=True)
        terms = jnp.exp2((masked(start) - state["peak"]) * (LOG2E * SCALE))
        weighted = fold(terms * dprob_ref[start : start + CHUNK, :], jnp.add)
        score_ref[start : start + CHUNK, :] = terms
        terms = fold(terms, jnp.add)
        state["sum"] = terms if start == 0 else state["sum"] + terms
        state["weighted"] = weighted if start == 0 else state["weighted"] + weighted

    def prob_step(start):
        if start == 0:
            state["inverse"] = 1.0 / jnp.sum(state["sum"], 0, keepdims=True)
            state["delta"] = jnp.sum(state["weighted"], 0, keepdims=True) * state["inverse"]
        span = slice(start, start + CHUNK)
        prob = score_ref[span, :] * state["inverse"]
        prob_ref[span, :] = prob.astype(BF16)
        dscore_ref[span, :] = (prob * (dprob_ref[span, :] - state["delta"])).astype(BF16)

    def value_step(index):
        span = slice(index * size, (index + 1) * size)
        dv_ref[places[index], acc_cols] += dot(prob_ref[span, :], state["douts"])

    def key_step(index):
        span = slice(index * size, (index + 1) * size)
        dk_ref[places[index], acc_cols] += dot(dscore_ref[span, :], state["queries"]) * SCALE

    def query_step():
        keys = jnp.concatenate([k_ref[place, cols] for place in places], 0)
        emit(cluster, column, joined(dot(keys, dscore_ref[...], TN) * SCALE).astype(BF16), prob_ref)

    step = functools.partial
    blocks, chunks = range(listed // size), range(0, listed, CHUNK)
    ahead = [load] + [step(f, i) for i in blocks for f in (score_step, dprob_step)]
    middle = [step(f, start) for f in (peak_step, term_step, prob_step) for start in chunks]
    behind = [step(f, i) for i in blocks for f in (value_step, key_step)] + [query_step]
    return ahead, middle, behind


def joined(block):
    size = GROUP_VERTICES
    return jnp.concatenate([block[:HDIM, :size], block[HDIM:, size:]], 0).T


def run_units(units):
    for step in units[0][0]:
        step()
    for index, (_, middle, _) in enumerate(units):
        beside = units[index - 1][2] if index else []
        beside = beside + (units[index + 1][0] if index + 1 < len(units) else [])
        done = 0
        for position, step in enumerate(middle):
            step()
            while done < (position + 1) * len(beside) // len(middle):
                beside[done]()
                done += 1
    for step in units[-1][2]:
        step()


def attend_kernel(shard, total, lookups, first, place_ref, fill_ref, q_ref, dout_ref, k_ref, v_ref, *refs):
    scratch, refs = refs[-4:], refs[:-4]
    if first:
        dq_ref, dk_ref, dv_ref, probs_ref = refs
        dk_ref[...] = jnp.zeros_like(dk_ref)
        dv_ref[...] = jnp.zeros_like(dv_ref)
    else:
        dk_in, dv_in, dq_ref, dk_ref, dv_ref = refs
        dk_ref[...] = dk_in[...]
        dv_ref[...] = dv_in[...]
    nodes, width = dq_ref.shape
    clusters = nodes // GROUP_VERTICES
    entries = read_pairs(place_ref, fill_ref, dout_ref, nodes, clusters, lookups)

    def emit(cluster, column, dq, prob_ref):
        dq_ref[cluster * GROUP_VERTICES : (cluster + 1) * GROUP_VERTICES, column : column + PAIR] = dq
        if first:
            probs_ref[cluster * (width // PAIR) + column // PAIR] = prob_ref[...]

    units = []
    for cluster in range(clusters):
        for column in range(0, width, PAIR):
            units.append(
                unit(
                    len(units) % 2, shard, total, entries[cluster], cluster, column,
                    (q_ref, dout_ref, k_ref, v_ref), (dk_ref, dv_ref),
                    slice(column, column + PAIR), emit, scratch,
                )
            )
    run_units(units)


def mix_kernel(total, lookups, place_ref, fill_ref, dout_ref, v_ref, probs_ref, out_ref):
    size = GROUP_VERTICES
    nodes, width = out_ref.shape
    clusters = nodes // size
    entries = read_pairs(place_ref, fill_ref, dout_ref, nodes, clusters, lookups)
    for cluster in range(clusters):
        real = lax.broadcasted_iota(jnp.int32, (size, 1), 0) < entries[cluster][0][1]
        for column in range(0, width, PAIR):
            cols = slice(column, column + PAIR)
            values = [v_ref[pl.ds(start, size), cols] for start, _ in entries[cluster]]
            values = jnp.concatenate(values + [v_ref[total:, cols]], 0)
            probs = probs_ref[cluster * (width // PAIR) + column // PAIR]
            mixed = jnp.where(real, joined(dot(values, probs, TN)), 0.0)
            out_ref[cluster * size : (cluster + 1) * size, cols] = mixed.astype(BF16)


def finish_kernel(shard, shards, total, lookups, column, place_ref, fill_ref, q_ref, dout_ref, k_ref, v_ref, *refs):
    scratch, refs = refs[-4:], refs[:-4]
    dk_in, dv_in, left_ref, put_ref = refs[:4]
    dq_refs, refs = refs[4 : 3 + shards], refs[3 + shards :]
    mine_ref, other_ref, own_ref, dk_ref, dv_ref, dq_ref = refs
    cols = slice(column, column + PAIR)
    dk_ref[...] = dk_in[:, cols]
    dv_ref[...] = dv_in[:, cols]
    nodes = dq_ref.shape[0]
    clusters = nodes // GROUP_VERTICES
    entries = read_pairs(place_ref, fill_ref, dout_ref, nodes, clusters, lookups)

    def emit(cluster, column, dq, prob_ref):
        dq_ref[cluster * GROUP_VERTICES : (cluster + 1) * GROUP_VERTICES, :] = dq

    run_units(
        [
            unit(
                cluster % 2, shard, total, entries[cluster], cluster, column,
                (q_ref, dout_ref, k_ref, v_ref), (dk_ref, dv_ref), slice(0, PAIR), emit, scratch,
            )
            for cluster in range(clusters)
        ]
    )
    share = mine_ref.shape[1]
    picked = []
    for ref in (dk_ref, dv_ref):
        wide = ref[total:, :]
        high = wide.astype(BF16)
        picked += [high, (wide - high.astype(F32)).astype(BF16)]
    picked = jnp.concatenate(picked, 1)
    sums = None
    order = iter(dq_refs)
    for block in range(shards):
        span = slice(block * nodes, (block + 1) * nodes)
        added = dot(put_ref[span, :], picked)
        dq = dq_ref[...] if block == shard else next(order)[:, cols]
        dk = (dk_ref[span, :] + (added[:, :PAIR] + added[:, PAIR : 2 * PAIR])).astype(BF16)
        dv = (dv_ref[span, :] + (added[:, 2 * PAIR : 3 * PAIR] + added[:, 3 * PAIR :])).astype(BF16)
        if block == 0:
            own_ref[0], own_ref[1], own_ref[2] = dq, dk, dv
        term = dot(left_ref[:, span], jnp.concatenate([dq, dk, dv], 1))
        sums = term if sums is None else sums + term
    for i in range(3):
        mine_ref[i] = sums[:share, i * PAIR : (i + 1) * PAIR]
        other_ref[i] = sums[share:, i * PAIR : (i + 1) * PAIR]


def node_kernel(w_ref, *refs):
    node_ref = refs[-1]
    total = None
    for i in range(3):
        grads = jnp.concatenate([ref[i] for ref in refs[:-1]], 1)
        part = dot(grads, w_ref[i], NT)
        total = part if total is None else total + part
    node_ref[...] = total


def join_kernel(*refs):
    out_ref = refs[-1]
    half = (len(refs) - 1) // 2
    for index in range(half):
        cols = slice(index * PAIR, (index + 1) * PAIR)
        out_ref[:, :, cols] = refs[index][...] + refs[half + index][...]


def local(node_features, result_cotangent, proj_weights, cluster_pairs, cluster_fill, global_nodes):
    features = node_features[0]
    cotangent = result_cotangent[0]
    pairs = cluster_pairs[0]
    fill = cluster_fill[0]
    global_ids = global_nodes[0]
    weights = jnp.transpose(proj_weights, (1, 0, 2))
    nodes, width = features.shape
    half_width = cotangent.shape[1]
    lookups = pairs.shape[1]
    shards = lax.axis_size("seq")
    reps = lax.axis_size("rep")
    me = lax.axis_index("seq")
    total = shards * nodes
    count = global_ids.shape[0]
    share = width // (shards * reps)
    place = jnp.stack([me, lax.axis_index("tp"), lax.axis_index("rep"), jnp.int32(share)])
    place = place.astype(jnp.int32)

    def trade(value, step):
        return lax.ppermute(value, "seq", [(j, j ^ step) for j in range(shards)])

    def swap(value, axis):
        return lax.ppermute(value, axis, [(0, 1), (1, 0)])

    half, dout = call(
        prepare_kernel, "prepare", total, (place, pairs), (features, cotangent),
        (shape(BF16, nodes // 2, width), shape(BF16, nodes + TAIL, half_width)),
        (pltpu.SemaphoreType.DMA((2,)),), remote=(0, 1),
    )
    steps = [1] + list(range(shards - 1, 1, -1))
    near = {step: trade(half, step) for step in steps}
    far = {step: swap(near[step], "tp") for step in steps}
    douts = {0: dout}
    for step in steps:
        ready, _ = lax.optimization_barrier((dout, near[step]))
        douts[step] = trade(ready, step)

    ids = ((global_ids // nodes) ^ me) * nodes + global_ids % nodes
    flat = shape(BF16, nodes, half_width)
    *own, put = call(
        project_first_kernel, "project_first", total, (place,), (ids[None, :], weights, features),
        (flat, flat, flat, shape(BF16, reps * share, nodes), shape(BF16, total, count)),
    )
    others = range(1, shards)
    q, k, v, left = call(
        functools.partial(project_kernel, shards), "project", total, (place,),
        (ids[:, None], weights, *own, *[near[i] for i in others], *[far[i] for i in others]),
        (
            shape(BF16, total, half_width),
            shape(BF16, total + count, half_width),
            shape(BF16, total + count, half_width),
            shape(BF16, reps * share, total),
        ),
        (pltpu.VMEM((nodes, width), BF16), pltpu.SemaphoreType.DMA((4,))),
        micros=4, remote=(2, 3, 4, 5),
    )

    acc = shape(F32, total + count, half_width)
    listed = lookups * GROUP_VERTICES + count
    grid = (listed, 2 * GROUP_VERTICES)
    probs = shape(BF16, nodes // GROUP_VERTICES * (half_width // PAIR), *grid)
    scratch = tuple(pltpu.VMEM((2,) + grid, kind) for kind in (F32, F32, BF16, BF16))
    dqs = {}
    dk = dv = kept = None
    for shard in [0] + steps[:-1]:
        first = shard == 0
        got = call(
            functools.partial(attend_kernel, shard, total, lookups, first), "attend_%d" % shard, total,
            (place, fill), (q, douts[shard], k, v) + (() if first else (dk, dv)),
            (flat, acc, acc) + ((probs,) if first else ()), scratch, micros=4,
        )
        dqs[shard], dk, dv = got[:3]
        if first:
            kept = got[3]
    last = steps[-1]
    mine, other, grads = [], [], []
    for column in range(0, half_width, PAIR):
        got = call(
            functools.partial(finish_kernel, last, shards, total, lookups, column),
            "finish_%d" % column, total, (place, fill),
            (q, douts[last], k, v, dk, dv, left, put) + tuple(dqs[i] for i in sorted(dqs)),
            (
                shape(F32, 3, share, PAIR),
                shape(F32, 3, (reps - 1) * share, PAIR),
                shape(BF16, 3, nodes, PAIR),
            ),
            (
                pltpu.VMEM((total + count, PAIR), F32),
                pltpu.VMEM((total + count, PAIR), F32),
                pltpu.VMEM((nodes, PAIR), BF16),
            ) + scratch,
            micros=3,
        )
        mine.append(got[0])
        other.append(got[1])
        grads.append(got[2])
    node_part = call(node_kernel, "node", total, (), (weights, *grads), (shape(F32, nodes, width),))[0]
    later, _ = lax.optimization_barrier((kept, node_part))
    mixed = call(
        functools.partial(mix_kernel, total, lookups), "mix", total, (place, fill), (dout, v, later), (flat,)
    )[0]

    if reps == 2:
        back = [swap(block, "rep") for block in other]
        grad_w = call(join_kernel, "join", total, (), (*mine, *back), (shape(F32, 3, share, half_width),))[0]
    else:
        whole = jnp.concatenate([jnp.concatenate(mine, 2), jnp.concatenate(other, 2)], 1)
        whole = jnp.roll(whole, place[2] * share, 1)
        grad_w = lax.psum_scatter(whole, "rep", scatter_dimension=1, tiled=True)
    node_grad = node_part + swap(node_part, "tp")
    wide = features.astype(F32)
    inverse = lax.rsqrt(jnp.mean(wide * wide, -1, keepdims=True) + NORM_EPS)
    normed32 = wide * inverse
    grad_x = inverse * (node_grad - normed32 * jnp.mean(normed32 * node_grad, -1, keepdims=True))
    return mixed[None], grad_x.astype(BF16)[None], jnp.transpose(grad_w, (1, 0, 2))


def solution(mesh):
    placed = (
        P(("groups", "rep"), "seq", None),
        P(("groups", "rep"), "seq", "tp"),
        P(None, None, "tp"),
        P(("groups", "rep"), "seq", None),
        P(("groups", "rep"), None),
        P(("groups", "rep"), None),
    )
    return jax.shard_map(
        local,
        mesh=mesh,
        in_specs=placed,
        out_specs=(
            P(("groups", "rep"), "seq", "tp"),
            P(("groups", "rep"), "seq", None),
            P(("groups", "seq", "rep"), None, "tp"),
        ),
        check_vma=False,
    )
```

time: 109 us -> 73.3 us (0.67)
  local copies, waits for them, and re-layouts: 18.5 us -> 2.75 us
  starting transfers between devices: 29.6 us -> 15.2 us
  Pallas kernels: 39.7 us -> 32.3 us
  waiting for transfers between devices: 14.7 us -> 20.4 us
  other arithmetic: 4.99 us -> 1.66 us
    ppermute x9 -> x6, starting transfers between devices: 27.1 us -> 11.1 us  [trade(): return lax.ppermute(value, 'seq', [(j, j ^ step) for j in range(shards)])]
    unnamed x30 -> x14, local copies, waits for them, and re-layouts: 13 us -> 2.62 us
    ppermute x9 -> x6, waiting for transfers between devices: 3.89 us -> 13.2 us  [trade(): return lax.ppermute(value, 'seq', [(j, j ^ step) for j in range(shards)])]
    pallas_call x6 -> x12, Pallas kernels: 39.7 us -> 32.3 us  [call(): pl.pallas_call(kernel, out_shape=outs, in_specs=[SMEM] * len(scalars) + s...]
    ppermute x5 -> x7, waiting for transfers between devices: 10.8 us -> 7.21 us  [swap(): return lax.ppermute(value, axis, [(0, 1), (1, 0)])]
    pallas_call x1 -> x0, local copies, waits for them, and re-layouts: 2.57 us -> none  [local(): pl.pallas_call(functools.partial(project_kernel, shards), out_shape=(jax....]
    ppermute x5 -> x7, starting transfers between devices: 2.44 us -> 4.16 us  [swap(): return lax.ppermute(value, axis, [(0, 1), (1, 0)])]
  transfers between devices with their start and end apart: 14 -> 13, of which waited for: 4 -> 6; matrix products, arithmetic and copies ran while one was open for 8% -> 1% of each run, Pallas kernels for 25% -> 30%
where the time goes in v2:
time: 73.3 us; the launch traced here: 73.1 us
  Pallas kernels  32.3 us (44%)
  waiting for transfers between devices  20.4 us (28%)
  starting transfers between devices  15.2 us (21%)
  local copies, waits for them, and re-layouts  2.75 us (4%)
  other arithmetic  1.66 us (2%)
  between operations  0.81 us (1%)
    pallas_call x12, Pallas kernels, call(): pl.pallas_call(kernel, out_shape=outs, in_specs=[SMEM] * len(scalars) + s...  32.3 us
    ppermute x6, waiting for transfers between devices, trade(): return lax.ppermute(value, 'seq', [(j, j ^ step) for j in range(shards)])  13.2 us
    ppermute x6, starting transfers between devices, trade(): return lax.ppermute(value, 'seq', [(j, j ^ step) for j in range(shards)])  11.1 us
    ppermute x7, waiting for transfers between devices, swap(): return lax.ppermute(value, axis, [(0, 1), (1, 0)])  7.21 us
    ppermute x7, starting transfers between devices, swap(): return lax.ppermute(value, axis, [(0, 1), (1, 0)])  4.16 us
    unnamed x14, local copies, waits for them, and re-layouts  2.62 us
  transfers between devices with their start and end apart: 13, of which 6 were waited for; matrix products, arithmetic and copies ran while one was open for 1% of the time, Pallas kernels for 30%

profile of v2, /device:TPU:0, one launch (start us, length us, event | category | flops | bytes accessed | tf_op | source)
XLA Modules:
  0.0 73.1 jit_solution(13399035475732454664)
XLA Ops:
  0.7 1.0 %copy-done = bf16[1,256,768]{2,1,0:T(8,128)(2,1)S(1)} copy-done((bf16[1,256,768]{2,1,0:T(8,128)(2,1)S(1)}, bf16[1,256,768]{2,1,0:T(8,128)(2,1)}, u32[]{:S(2)}) %copy-start) | copy-done | bytes 393240
  1.7 0.9 %copy-done.3 = bf16[1,256,384]{2,1,0:T(8,128)(2,1)S(1)} copy-done((bf16[1,256,384]{2,1,0:T(8,128)(2,1)S(1)}, bf16[1,256,384]{2,1,0:T(8,128)(2,1)}, u32[]{:S(2)}) %copy-start.3) | copy-done | bytes 196632
  3.3 1.1 %prepare.1 = (bf16[128,768]{1,0:T(8,128)(2,1)S(1)}, bf16[272,384]{1,0:T(8,128)(2,1)S(1)}) custom-call(s32[4]{0:T(128)S(1)} %pad_add_fusion.place_ref, s32[2,2]{1,0:T(2,128)S(1)} %bitcast.22, bf16[256,768]{1,0:T(8,128)(2,1)S(1)} %bitcast.16, bf16[256,384]{1,0:T(8,128)(2,1)S(1)} %bitcast.21), custom_call_target="tpu_custom_call" | custom-call | flops 1000000000 | tf_op jit(solution)/shard_map/prepare/pallas_call | solution.py:39
  4.4 3.1 %collective-permute-start = (bf16[128,768]{1,0:T(8,128)(2,1)S(1)}, bf16[128,768]{1,0:T(8,128)(2,1)S(1)}, u32[]{:S(2)}, u32[]{:S(2)}) collective-permute-start(bf16[128,768]{1,0:T(8,128)(2,1)S(1)} %get-tuple-element.42), channel_id=1, source_target_pairs={{0,4},{4,0},{8,12},{12,8},{1,5},{5,1},{9,13},{13,9},{2,6},{6,2},{1... | collective-permute-start | bytes 589832 | tf_op jit(solution)/shard_map/ppermute | solution.py:391
  7.5 2.6 %collective-permute-start.1 = (bf16[128,768]{1,0:T(8,128)(2,1)S(1)}, bf16[128,768]{1,0:T(8,128)(2,1)S(1)}, u32[]{:S(2)}, u32[]{:S(2)}) collective-permute-start(bf16[128,768]{1,0:T(8,128)(2,1)S(1)} %get-tuple-element.42), channel_id=1, source_target_pairs={{0,8},{4,12},{8,0},{12,4},{1,9},{5,13},{9,1},{13,5},{2,10},{6,14},... | collective-permute-start | bytes 589832 | tf_op jit(solution)/shard_map/ppermute | solution.py:391
  10.3 1.7 %project_first.1 = (bf16[256,384]{1,0:T(8,128)(2,1)S(1)}, bf16[256,384]{1,0:T(8,128)(2,1)S(1)}, bf16[256,384]{1,0:T(8,128)(2,1)S(1)}, bf16[192,256]{1,0:T(8,128)(2,1)S(1)}, bf16[1024,256]{1,0:T(8,128)(2,1)S(1)}) custom-call(s32[4]{0:T(128)S(1)} %pad_add_fusion.place_ref, s32[1,256]{1,0:T(1,128)S(1)} %fusion.15.row_ref, bf16[3,768,384]{2,1,0:T(8,128)(2,1)S(1)} %bitcast.18, ...), custom_call_target="tpu_custom_call" | custom-call | flops 1000000000 | tf_op jit(solution)/shard_map/project_first/pallas_call | solution.py:39
  12.0 3.9 %collective-permute-done.refs_4_ = bf16[128,768]{1,0:T(8,128)(2,1)S(1)} collective-permute-done((bf16[128,768]{1,0:T(8,128)(2,1)S(1)}, bf16[128,768]{1,0:T(8,128)(2,1)S(1)}, u32[]{:S(2)}, u32[]{:S(2)}) %collective-permute-start) | collective-permute-done | bytes 196640 | tf_op jit(solution)/shard_map/ppermute | solution.py:391
  15.9 8.8 %collective-permute-done.1.refs_5_ = bf16[128,768]{1,0:T(8,128)(2,1)S(1)} collective-permute-done((bf16[128,768]{1,0:T(8,128)(2,1)S(1)}, bf16[128,768]{1,0:T(8,128)(2,1)S(1)}, u32[]{:S(2)}, u32[]{:S(2)}) %collective-permute-start.1) | collective-permute-done | bytes 196640 | tf_op jit(solution)/shard_map/ppermute | solution.py:391
  25.3 2.9 %collective-permute-start.8 = (bf16[272,384]{1,0:T(8,128)(2,1)S(1)}, bf16[272,384]{1,0:T(8,128)(2,1)S(1)}, u32[]{:S(2)}, u32[]{:S(2)}) collective-permute-start(bf16[272,384]{1,0:T(8,128)(2,1)S(1)} %get-tuple-element.49.dout_ref), channel_id=1, source_target_pairs={{0,4},{4,0},{8,12},{12,8},{1,5},{5,1},{9,13},{13,9},{2,6},{6,2},{1... | collective-permute-start | bytes 626696 | tf_op jit(solution)/shard_map/ppermute | solution.py:391
  28.2 2.5 %collective-permute-start.7 = (bf16[272,384]{1,0:T(8,128)(2,1)S(1)}, bf16[272,384]{1,0:T(8,128)(2,1)S(1)}, u32[]{:S(2)}, u32[]{:S(2)}) collective-permute-start(bf16[272,384]{1,0:T(8,128)(2,1)S(1)} %get-tuple-element.49.dout_ref), channel_id=1, source_target_pairs={{0,12},{4,8},{8,4},{12,0},{1,13},{5,9},{9,5},{13,1},{2,14},{6,10},... | collective-permute-start | bytes 626696 | tf_op jit(solution)/shard_map/ppermute | solution.py:391
  30.7 4.8 %project.1 = (bf16[1024,384]{1,0:T(8,128)(2,1)S(1)}, bf16[1280,384]{1,0:T(8,128)(2,1)S(1)}, bf16[1280,384]{1,0:T(8,128)(2,1)S(1)}, bf16[192,1024]{1,0:T(8,128)(2,1)S(1)}) custom-call(s32[4]{0:T(128)S(1)} %pad_add_fusion.place_ref, s32[256,1]{1,0:T(8,128)S(1)} %fusion.10.col_ref, bf16[3,768,384]{2,1,0:T(8,128)(2,1)S(1)} %bitcast.19, ...), custom_call_target="tpu_custom_call" | custom-call | flops 4000000000 | tf_op jit(solution)/shard_map/project/pallas_call | solution.py:39
  35.5 4.3 %attend_0.1 = (bf16[256,384]{1,0:T(8,128)(2,1)S(1)}, f32[1280,384]{1,0:T(8,128)S(1)}, f32[1280,384]{1,0:T(8,128)S(1)}, bf16[6,512,256]{2,1,0:T(8,128)(2,1)S(1)}) custom-call(s32[4]{0:T(128)S(1)} %pad_add_fusion.place_ref, s32[8]{0:T(128)S(1)} %bitcast.23, bf16[1024,384]{1,0:T(8,128)(2,1)S(1)} %get-tuple-element.44.q_ref, ...), custom_call_target="tpu_custom_call" | custom-call | flops 4000000000 | tf_op jit(solution)/shard_map/attend_0/pallas_call | solution.py:39
  39.8 4.1 %attend_1.1 = (bf16[256,384]{1,0:T(8,128)(2,1)S(1)}, f32[1280,384]{1,0:T(8,128)S(1)}, f32[1280,384]{1,0:T(8,128)S(1)}) custom-call(s32[4]{0:T(128)S(1)} %pad_add_fusion.place_ref, s32[8]{0:T(128)S(1)} %bitcast.24, bf16[1024,384]{1,0:T(8,128)(2,1)S(1)} %get-tuple-element.44.q_ref, bf16[272,384]{1,0:T(8,128)(2,1)S(1)} %collective-permute-done.8.dout_ref, ...), custom_call_target="tpu_custom_call" | custom-call | flops 4000000000 | tf_op jit(solution)/shard_map/attend_1/pallas_call | solution.py:39
  44.0 4.3 %attend_3.1 = (bf16[256,384]{1,0:T(8,128)(2,1)S(1)}, f32[1280,384]{1,0:T(8,128)S(1)}, f32[1280,384]{1,0:T(8,128)S(1)}) custom-call(s32[4]{0:T(128)S(1)} %pad_add_fusion.place_ref, s32[8]{0:T(128)S(1)} %bitcast.25, bf16[1024,384]{1,0:T(8,128)(2,1)S(1)} %get-tuple-element.44.q_ref, bf16[272,384]{1,0:T(8,128)(2,1)S(1)} %collective-permute-done.7.dout_ref, ...), custom_call_target="tpu_custom_call" | custom-call | flops 4000000000 | tf_op jit(solution)/shard_map/attend_3/pallas_call | solution.py:39
  48.8 2.9 %finish_256.1 = (f32[3,96,128]{2,1,0:T(8,128)S(1)}, f32[3,96,128]{2,1,0:T(8,128)S(1)}, bf16[3,256,128]{2,1,0:T(8,128)(2,1)S(1)}) custom-call(s32[4]{0:T(128)S(1)} %pad_add_fusion.place_ref, s32[8]{0:T(128)S(1)} %bitcast.26, bf16[1024,384]{1,0:T(8,128)(2,1)S(1)} %get-tuple-element.44.q_ref, bf16[272,384]{1,0:T(8,128)(2,1)S(1)} %collective-permute-done.6.dout_ref, ...), custom_call_target="tpu_custom_call" | custom-call | flops 3000000000 | tf_op jit(solution)/shard_map/finish_256/pallas_call | solution.py:39
  51.6 2.9 %finish_128.1 = (f32[3,96,128]{2,1,0:T(8,128)S(1)}, f32[3,96,128]{2,1,0:T(8,128)S(1)}, bf16[3,256,128]{2,1,0:T(8,128)(2,1)S(1)}) custom-call(s32[4]{0:T(128)S(1)} %pad_add_fusion.place_ref, s32[8]{0:T(128)S(1)} %bitcast.27, bf16[1024,384]{1,0:T(8,128)(2,1)S(1)} %get-tuple-element.44.q_ref, bf16[272,384]{1,0:T(8,128)(2,1)S(1)} %collective-permute-done.6.dout_ref, ...), custom_call_target="tpu_custom_call" | custom-call | flops 3000000000 | tf_op jit(solution)/shard_map/finish_128/pallas_call | solution.py:39
  54.5 2.9 %finish_0.1 = (f32[3,96,128]{2,1,0:T(8,128)S(1)}, f32[3,96,128]{2,1,0:T(8,128)S(1)}, bf16[3,256,128]{2,1,0:T(8,128)(2,1)S(1)}) custom-call(s32[4]{0:T(128)S(1)} %pad_add_fusion.place_ref, s32[8]{0:T(128)S(1)} %bitcast.28, bf16[1024,384]{1,0:T(8,128)(2,1)S(1)} %get-tuple-element.44.q_ref, bf16[272,384]{1,0:T(8,128)(2,1)S(1)} %collective-permute-done.6.dout_ref, ...), custom_call_target="tpu_custom_call" | custom-call | flops 3000000000 | tf_op jit(solution)/shard_map/finish_0/pallas_call | solution.py:39
  58.4 1.6 %collective-permute-start.12 = (f32[3,96,128]{2,1,0:T(8,128)S(1)}, f32[3,96,128]{2,1,0:T(8,128)S(1)}, u32[]{:S(2)}, u32[]{:S(2)}) collective-permute-start(f32[3,96,128]{2,1,0:T(8,128)S(1)} %get-tuple-element.70), channel_id=1, source_target_pairs={{0,2},{2,0},{1,3},{3,1},{4,6},{6,4},{5,7},{7,5},{8,10},{10,8},{9,1... | collective-permute-start | bytes 442376 | tf_op jit(solution)/shard_map/ppermute | solution.py:394
  60.5 1.5 %collective-permute-start.10 = (f32[3,96,128]{2,1,0:T(8,128)S(1)}, f32[3,96,128]{2,1,0:T(8,128)S(1)}, u32[]{:S(2)}, u32[]{:S(2)}) collective-permute-start(f32[3,96,128]{2,1,0:T(8,128)S(1)} %get-tuple-element.68), channel_id=1, source_target_pairs={{0,2},{2,0},{1,3},{3,1},{4,6},{6,4},{5,7},{7,5},{8,10},{10,8},{9,1... | collective-permute-start | bytes 442376 | tf_op jit(solution)/shard_map/ppermute | solution.py:394
  62.0 1.8 %mix.1 = bf16[256,384]{1,0:T(8,128)(2,1)} custom-call(s32[4]{0:T(128)S(1)} %pad_add_fusion.place_ref, s32[8]{0:T(128)S(1)} %bitcast.29, bf16[272,384]{1,0:T(8,128)(2,1)S(1)} %get-tuple-element.49.dout_ref, bf16[1280,384]{1,0:T(8,128)(2,1)S(1)} %get-tuple-element.43.v_ref, bf16[6,512,256]{2,1,0:T(8,128)(2,1)S(1)} %get-tuple-element.64.probs_ref), custom_call_target="tpu_custom_call" | custom-call | flops 1000000000 | tf_op jit(solution)/shard_map/mix/pallas_call | solution.py:39
  63.8 1.3 %collective-permute-done.12.refs_5_ = f32[3,96,128]{2,1,0:T(8,128)S(1)} collective-permute-done((f32[3,96,128]{2,1,0:T(8,128)S(1)}, f32[3,96,128]{2,1,0:T(8,128)S(1)}, u32[]{:S(2)}, u32[]{:S(2)}) %collective-permute-start.12) | collective-permute-done | bytes 147488 | tf_op jit(solution)/shard_map/ppermute | solution.py:394
  65.1 3.2 %collective-permute-done.11.refs_4_ = f32[3,96,128]{2,1,0:T(8,128)S(1)} collective-permute-done((f32[3,96,128]{2,1,0:T(8,128)S(1)}, f32[3,96,128]{2,1,0:T(8,128)S(1)}, u32[]{:S(2)}, u32[]{:S(2)}) %collective-permute-start.11) | collective-permute-done | bytes 147488 | tf_op jit(solution)/shard_map/ppermute | solution.py:394
  68.2 2.8 %collective-permute-done.10.refs_3_ = f32[3,96,128]{2,1,0:T(8,128)S(1)} collective-permute-done((f32[3,96,128]{2,1,0:T(8,128)S(1)}, f32[3,96,128]{2,1,0:T(8,128)S(1)}, u32[]{:S(2)}, u32[]{:S(2)}) %collective-permute-start.10) | collective-permute-done | bytes 147488 | tf_op jit(solution)/shard_map/ppermute | solution.py:394
  72.2 1.0 %fusion.7 = bf16[1,256,768]{2,1,0:T(8,128)(2,1)} fusion(f32[256,768]{1,0:T(8,128)S(1)} %get-tuple-element.72, f32[256]{0:T(256)S(1)} %broadcast_multiply_fusion, f32[256]{0:T(256)S(1)} %add_rsqrt_fusion, bf16[1,256,768]{2,1,0:T(8,128)(2,1)S(1)} %copy-done.1), kind=kLoop, calls=%fused_computation.9 | loop fusion | flops 1179648 | bytes 1574912 | tf_op jit(solution)/shard_map/broadcast_in_dim | solution.py:486
  (37 shorter events, 4.7 us)
Async XLA Ops:
  0.6 9.5 %copy-start.6 = (s32[1,256]{1,0:T(1,128)S(1)}, s32[1,256]{1,0:T(1,128)}, u32[]{:S(2)}) copy-start(s32[1,256]{1,0:T(1,128)} %param.11) | copy-start | bytes 3076
  0.7 1.0 %copy-start = (bf16[1,256,768]{2,1,0:T(8,128)(2,1)S(1)}, bf16[1,256,768]{2,1,0:T(8,128)(2,1)}, u32[]{:S(2)}) copy-start(bf16[1,256,768]{2,1,0:T(8,128)(2,1)} %param.6) | copy-start | bytes 1179652
  1.7 0.9 %copy-start.3 = (bf16[1,256,384]{2,1,0:T(8,128)(2,1)S(1)}, bf16[1,256,384]{2,1,0:T(8,128)(2,1)}, u32[]{:S(2)}) copy-start(bf16[1,256,384]{2,1,0:T(8,128)(2,1)} %param.7) | copy-start | bytes 589828
  2.6 0.7 copy-start.4
  3.3 6.9 %copy-start.1 = (bf16[1,256,768]{2,1,0:T(8,128)(2,1)S(1)}, bf16[1,256,768]{2,1,0:T(8,128)(2,1)}, u32[]{:S(2)}) copy-start(bf16[1,256,768]{2,1,0:T(8,128)(2,1)} %param.6) | copy-start | bytes 1179652
  3.3 7.0 %copy-start.2 = (bf16[768,3,384]{2,0,1:T(8,128)(2,1)S(1)}, bf16[768,3,384]{2,0,1:T(8,128)(2,1)}, u32[]{:S(2)}) copy-start(bf16[768,3,384]{2,0,1:T(8,128)(2,1)} %param.8) | copy-start | bytes 5308420
  4.4 11.4 %collective-permute-start = (bf16[128,768]{1,0:T(8,128)(2,1)S(1)}, bf16[128,768]{1,0:T(8,128)(2,1)S(1)}, u32[]{:S(2)}, u32[]{:S(2)}) collective-permute-start(bf16[128,768]{1,0:T(8,128)(2,1)S(1)} %get-tuple-element.42), channel_id=1, source_target_pairs={{0,4},{4,0},{8,12},{12,8},{1,5},{5,1},{9,13},{13,9},{2,6},{6,2},{1... | collective-permute-start | bytes 589832 | tf_op jit(solution)/shard_map/ppermute | solution.py:391
  7.5 17.2 %collective-permute-start.1 = (bf16[128,768]{1,0:T(8,128)(2,1)S(1)}, bf16[128,768]{1,0:T(8,128)(2,1)S(1)}, u32[]{:S(2)}, u32[]{:S(2)}) collective-permute-start(bf16[128,768]{1,0:T(8,128)(2,1)S(1)} %get-tuple-element.42), channel_id=1, source_target_pairs={{0,8},{4,12},{8,0},{12,4},{1,9},{5,13},{9,1},{13,5},{2,10},{6,14},... | collective-permute-start | bytes 589832 | tf_op jit(solution)/shard_map/ppermute | solution.py:391
  10.1 14.6 %collective-permute-start.2 = (bf16[128,768]{1,0:T(8,128)(2,1)S(1)}, bf16[128,768]{1,0:T(8,128)(2,1)S(1)}, u32[]{:S(2)}, u32[]{:S(2)}) collective-permute-start(bf16[128,768]{1,0:T(8,128)(2,1)S(1)} %get-tuple-element.42), channel_id=1, source_target_pairs={{0,12},{4,8},{8,4},{12,0},{1,13},{5,9},{9,5},{13,1},{2,14},{6,10},... | collective-permute-start | bytes 589832 | tf_op jit(solution)/shard_map/ppermute | solution.py:391
  15.9 14.9 %collective-permute-start.3 = (bf16[128,768]{1,0:T(8,128)(2,1)S(1)}, bf16[128,768]{1,0:T(8,128)(2,1)S(1)}, u32[]{:S(2)}, u32[]{:S(2)}) collective-permute-start(bf16[128,768]{1,0:T(8,128)(2,1)S(1)} %collective-permute-done.refs_4_), channel_id=1, source_target_pairs={{0,1},{1,0},{2,3},{3,2},{4,5},{5,4},{6,7},{7,6},{8,9},{9,8},{10,11... | collective-permute-start | bytes 589832 | tf_op jit(solution)/shard_map/ppermute | solution.py:394
  24.7 6.0 %collective-permute-start.4 = (bf16[128,768]{1,0:T(8,128)(2,1)S(1)}, bf16[128,768]{1,0:T(8,128)(2,1)S(1)}, u32[]{:S(2)}, u32[]{:S(2)}) collective-permute-start(bf16[128,768]{1,0:T(8,128)(2,1)S(1)} %collective-permute-done.1.refs_5_), channel_id=1, source_target_pairs={{0,1},{1,0},{2,3},{3,2},{4,5},{5,4},{6,7},{7,6},{8,9},{9,8},{10,11... | collective-permute-start | bytes 589832 | tf_op jit(solution)/shard_map/ppermute | solution.py:394
  24.7 6.0 %collective-permute-start.5 = (bf16[128,768]{1,0:T(8,128)(2,1)S(1)}, bf16[128,768]{1,0:T(8,128)(2,1)S(1)}, u32[]{:S(2)}, u32[]{:S(2)}) collective-permute-start(bf16[128,768]{1,0:T(8,128)(2,1)S(1)} %collective-permute-done.2.refs_6_), channel_id=1, source_target_pairs={{0,1},{1,0},{2,3},{3,2},{4,5},{5,4},{6,7},{7,6},{8,9},{9,8},{10,11... | collective-permute-start | bytes 589832 | tf_op jit(solution)/shard_map/ppermute | solution.py:394
  25.3 14.5 %collective-permute-start.8 = (bf16[272,384]{1,0:T(8,128)(2,1)S(1)}, bf16[272,384]{1,0:T(8,128)(2,1)S(1)}, u32[]{:S(2)}, u32[]{:S(2)}) collective-permute-start(bf16[272,384]{1,0:T(8,128)(2,1)S(1)} %get-tuple-element.49.dout_ref), channel_id=1, source_target_pairs={{0,4},{4,0},{8,12},{12,8},{1,5},{5,1},{9,13},{13,9},{2,6},{6,2},{1... | collective-permute-start | bytes 626696 | tf_op jit(solution)/shard_map/ppermute | solution.py:391
  28.2 15.7 %collective-permute-start.7 = (bf16[272,384]{1,0:T(8,128)(2,1)S(1)}, bf16[272,384]{1,0:T(8,128)(2,1)S(1)}, u32[]{:S(2)}, u32[]{:S(2)}) collective-permute-start(bf16[272,384]{1,0:T(8,128)(2,1)S(1)} %get-tuple-element.49.dout_ref), channel_id=1, source_target_pairs={{0,12},{4,8},{8,4},{12,0},{1,13},{5,9},{9,5},{13,1},{2,14},{6,10},... | collective-permute-start | bytes 626696 | tf_op jit(solution)/shard_map/ppermute | solution.py:391
  30.7 18.0 %collective-permute-start.6 = (bf16[272,384]{1,0:T(8,128)(2,1)S(1)}, bf16[272,384]{1,0:T(8,128)(2,1)S(1)}, u32[]{:S(2)}, u32[]{:S(2)}) collective-permute-start(bf16[272,384]{1,0:T(8,128)(2,1)S(1)} %get-tuple-element.49.dout_ref), channel_id=1, source_target_pairs={{0,8},{4,12},{8,0},{12,4},{1,9},{5,13},{9,1},{13,5},{2,10},{6,14},... | collective-permute-start | bytes 626696 | tf_op jit(solution)/shard_map/ppermute | solution.py:391
  30.7 4.8 %copy-start.5 = (s32[1,8]{1,0:T(1,128)S(1)}, s32[1,8]{1,0:T(1,128)}, u32[]{:S(2)}) copy-start(s32[1,8]{1,0:T(1,128)} %param.10) | copy-start | bytes 100
  58.1 13.7 %collective-permute-start.9 = (f32[256,768]{1,0:T(8,128)S(1)}, f32[256,768]{1,0:T(8,128)S(1)}, u32[]{:S(2)}, u32[]{:S(2)}) collective-permute-start(f32[256,768]{1,0:T(8,128)S(1)} %node.1), channel_id=1, source_target_pairs={{0,1},{1,0},{2,3},{3,2},{4,5},{5,4},{6,7},{7,6},{8,9},{9,8},{10,11... | collective-permute-start | bytes 2359304 | tf_op jit(solution)/shard_map/ppermute | solution.py:394
  58.4 6.7 %collective-permute-start.12 = (f32[3,96,128]{2,1,0:T(8,128)S(1)}, f32[3,96,128]{2,1,0:T(8,128)S(1)}, u32[]{:S(2)}, u32[]{:S(2)}) collective-permute-start(f32[3,96,128]{2,1,0:T(8,128)S(1)} %get-tuple-element.70), channel_id=1, source_target_pairs={{0,2},{2,0},{1,3},{3,1},{4,6},{6,4},{5,7},{7,5},{8,10},{10,8},{9,1... | collective-permute-start | bytes 442376 | tf_op jit(solution)/shard_map/ppermute | solution.py:394
  59.9 8.3 %collective-permute-start.11 = (f32[3,96,128]{2,1,0:T(8,128)S(1)}, f32[3,96,128]{2,1,0:T(8,128)S(1)}, u32[]{:S(2)}, u32[]{:S(2)}) collective-permute-start(f32[3,96,128]{2,1,0:T(8,128)S(1)} %get-tuple-element.69), channel_id=1, source_target_pairs={{0,2},{2,0},{1,3},{3,1},{4,6},{6,4},{5,7},{7,5},{8,10},{10,8},{9,1... | collective-permute-start | bytes 442376 | tf_op jit(solution)/shard_map/ppermute | solution.py:394
  60.5 10.5 %collective-permute-start.10 = (f32[3,96,128]{2,1,0:T(8,128)S(1)}, f32[3,96,128]{2,1,0:T(8,128)S(1)}, u32[]{:S(2)}, u32[]{:S(2)}) collective-permute-start(f32[3,96,128]{2,1,0:T(8,128)S(1)} %get-tuple-element.68), channel_id=1, source_target_pairs={{0,2},{2,0},{1,3},{3,1},{4,6},{6,4},{5,7},{7,5},{8,10},{10,8},{9,1... | collective-permute-start | bytes 442376 | tf_op jit(solution)/shard_map/ppermute | solution.py:394

commit v3 on v2

v3 whole, which is shorter than its diff:
```python
import functools

import jax
import jax.numpy as jnp
from jax import lax
from jax.experimental import pallas as pl
from jax.experimental.pallas import tpu as pltpu
from jax.sharding import PartitionSpec as P

HDIM = 64
GROUP_VERTICES = 128
PAIR = 2 * HDIM
TAIL = 16
CHUNK = 32
BATCH = 4
NORM_EPS = 1e-06
SCALE = HDIM ** (-0.5)
LOG2E = 1.4426950408889634
F32 = jnp.float32
BF16 = jnp.bfloat16
NT = (((1,), (1,)), ((), ()))
NN = (((1,), (0,)), ((), ()))
TN = (((0,), (0,)), ((), ()))

VMEM = pl.BlockSpec(memory_space=pltpu.VMEM)
SMEM = pl.BlockSpec(memory_space=pltpu.SMEM)


def dot(a, b, dims=NN):
    return lax.dot_general(a, b, dims, preferred_element_type=F32)


def shape(dtype, *sizes):
    return jax.ShapeDtypeStruct(sizes, dtype)


def call(kernel, name, total, scalars, arrays, outs, scratch=(), micros=0):
    return pl.pallas_call(
        kernel,
        out_shape=outs,
        in_specs=[SMEM] * len(scalars) + [VMEM] * len(arrays),
        out_specs=(VMEM,) * len(outs),
        scratch_shapes=scratch,
        compiler_params=pltpu.CompilerParams(vmem_limit_bytes=(10 + 9 * total // 1024) << 20),
        cost_estimate=pl.CostEstimate(flops=micros * 10**9, bytes_accessed=0, transcendentals=0),
        name=name,
    )(*scalars, *arrays)


def prepare_kernel(pairs_ref, cotangent_ref, dout_ref):
    nodes, width = cotangent_ref.shape
    dout_ref[:nodes, :] = cotangent_ref[...]
    row = lax.broadcasted_iota(jnp.int32, (TAIL, width), 0)
    lane = lax.broadcasted_iota(jnp.int32, (TAIL, width), 1)
    tail = jnp.zeros((TAIL, width), F32)
    clusters, lookups = pairs_ref.shape
    for index in range(clusters * lookups):
        entry = pairs_ref[index // lookups, index % lookups].astype(F32)
        tail = jnp.where((row == 0) & (lane == index), entry, tail)
    dout_ref[nodes:, :] = tail.astype(BF16)


def norm(block):
    wide = block.astype(F32)
    inverse = lax.rsqrt(jnp.mean(wide * wide, -1, keepdims=True) + NORM_EPS)
    return (wide * inverse).astype(BF16)


def share_columns(share, width):
    shift = lax.axis_index("rep") * (share // lax.axis_size("rep"))
    index = lax.broadcasted_iota(jnp.int32, (share, width), 0) + shift
    index = jnp.where(index >= share, index - share, index) + lax.axis_index("seq") * share
    columns = lax.broadcasted_iota(jnp.int32, (share, width), 1)
    return jnp.where(columns == index, 1.0, 0.0).astype(BF16)


def project_first_kernel(row_ref, col_ref, w_ref, x_ref, q_ref, k_ref, v_ref, left_ref, put_ref, pick_ref):
    normed = norm(x_ref[...])
    for i, ref in enumerate((q_ref, k_ref, v_ref)):
        ref[...] = dot(normed, w_ref[i]).astype(BF16)
    left_ref[...] = dot(share_columns(*left_ref.shape[:1], normed.shape[1]), normed, NT).astype(BF16)
    places = lax.broadcasted_iota(jnp.int32, put_ref.shape, 0)
    put_ref[...] = jnp.where(places == row_ref[...], 1.0, 0.0).astype(BF16)
    places = lax.broadcasted_iota(jnp.int32, pick_ref.shape, 1)
    pick_ref[...] = jnp.where(places == col_ref[...], 1.0, 0.0).astype(BF16)


def project_next_kernel(w_ref, near_ref, far_ref, q_ref, k_ref, v_ref, left_ref, normed_ref):
    rows = near_ref.shape[0]
    core = lax.axis_index("tp")
    normed_ref[pl.ds(pl.multiple_of(core * rows, rows), rows), :] = norm(near_ref[...])
    normed_ref[pl.ds(pl.multiple_of((1 - core) * rows, rows), rows), :] = norm(far_ref[...])
    normed = normed_ref[...]
    for i, ref in enumerate((q_ref, k_ref, v_ref)):
        ref[...] = dot(normed, w_ref[i]).astype(BF16)
    left_ref[...] = dot(share_columns(*left_ref.shape[:1], normed.shape[1]), normed, NT).astype(BF16)


def project_kernel(shards, w_ref, pick_ref, *refs):
    early, refs = refs[:8], refs[8:]
    near, refs = refs[: shards - 2], refs[shards - 2 :]
    far, refs = refs[: shards - 2], refs[shards - 2 :]
    q_ref, k_ref, v_ref, left_ref, normed_ref = refs
    nodes = early[0].shape[0]
    rows = nodes // 2
    total = shards * nodes
    core = lax.axis_index("tp")
    for i, early_ref in enumerate(early):
        span = slice(i // 4 * nodes, (i // 4 + 1) * nodes)
        if i % 4 == 3:
            left_ref[:, span] = early_ref[...]
        else:
            (q_ref, k_ref, v_ref)[i % 4][span, :] = early_ref[...]
    for shard in range(2, shards):
        mine = pl.multiple_of((shard - 2) * nodes + core * rows, rows)
        other = pl.multiple_of((shard - 2) * nodes + (1 - core) * rows, rows)
        normed_ref[pl.ds(mine, rows), :] = norm(near[shard - 2][...])
        normed_ref[pl.ds(other, rows), :] = norm(far[shard - 2][...])
    columns = share_columns(left_ref.shape[0], normed_ref.shape[1])
    for start in range(2 * nodes, total, BATCH * nodes):
        stop = min(start + BATCH * nodes, total)
        normed = normed_ref[start - 2 * nodes : stop - 2 * nodes, :]
        for i, ref in enumerate((q_ref, k_ref, v_ref)):
            ref[start:stop, :] = dot(normed, w_ref[i]).astype(BF16)
        left_ref[:, start:stop] = dot(columns, normed, NT).astype(BF16)
    key_sum = value_sum = None
    for start in range(0, total, BATCH * nodes):
        stop = min(start + BATCH * nodes, total)
        pick = pick_ref[:, start:stop]
        keys, values = dot(pick, k_ref[start:stop, :]), dot(pick, v_ref[start:stop, :])
        key_sum = keys if start == 0 else key_sum + keys
        value_sum = values if start == 0 else value_sum + values
    k_ref[total:, :] = key_sum.astype(BF16)
    v_ref[total:, :] = value_sum.astype(BF16)


def read_pairs(fill_ref, dout_ref, nodes, clusters, lookups):
    tail = dout_ref[nodes:, :PAIR].astype(F32)
    lane = lax.broadcasted_iota(jnp.int32, tail.shape, 1)
    base = fill_ref.shape[0]
    weight = jnp.zeros(tail.shape, F32)
    for index in range(clusters * lookups):
        weight = jnp.where(lane == index, float(base**index), weight)
    code = jnp.sum(tail * weight).astype(jnp.int32)
    me = lax.axis_index("seq")
    entries = []
    for index in range(clusters * lookups):
        cluster = lax.rem(lax.div(code, base**index), base)
        block = (lax.div(cluster, clusters) ^ me) * clusters + lax.rem(cluster, clusters)
        entries.append((pl.multiple_of(block * GROUP_VERTICES, GROUP_VERTICES), fill_ref[cluster]))
    return [entries[i * lookups : (i + 1) * lookups] for i in range(clusters)]


def fold(block, op):
    result = block[:8]
    for start in range(8, block.shape[0], 8):
        result = op(result, block[start : start + 8])
    return result


def unit(slot, shard, total, entries, cluster, column, refs, accs, acc_cols, emit, scratch):
    q_ref, dout_ref, k_ref, v_ref = refs
    score_ref, dprob_ref, prob_ref, dscore_ref = (ref.at[slot] for ref in scratch)
    dk_ref, dv_ref = accs
    size = GROUP_VERTICES
    clusters = (dout_ref.shape[0] - TAIL) // size
    local_rows = len(entries) * size
    listed = local_rows + k_ref.shape[0] - total
    cols = slice(column, column + PAIR)
    state = {}
    places = [pl.ds(start, size) for start, _ in entries]
    places += [pl.ds(start, size) for start in range(total, k_ref.shape[0], size)]

    def split(block):
        low = lax.broadcasted_iota(jnp.int32, (size, PAIR), 1) < HDIM
        zero = jnp.zeros((), BF16)
        return jnp.concatenate([jnp.where(low, block, zero), jnp.where(low, zero, block)], 0)

    def load():
        start = (shard * clusters + cluster) * size
        real = lax.broadcasted_iota(jnp.int32, (size, 1), 0) < entries[0][1]
        douts = dout_ref[cluster * size : (cluster + 1) * size, cols]
        state["queries"] = split(q_ref[start : start + size, cols])
        state["douts"] = split(jnp.where(real, douts, jnp.zeros((), BF16)))

    def score_step(index):
        span = slice(index * size, (index + 1) * size)
        score_ref[span, :] = dot(k_ref[places[index], cols], state["queries"], NT)

    def dprob_step(index):
        span = slice(index * size, (index + 1) * size)
        dprob_ref[span, :] = dot(v_ref[places[index], cols], state["douts"], NT)

    def masked(start):
        block = score_ref[start : start + CHUNK, :]
        if start >= local_rows:
            return block
        slots = lax.broadcasted_iota(jnp.int32, (CHUNK, 2 * size), 0) + start % size
        return jnp.where(slots < entries[start // size][1], block, -1e30)

    def peak_step(start):
        part = fold(masked(start), jnp.maximum)
        state["peak"] = part if start == 0 else jnp.maximum(state["peak"], part)

    def term_step(start):
        if start == 0:
            state["peak"] = jnp.max(state["peak"], 0, keepdims=True)
        terms = jnp.exp2((masked(start) - state["peak"]) * (LOG2E * SCALE))
        weighted = fold(terms * dprob_ref[start : start + CHUNK, :], jnp.add)
        score_ref[start : start + CHUNK, :] = terms
        terms = fold(terms, jnp.add)
        state["sum"] = terms if start == 0 else state["sum"] + terms
        state["weighted"] = weighted if start == 0 else state["weighted"] + weighted

    def prob_step(start):
        if start == 0:
            state["inverse"] = 1.0 / jnp.sum(state["sum"], 0, keepdims=True)
            state["delta"] = jnp.sum(state["weighted"], 0, keepdims=True) * state["inverse"]
        span = slice(start, start + CHUNK)
        prob = score_ref[span, :] * state["inverse"]
        prob_ref[span, :] = prob.astype(BF16)
        dscore_ref[span, :] = (prob * (dprob_ref[span, :] - state["delta"])).astype(BF16)

    def value_step(index):
        span = slice(index * size, (index + 1) * size)
        dv_ref[places[index], acc_cols] += dot(prob_ref[span, :], state["douts"])

    def key_step(index):
        span = slice(index * size, (index + 1) * size)
        dk_ref[places[index], acc_cols] += dot(dscore_ref[span, :], state["queries"]) * SCALE

    def query_step():
        keys = jnp.concatenate([k_ref[place, cols] for place in places], 0)
        emit(cluster, column, joined(dot(keys, dscore_ref[...], TN) * SCALE).astype(BF16), prob_ref)

    step = functools.partial
    blocks, chunks = range(listed // size), range(0, listed, CHUNK)
    ahead = [load] + [step(f, i) for i in blocks for f in (score_step, dprob_step)]
    middle = [step(f, start) for f in (peak_step, term_step, prob_step) for start in chunks]
    behind = [step(f, i) for i in blocks for f in (value_step, key_step)] + [query_step]
    return ahead, middle, behind


def joined(block):
    size = GROUP_VERTICES
    return jnp.concatenate([block[:HDIM, :size], block[HDIM:, size:]], 0).T


def run_units(units):
    for step in units[0][0]:
        step()
    for index, (_, middle, _) in enumerate(units):
        beside = units[index - 1][2] if index else []
        beside = beside + (units[index + 1][0] if index + 1 < len(units) else [])
        done = 0
        for position, step in enumerate(middle):
            step()
            while done < (position + 1) * len(beside) // len(middle):
                beside[done]()
                done += 1
    for step in units[-1][2]:
        step()


def attend_kernel(group, total, lookups, first, fill_ref, q_ref, k_ref, v_ref, *refs):
    scratch, refs = refs[-4:], refs[:-4]
    dout_refs, refs = refs[: len(group)], refs[len(group) :]
    if first:
        dk_ref, dv_ref, probs_ref, *dq_refs = refs
        dk_ref[...] = jnp.zeros_like(dk_ref)
        dv_ref[...] = jnp.zeros_like(dv_ref)
    else:
        dk_in, dv_in, dk_ref, dv_ref, *dq_refs = refs
        dk_ref[...] = dk_in[...]
        dv_ref[...] = dv_in[...]
    nodes, width = dq_refs[0].shape
    clusters = nodes // GROUP_VERTICES

    def emit_to(shard, dq_ref):
        def emit(cluster, column, dq, prob_ref):
            dq_ref[cluster * GROUP_VERTICES : (cluster + 1) * GROUP_VERTICES, column : column + PAIR] = dq
            if shard == 0:
                probs_ref[cluster * (width // PAIR) + column // PAIR] = prob_ref[...]

        return emit

    units = []
    for shard, dout_ref, dq_ref in zip(group, dout_refs, dq_refs):
        entries = read_pairs(fill_ref, dout_ref, nodes, clusters, lookups)
        for cluster in range(clusters):
            for column in range(0, width, PAIR):
                units.append(
                    unit(
                        len(units) % 2, shard, total, entries[cluster], cluster, column,
                        (q_ref, dout_ref, k_ref, v_ref), (dk_ref, dv_ref),
                        slice(column, column + PAIR), emit_to(shard, dq_ref), scratch,
                    )
                )
    run_units(units)


def mix_kernel(total, lookups, fill_ref, dout_ref, v_ref, probs_ref, out_ref):
    size = GROUP_VERTICES
    nodes, width = out_ref.shape
    clusters = nodes // size
    entries = read_pairs(fill_ref, dout_ref, nodes, clusters, lookups)
    for cluster in range(clusters):
        real = lax.broadcasted_iota(jnp.int32, (size, 1), 0) < entries[cluster][0][1]
        for column in range(0, width, PAIR):
            cols = slice(column, column + PAIR)
            values = [v_ref[pl.ds(start, size), cols] for start, _ in entries[cluster]]
            values = jnp.concatenate(values + [v_ref[total:, cols]], 0)
            probs = probs_ref[cluster * (width // PAIR) + column // PAIR]
            mixed = jnp.where(real, joined(dot(values, probs, TN)), 0.0)
            out_ref[cluster * size : (cluster + 1) * size, cols] = mixed.astype(BF16)


def finish_kernel(shard, shards, total, lookups, column, final, fill_ref, q_ref, dout_ref, k_ref, v_ref, *refs):
    scratch, refs = refs[-4:], refs[:-4]
    dk_in, dv_in, left_ref, put_ref = refs[:4]
    dq_refs, refs = refs[4 : 3 + shards], refs[3 + shards :]
    own_refs = []
    if final:
        w_ref, own_refs, refs = refs[0], list(refs[1 : 1 + column // PAIR]), refs[1 + column // PAIR :]
    mine_ref, other_ref, own_ref, dk_ref, dv_ref, dq_ref, all_ref = refs
    cols = slice(column, column + PAIR)
    dk_ref[...] = dk_in[:, cols]
    dv_ref[...] = dv_in[:, cols]
    nodes = dq_ref.shape[0]
    clusters = nodes // GROUP_VERTICES
    entries = read_pairs(fill_ref, dout_ref, nodes, clusters, lookups)

    def emit(cluster, column, dq, prob_ref):
        dq_ref[cluster * GROUP_VERTICES : (cluster + 1) * GROUP_VERTICES, :] = dq

    run_units(
        [
            unit(
                cluster % 2, shard, total, entries[cluster], cluster, column,
                (q_ref, dout_ref, k_ref, v_ref), (dk_ref, dv_ref), slice(0, PAIR), emit, scratch,
            )
            for cluster in range(clusters)
        ]
    )
    share = mine_ref.shape[1]
    wide = jnp.concatenate([dk_ref[total:, :], dv_ref[total:, :]], 1)
    high = wide.astype(BF16)
    picked = jnp.concatenate([high, (wide - high.astype(F32)).astype(BF16)], 0)
    order = iter(dq_refs)
    for block in range(shards):
        span = slice(block * nodes, (block + 1) * nodes)
        put = put_ref[span, :]
        added = dot(jnp.concatenate([put, put], 1), picked)
        all_ref[span, :PAIR] = dq_ref[...] if block == shard else next(order)[:, cols]
        all_ref[span, PAIR : 2 * PAIR] = (dk_ref[span, :] + added[:, :PAIR]).astype(BF16)
        all_ref[span, 2 * PAIR :] = (dv_ref[span, :] + added[:, PAIR:]).astype(BF16)
    sums = None
    for start in range(0, total, BATCH * nodes):
        stop = min(start + BATCH * nodes, total)
        term = dot(left_ref[:, start:stop], all_ref[start:stop, :])
        sums = term if start == 0 else sums + term
    for i in range(3):
        mine_ref[i] = sums[:share, i * PAIR : (i + 1) * PAIR]
        other_ref[i] = sums[share:, i * PAIR : (i + 1) * PAIR]
    if not final:
        own_ref[...] = all_ref[:nodes, :]
        return
    node = None
    for i in range(3):
        part = slice(i * PAIR, (i + 1) * PAIR)
        grads = [ref[:, part] for ref in own_refs] + [all_ref[:nodes, part]]
        term = dot(jnp.concatenate(grads, 1), w_ref[i], NT)
        node = term if node is None else node + term
    own_ref[...] = node


def features_kernel(x_ref, mine_ref, other_ref, out_ref):
    wide = x_ref[...].astype(F32)
    inverse = lax.rsqrt(jnp.mean(wide * wide, -1, keepdims=True) + NORM_EPS)
    normed = wide * inverse
    grad = mine_ref[...] + other_ref[...]
    out_ref[...] = (inverse * (grad - normed * jnp.mean(normed * grad, -1, keepdims=True))).astype(BF16)


def join_kernel(*refs):
    out_ref = refs[-1]
    half = (len(refs) - 1) // 2
    for index in range(half):
        cols = slice(index * PAIR, (index + 1) * PAIR)
        out_ref[:, :, cols] = refs[index][...] + refs[half + index][...]


def local(node_features, result_cotangent, proj_weights, cluster_pairs, cluster_fill, global_nodes):
    features = node_features[0]
    cotangent = result_cotangent[0]
    pairs = cluster_pairs[0]
    fill = cluster_fill[0]
    global_ids = global_nodes[0]
    weights = jnp.transpose(proj_weights, (1, 0, 2))
    nodes, width = features.shape
    half_width = cotangent.shape[1]
    lookups = pairs.shape[1]
    shards = lax.axis_size("seq")
    reps = lax.axis_size("rep")
    me = lax.axis_index("seq")
    total = shards * nodes
    count = global_ids.shape[0]
    share = width // (shards * reps)

    def trade(value, step):
        return lax.ppermute(value, "seq", [(j, j ^ step) for j in range(shards)])

    def swap(value, axis):
        return lax.ppermute(value, axis, [(0, 1), (1, 0)])

    half = lax.dynamic_slice_in_dim(features, lax.axis_index("tp") * (nodes // 2), nodes // 2)
    steps = list(range(1, shards))
    near = {step: trade(half, step) for step in steps}
    far = {1: swap(near[1], "tp")}
    ready, _ = lax.optimization_barrier((cotangent, near[1]))
    dout = call(
        prepare_kernel, "prepare", total, (pairs,), (ready,), (shape(BF16, nodes + TAIL, half_width),),
        micros=1,
    )[0]
    douts = {0: dout, 1: trade(dout, 1)}
    ids = ((global_ids // nodes) ^ me) * nodes + global_ids % nodes
    flat = shape(BF16, nodes, half_width)
    columns = shape(BF16, reps * share, nodes)
    *first, put, pick = call(
        project_first_kernel, "project_first", total, (),
        (ids[None, :], ids[:, None], weights, features),
        (flat, flat, flat, columns, shape(BF16, total, count), shape(BF16, count, total)), micros=2,
    )
    second = call(
        project_next_kernel, "project_next", total, (), (weights, near[1], far[1]),
        (flat, flat, flat, columns), (pltpu.VMEM((nodes, width), BF16),), micros=2,
    )
    for step in steps[1:]:
        near[step], _ = lax.optimization_barrier((near[step], (first[0], second[0])))
        far[step] = swap(near[step], "tp")
    ready, _ = lax.optimization_barrier((dout, [near[step] for step in steps]))
    for step in steps[1:]:
        douts[step] = trade(ready, step)
    q, k, v, left = call(
        functools.partial(project_kernel, shards), "project", total, (),
        (weights, pick, *first, *second, *[near[i] for i in steps[1:]], *[far[i] for i in steps[1:]]),
        (
            shape(BF16, total, half_width),
            shape(BF16, total + count, half_width),
            shape(BF16, total + count, half_width),
            shape(BF16, reps * share, total),
        ),
        (pltpu.VMEM((total - 2 * nodes, width), BF16),),
    )

    acc = shape(F32, total + count, half_width)
    listed = lookups * GROUP_VERTICES + count
    grid = (listed, 2 * GROUP_VERTICES)
    probs = shape(BF16, nodes // GROUP_VERTICES * (half_width // PAIR), *grid)
    scratch = tuple(pltpu.VMEM((2,) + grid, kind) for kind in (F32, F32, BF16, BF16))
    dqs = {}
    dk = dv = kept = None
    for group in [[0] + steps[:1]] + [[step] for step in steps[1:-1]]:
        first = 0 in group
        got = call(
            functools.partial(attend_kernel, group, total, lookups, first), "attend_%d" % group[-1], total,
            (fill,), (q, k, v, *[douts[i] for i in group]) + (() if first else (dk, dv)),
            (acc, acc) + ((probs,) if first else ()) + (flat,) * len(group), scratch,
        )
        dk, dv = got[:2]
        kept = got[2] if first else kept
        dqs.update(zip(group, got[-len(group) :]))
    last = steps[-1]
    mine, other, grads = [], [], []
    for column in range(0, half_width, PAIR):
        final = column + PAIR == half_width
        got = call(
            functools.partial(finish_kernel, last, shards, total, lookups, column, final),
            "finish_%d" % column, total, (fill,),
            (q, douts[last], k, v, dk, dv, left, put)
            + tuple(dqs[i] for i in sorted(dqs)) + ((weights, *grads) if final else ()),
            (
                shape(F32, 3, share, PAIR),
                shape(F32, 3, (reps - 1) * share, PAIR),
                shape(F32, nodes, width) if final else shape(BF16, nodes, 3 * PAIR),
            ),
            (
                pltpu.VMEM((total + count, PAIR), F32),
                pltpu.VMEM((total + count, PAIR), F32),
                pltpu.VMEM((nodes, PAIR), BF16),
                pltpu.VMEM((total, 3 * PAIR), BF16),
            ) + scratch,
        )
        mine.append(got[0])
        other.append(got[1])
        grads.append(got[2])
    node_part = grads.pop()
    back = [swap(block, "rep") for block in other] if reps == 2 else [block for block in other]
    later, _ = lax.optimization_barrier((kept, (node_part, back[:-1])))
    mixed = call(
        functools.partial(mix_kernel, total, lookups), "mix", total, (fill,), (dout, v, later), (flat,), micros=40,
    )[0]

    grad_x = call(
        features_kernel, "features", total, (), (features, node_part, swap(node_part, "tp")),
        (shape(BF16, nodes, width),), micros=5,
    )[0]
    if reps == 2:
        ready, _ = lax.optimization_barrier((mine[0], grad_x))
        grad_w = call(
            join_kernel, "join", total, (), (ready, *mine[1:], *back), (shape(F32, 3, share, half_width),),
        )[0]
    else:
        whole = jnp.concatenate([jnp.concatenate(mine, 2), jnp.concatenate(other, 2)], 1)
        whole = jnp.roll(whole, lax.axis_index("rep") * share, 1)
        grad_w = lax.psum_scatter(whole, "rep", scatter_dimension=1, tiled=True)
    return mixed[None], grad_x[None], jnp.transpose(grad_w, (1, 0, 2))


def solution(mesh):
    placed = (
        P(("groups", "rep"), "seq", None),
        P(("groups", "rep"), "seq", "tp"),
        P(None, None, "tp"),
        P(("groups", "rep"), "seq", None),
        P(("groups", "rep"), None),
        P(("groups", "rep"), None),
    )
    return jax.shard_map(
        local,
        mesh=mesh,
        in_specs=placed,
        out_specs=(
            P(("groups", "rep"), "seq", "tp"),
            P(("groups", "rep"), "seq", None),
            P(("groups", "seq", "rep"), None, "tp"),
        ),
        check_vma=False,
    )
```

time: 73.3 us -> 62.6 us (0.85)
  waiting for transfers between devices: 20.4 us -> 12.7 us
  Pallas kernels: 32.3 us -> 28.6 us
  local copies, waits for them, and re-layouts: 2.75 us -> 4.24 us
  other arithmetic: 1.66 us -> 0.82 us
    ppermute x7, waiting for transfers between devices: 7.21 us -> 3 us  [swap(): return lax.ppermute(value, axis, [(0, 1), (1, 0)])]
    pallas_call x12, Pallas kernels: 32.3 us -> 28.6 us  [call(): pl.pallas_call(kernel, out_shape=outs, in_specs=[SMEM] * len(scalars) + [...]
    ppermute x6, waiting for transfers between devices: 13.2 us -> 9.71 us  [trade(): return lax.ppermute(value, 'seq', [(j, j ^ step) for j in range(shards)])]
    broadcast_in_dim x1 -> x0, other arithmetic: 0.96 us -> none  [local(): grad_x.astype(BF16)[None]]
    dynamic_slice x0 -> x1, local copies, waits for them, and re-layouts: none -> 0.94 us  [local(): lax.dynamic_slice_in_dim(features, lax.axis_index('tp') * (nodes // 2), n...]
  transfers between devices with their start and end apart: 13 -> 13, of which waited for: 6 -> 6; matrix products, arithmetic and copies ran while one was open for 1% -> 3% of each run, Pallas kernels for 30% -> 40%
where the time goes in v3:
time: 62.6 us; the launch traced here: 62.4 us
  Pallas kernels  28.6 us (46%)
  starting transfers between devices  15.2 us (24%)
  waiting for transfers between devices  12.7 us (20%)
  local copies, waits for them, and re-layouts  4.24 us (7%)
  other arithmetic  0.82 us (1%)
  between operations  0.8 us (1%)
    pallas_call x12, Pallas kernels, call(): pl.pallas_call(kernel, out_shape=outs, in_specs=[SMEM] * len(scalars) + [...  28.6 us
    ppermute x6, starting transfers between devices, trade(): return lax.ppermute(value, 'seq', [(j, j ^ step) for j in range(shards)])  10.9 us
    ppermute x6, waiting for transfers between devices, trade(): return lax.ppermute(value, 'seq', [(j, j ^ step) for j in range(shards)])  9.71 us
    ppermute x7, starting transfers between devices, swap(): return lax.ppermute(value, axis, [(0, 1), (1, 0)])  4.3 us
    ppermute x7, waiting for transfers between devices, swap(): return lax.ppermute(value, axis, [(0, 1), (1, 0)])  3 us
    unnamed x14, local copies, waits for them, and re-layouts  2.49 us
  transfers between devices with their start and end apart: 13, of which 6 were waited for; matrix products, arithmetic and copies ran while one was open for 3% of the time, Pallas kernels for 40%

profile of v3, /device:TPU:0, one launch (start us, length us, event | category | flops | bytes accessed | tf_op | source)
XLA Modules:
  0.0 62.4 jit_solution(6336353770565572859)
XLA Ops:
  0.6 0.9 %dynamic-slice_bitcast_fusion = bf16[128,768]{1,0:T(8,128)(2,1)S(1)} fusion(bf16[1,256,768]{2,1,0:T(8,128)(2,1)} %param.6, s32[]{:T(128)S(6)} %select_n.35), kind=kLoop, calls=%fused_computation.5 | loop fusion | bytes 393220 | tf_op jit(solution)/shard_map/dynamic_slice | solution.py:416
  1.6 3.1 %collective-permute-start = (bf16[128,768]{1,0:T(8,128)(2,1)S(1)}, bf16[128,768]{1,0:T(8,128)(2,1)S(1)}, u32[]{:S(2)}, u32[]{:S(2)}) collective-permute-start(bf16[128,768]{1,0:T(8,128)(2,1)S(1)} %dynamic-slice_bitcast_fusion), channel_id=1, source_target_pairs={{0,4},{4,0},{8,12},{12,8},{1,5},{5,1},{9,13},{13,9},{2,6},{6,2},{1... | collective-permute-start | bytes 589832 | tf_op jit(solution)/shard_map/ppermute | solution.py:411
  4.7 2.5 %collective-permute-start.3 = (bf16[128,768]{1,0:T(8,128)(2,1)S(1)}, bf16[128,768]{1,0:T(8,128)(2,1)S(1)}, u32[]{:S(2)}, u32[]{:S(2)}) collective-permute-start(bf16[128,768]{1,0:T(8,128)(2,1)S(1)} %dynamic-slice_bitcast_fusion), channel_id=1, source_target_pairs={{0,12},{4,8},{8,4},{12,0},{1,13},{5,9},{9,5},{13,1},{2,14},{6,10},... | collective-permute-start | bytes 589832 | tf_op jit(solution)/shard_map/ppermute | solution.py:411
  8.9 1.1 %collective-permute-done.near_ref = bf16[128,768]{1,0:T(8,128)(2,1)S(1)} collective-permute-done((bf16[128,768]{1,0:T(8,128)(2,1)S(1)}, bf16[128,768]{1,0:T(8,128)(2,1)S(1)}, u32[]{:S(2)}, u32[]{:S(2)}) %collective-permute-start) | collective-permute-done | bytes 196640 | tf_op jit(solution)/shard_map/ppermute | solution.py:411
  10.0 1.5 %copy-done = bf16[768,3,384]{2,0,1:T(8,128)(2,1)S(1)} copy-done((bf16[768,3,384]{2,0,1:T(8,128)(2,1)S(1)}, bf16[768,3,384]{2,0,1:T(8,128)(2,1)}, u32[]{:S(2)}) %copy-start) | copy-done | bytes 1769496
  11.5 1.0 %copy-done.2 = bf16[1,256,768]{2,1,0:T(8,128)(2,1)S(1)} copy-done((bf16[1,256,768]{2,1,0:T(8,128)(2,1)S(1)}, bf16[1,256,768]{2,1,0:T(8,128)(2,1)}, u32[]{:S(2)}) %copy-start.2) | copy-done | bytes 393240
  12.5 1.1 %project_first.1 = (bf16[256,384]{1,0:T(8,128)(2,1)S(1)}, bf16[256,384]{1,0:T(8,128)(2,1)S(1)}, bf16[256,384]{1,0:T(8,128)(2,1)S(1)}, bf16[192,256]{1,0:T(8,128)...) custom-call(s32[1,256]{1,0:T(1,128)S(1)} %fusion.7.row_ref, s32[256,1]{1,0:T(8,128)S(1)} %fusion.2.col_ref, ...), custom_call_target="tpu_custom_call" | custom-call | flops 2000000000 | tf_op jit(solution)/shard_map/project_first/pallas_call | solution.py:38
  14.2 2.5 %collective-permute-start.6 = (bf16[272,384]{1,0:T(8,128)(2,1)S(1)}, bf16[272,384]{1,0:T(8,128)(2,1)S(1)}, u32[]{:S(2)}, u32[]{:S(2)}) collective-permute-start(bf16[272,384]{1,0:T(8,128)(2,1)S(1)} %prepare.1.refs_0_.dout_ref), channel_id=1, source_target_pairs={{0,4},{4,0},{8,12},{12,8},{1,5},{5,1},{9,13},{13,9},{2,6},{6,2},{1... | collective-permute-start | bytes 626696 | tf_op jit(solution)/shard_map/ppermute | solution.py:411
  16.8 1.0 %project_next.1 = (bf16[256,384]{1,0:T(8,128)(2,1)S(1)}, bf16[256,384]{1,0:T(8,128)(2,1)S(1)}, bf16[256,384]{1,0:T(8,128)(2,1)S(1)}, bf16[192,256]{1,0:T(8,128)(2,1)S(1)}) custom-call(bf16[3,768,384]{2,1,0:T(8,128)(2,1)S(1)} %bitcast.12, bf16[128,768]{1,0:T(8,128)(2,1)S(1)} %collective-permute-done.near_ref, bf16[128,768]{1,0:T(8,128)(2,1)S(1)} %collective-permute-done.1.far_ref), custom_call_target="tpu_custom_call" | custom-call | flops 2000000000 | tf_op jit(solution)/shard_map/project_next/pallas_call | solution.py:38
  17.8 6.9 %collective-permute-done.2.refs_8_ = bf16[128,768]{1,0:T(8,128)(2,1)S(1)} collective-permute-done((bf16[128,768]{1,0:T(8,128)(2,1)S(1)}, bf16[128,768]{1,0:T(8,128)(2,1)S(1)}, u32[]{:S(2)}, u32[]{:S(2)}) %collective-permute-start.2) | collective-permute-done | bytes 196640 | tf_op jit(solution)/shard_map/ppermute | solution.py:411
  24.6 2.6 %collective-permute-start.7 = (bf16[272,384]{1,0:T(8,128)(2,1)S(1)}, bf16[272,384]{1,0:T(8,128)(2,1)S(1)}, u32[]{:S(2)}, u32[]{:S(2)}) collective-permute-start(bf16[272,384]{1,0:T(8,128)(2,1)S(1)} %prepare.1.refs_0_.dout_ref), channel_id=1, source_target_pairs={{0,12},{4,8},{8,4},{12,0},{1,13},{5,9},{9,5},{13,1},{2,14},{6,10},... | collective-permute-start | bytes 626696 | tf_op jit(solution)/shard_map/ppermute | solution.py:411
  27.8 0.9 %collective-permute-done.5.refs_11_ = bf16[128,768]{1,0:T(8,128)(2,1)S(1)} collective-permute-done((bf16[128,768]{1,0:T(8,128)(2,1)S(1)}, bf16[128,768]{1,0:T(8,128)(2,1)S(1)}, u32[]{:S(2)}, u32[]{:S(2)}) %collective-permute-start.5) | collective-permute-done | bytes 196640 | tf_op jit(solution)/shard_map/ppermute | solution.py:414
  29.0 2.4 %project.1 = (bf16[1024,384]{1,0:T(8,128)(2,1)S(1)}, bf16[1280,384]{1,0:T(8,128)(2,1)S(1)}, bf16[1280,384]{1,0:T(8,128)(2,1)S(1)}, bf16[192,1024]{1,0:T(8,128)(2,1)S(1)}) custom-call(bf16[3,768,384]{2,1,0:T(8,128)(2,1)S(1)} %bitcast.13, bf16[256,1024]{1,0:T(8,128)(2,1)S(1)} %get-tuple-element.41.pick_ref, bf16[256,384]{1,0:T(8,128)(2,1)S(1)} %get-tuple-element.42.refs_0_, ...), custom_call_target="tpu_custom_call" | custom-call | tf_op jit(solution)/shard_map/project/pallas_call | solution.py:38
  31.4 7.1 %attend_1.1 = (f32[1280,384]{1,0:T(8,128)S(1)}, f32[1280,384]{1,0:T(8,128)S(1)}, bf16[6,512,256]{2,1,0:T(8,128)(2,1)S(1)}, bf16[256,384]{1,0:T(8,128)(2,1)S(1)}, bf16[256,384]{1,0:T(8,128)(2,1)S(1)}) custom-call(s32[8]{0:T(128)S(1)} %bitcast.17, bf16[1024,384]{1,0:T(8,128)(2,1)S(1)} %get-tuple-element.53.q_ref, ...), custom_call_target="tpu_custom_call" | custom-call | tf_op jit(solution)/shard_map/attend_1/pallas_call | solution.py:38
  38.6 1.8 %collective-permute-done.8.refs_0_ = bf16[272,384]{1,0:T(8,128)(2,1)S(1)} collective-permute-done((bf16[272,384]{1,0:T(8,128)(2,1)S(1)}, bf16[272,384]{1,0:T(8,128)(2,1)S(1)}, u32[]{:S(2)}, u32[]{:S(2)}) %collective-permute-start.8) | collective-permute-done | bytes 208928 | tf_op jit(solution)/shard_map/ppermute | solution.py:411
  40.3 4.2 %attend_2.1 = (f32[1280,384]{1,0:T(8,128)S(1)}, f32[1280,384]{1,0:T(8,128)S(1)}, bf16[256,384]{1,0:T(8,128)(2,1)S(1)}) custom-call(s32[8]{0:T(128)S(1)} %bitcast.18, bf16[1024,384]{1,0:T(8,128)(2,1)S(1)} %get-tuple-element.53.q_ref, bf16[1280,384]{1,0:T(8,128)(2,1)S(1)} %get-tuple-element.54.k_ref, bf16[1280,384]{1,0:T(8,128)(2,1)S(1)} %get-tuple-element.52.v_ref, ...), custom_call_target="tpu_custom_call" | custom-call | tf_op jit(solution)/shard_map/attend_2/pallas_call | solution.py:38
  44.6 2.6 %finish_128.1 = (f32[3,96,128]{2,1,0:T(8,128)S(1)}, f32[3,96,128]{2,1,0:T(8,128)S(1)}, bf16[256,384]{1,0:T(8,128)(2,1)S(1)}) custom-call(s32[8]{0:T(128)S(1)} %bitcast.19, bf16[1024,384]{1,0:T(8,128)(2,1)S(1)} %get-tuple-element.53.q_ref, bf16[272,384]{1,0:T(8,128)(2,1)S(1)} %collective-permute-done.7.dout_ref, ...), custom_call_target="tpu_custom_call" | custom-call | tf_op jit(solution)/shard_map/finish_128/pallas_call | solution.py:38
  47.2 1.6 %collective-permute-start.10 = (f32[3,96,128]{2,1,0:T(8,128)S(1)}, f32[3,96,128]{2,1,0:T(8,128)S(1)}, u32[]{:S(2)}, u32[]{:S(2)}) collective-permute-start(f32[3,96,128]{2,1,0:T(8,128)S(1)} %get-tuple-element.70), channel_id=1, source_target_pairs={{0,2},{2,0},{1,3},{3,1},{4,6},{6,4},{5,7},{7,5},{8,10},{10,8},{9,1... | collective-permute-start | bytes 442376 | tf_op jit(solution)/shard_map/ppermute | solution.py:414
  48.7 2.6 %finish_0.1 = (f32[3,96,128]{2,1,0:T(8,128)S(1)}, f32[3,96,128]{2,1,0:T(8,128)S(1)}, bf16[256,384]{1,0:T(8,128)(2,1)S(1)}) custom-call(s32[8]{0:T(128)S(1)} %bitcast.20, bf16[1024,384]{1,0:T(8,128)(2,1)S(1)} %get-tuple-element.53.q_ref, bf16[272,384]{1,0:T(8,128)(2,1)S(1)} %collective-permute-done.7.dout_ref, bf16[1280,384]{1,0:T(8,128)(2,1)S(1)} %get-tuple-element.54.k_ref, ...), custom_call_target="tpu_custom_call" | custom-call | tf_op jit(solution)/shard_map/finish_0/pallas_call | solution.py:38
  51.9 3.3 %finish_256.1 = (f32[3,96,128]{2,1,0:T(8,128)S(1)}, f32[3,96,128]{2,1,0:T(8,128)S(1)}, f32[256,768]{1,0:T(8,128)S(1)}) custom-call(s32[8]{0:T(128)S(1)} %bitcast.21, bf16[1024,384]{1,0:T(8,128)(2,1)S(1)} %get-tuple-element.53.q_ref, bf16[272,384]{1,0:T(8,128)(2,1)S(1)} %collective-permute-done.7.dout_ref, bf16[1280,384]{1,0:T(8,128)(2,1)S(1)} %get-tuple-element.54.k_ref, ...), custom_call_target="tpu_custom_call" | custom-call | tf_op jit(solution)/shard_map/finish_256/pallas_call | solution.py:38
  55.3 1.6 %collective-permute-start.12 = (f32[3,96,128]{2,1,0:T(8,128)S(1)}, f32[3,96,128]{2,1,0:T(8,128)S(1)}, u32[]{:S(2)}, u32[]{:S(2)}) collective-permute-start(f32[3,96,128]{2,1,0:T(8,128)S(1)} %get-tuple-element.76), channel_id=1, source_target_pairs={{0,2},{2,0},{1,3},{3,1},{4,6},{6,4},{5,7},{7,5},{8,10},{10,8},{9,1... | collective-permute-start | bytes 442376 | tf_op jit(solution)/shard_map/ppermute | solution.py:414
  56.9 1.8 %mix.1 = bf16[256,384]{1,0:T(8,128)(2,1)} custom-call(s32[8]{0:T(128)S(1)} %bitcast.22, bf16[272,384]{1,0:T(8,128)(2,1)S(1)} %prepare.1.refs_0_.dout_ref, bf16[1280,384]{1,0:T(8,128)(2,1)S(1)} %get-tuple-element.52.v_ref, bf16[6,512,256]{2,1,0:T(8,128)(2,1)S(1)} %get-tuple-element.71.probs_ref), custom_call_target="tpu_custom_call" | custom-call | flops 40000000000 | tf_op jit(solution)/shard_map/mix/pallas_call | solution.py:38
  58.7 1.1 %features.1 = bf16[256,768]{1,0:T(8,128)(2,1)} custom-call(bf16[256,768]{1,0:T(8,128)(2,1)S(1)} %bitcast.16, f32[256,768]{1,0:T(8,128)S(1)} %get-tuple-element.68.mine_ref, f32[256,768]{1,0:T(8,128)S(1)} %collective-permute-done.11.other_ref), custom_call_target="tpu_custom_call" | custom-call | flops 5000000000 | tf_op jit(solution)/shard_map/features/pallas_call | solution.py:38
  59.8 1.8 %collective-permute-done.12.refs_5_ = f32[3,96,128]{2,1,0:T(8,128)S(1)} collective-permute-done((f32[3,96,128]{2,1,0:T(8,128)S(1)}, f32[3,96,128]{2,1,0:T(8,128)S(1)}, u32[]{:S(2)}, u32[]{:S(2)}) %collective-permute-start.12) | collective-permute-done | bytes 147488 | tf_op jit(solution)/shard_map/ppermute | solution.py:414
  (32 shorter events, 4.6 us)
Async XLA Ops:
  1.6 8.4 %collective-permute-start = (bf16[128,768]{1,0:T(8,128)(2,1)S(1)}, bf16[128,768]{1,0:T(8,128)(2,1)S(1)}, u32[]{:S(2)}, u32[]{:S(2)}) collective-permute-start(bf16[128,768]{1,0:T(8,128)(2,1)S(1)} %dynamic-slice_bitcast_fusion), channel_id=1, source_target_pairs={{0,4},{4,0},{8,12},{12,8},{1,5},{5,1},{9,13},{13,9},{2,6},{6,2},{1... | collective-permute-start | bytes 589832 | tf_op jit(solution)/shard_map/ppermute | solution.py:411
  4.7 13.1 %collective-permute-start.3 = (bf16[128,768]{1,0:T(8,128)(2,1)S(1)}, bf16[128,768]{1,0:T(8,128)(2,1)S(1)}, u32[]{:S(2)}, u32[]{:S(2)}) collective-permute-start(bf16[128,768]{1,0:T(8,128)(2,1)S(1)} %dynamic-slice_bitcast_fusion), channel_id=1, source_target_pairs={{0,12},{4,8},{8,4},{12,0},{1,13},{5,9},{9,5},{13,1},{2,14},{6,10},... | collective-permute-start | bytes 589832 | tf_op jit(solution)/shard_map/ppermute | solution.py:411
  7.1 17.5 %collective-permute-start.2 = (bf16[128,768]{1,0:T(8,128)(2,1)S(1)}, bf16[128,768]{1,0:T(8,128)(2,1)S(1)}, u32[]{:S(2)}, u32[]{:S(2)}) collective-permute-start(bf16[128,768]{1,0:T(8,128)(2,1)S(1)} %dynamic-slice_bitcast_fusion), channel_id=1, source_target_pairs={{0,8},{4,12},{8,0},{12,4},{1,9},{5,13},{9,1},{13,5},{2,10},{6,14},... | collective-permute-start | bytes 589832 | tf_op jit(solution)/shard_map/ppermute | solution.py:411
  10.0 6.8 %collective-permute-start.1 = (bf16[128,768]{1,0:T(8,128)(2,1)S(1)}, bf16[128,768]{1,0:T(8,128)(2,1)S(1)}, u32[]{:S(2)}, u32[]{:S(2)}) collective-permute-start(bf16[128,768]{1,0:T(8,128)(2,1)S(1)} %collective-permute-done.near_ref), channel_id=1, source_target_pairs={{0,1},{1,0},{2,3},{3,2},{4,5},{5,4},{6,7},{7,6},{8,9},{9,8},{10,11... | collective-permute-start | bytes 589832 | tf_op jit(solution)/shard_map/ppermute | solution.py:414
  10.0 1.5 %copy-start = (bf16[768,3,384]{2,0,1:T(8,128)(2,1)S(1)}, bf16[768,3,384]{2,0,1:T(8,128)(2,1)}, u32[]{:S(2)}) copy-start(bf16[768,3,384]{2,0,1:T(8,128)(2,1)} %param.8) | copy-start | bytes 5308420
  11.5 1.0 %copy-start.2 = (bf16[1,256,768]{2,1,0:T(8,128)(2,1)S(1)}, bf16[1,256,768]{2,1,0:T(8,128)(2,1)}, u32[]{:S(2)}) copy-start(bf16[1,256,768]{2,1,0:T(8,128)(2,1)} %param.6) | copy-start | bytes 1179652
  12.5 1.2 %copy-start.5 = (bf16[1,256,384]{2,1,0:T(8,128)(2,1)S(1)}, bf16[1,256,384]{2,1,0:T(8,128)(2,1)}, u32[]{:S(2)}) copy-start(bf16[1,256,384]{2,1,0:T(8,128)(2,1)} %param.7) | copy-start | bytes 589828
  12.5 1.2 %copy-start.6 = (s32[1,2,2]{2,1,0:T(2,128)S(1)}, s32[1,2,2]{2,1,0:T(2,128)}, u32[]{:S(2)}) copy-start(s32[1,2,2]{2,1,0:T(2,128)} %param.9) | copy-start | bytes 52
  13.6 3.2 %copy-start.1 = (bf16[768,3,384]{2,0,1:T(8,128)(2,1)S(1)}, bf16[768,3,384]{2,0,1:T(8,128)(2,1)}, u32[]{:S(2)}) copy-start(bf16[768,3,384]{2,0,1:T(8,128)(2,1)} %param.8) | copy-start | bytes 5308420
  14.2 17.2 %collective-permute-start.6 = (bf16[272,384]{1,0:T(8,128)(2,1)S(1)}, bf16[272,384]{1,0:T(8,128)(2,1)S(1)}, u32[]{:S(2)}, u32[]{:S(2)}) collective-permute-start(bf16[272,384]{1,0:T(8,128)(2,1)S(1)} %prepare.1.refs_0_.dout_ref), channel_id=1, source_target_pairs={{0,4},{4,0},{8,12},{12,8},{1,5},{5,1},{9,13},{13,9},{2,6},{6,2},{1... | collective-permute-start | bytes 626696 | tf_op jit(solution)/shard_map/ppermute | solution.py:411
  24.6 15.7 %collective-permute-start.8 = (bf16[272,384]{1,0:T(8,128)(2,1)S(1)}, bf16[272,384]{1,0:T(8,128)(2,1)S(1)}, u32[]{:S(2)}, u32[]{:S(2)}) collective-permute-start(bf16[272,384]{1,0:T(8,128)(2,1)S(1)} %prepare.1.refs_0_.dout_ref), channel_id=1, source_target_pairs={{0,8},{4,12},{8,0},{12,4},{1,9},{5,13},{9,1},{13,5},{2,10},{6,14},... | collective-permute-start | bytes 626696 | tf_op jit(solution)/shard_map/ppermute | solution.py:411
  24.6 19.9 %collective-permute-start.7 = (bf16[272,384]{1,0:T(8,128)(2,1)S(1)}, bf16[272,384]{1,0:T(8,128)(2,1)S(1)}, u32[]{:S(2)}, u32[]{:S(2)}) collective-permute-start(bf16[272,384]{1,0:T(8,128)(2,1)S(1)} %prepare.1.refs_0_.dout_ref), channel_id=1, source_target_pairs={{0,12},{4,8},{8,4},{12,0},{1,13},{5,9},{9,5},{13,1},{2,14},{6,10},... | collective-permute-start | bytes 626696 | tf_op jit(solution)/shard_map/ppermute | solution.py:411
  27.3 1.4 %collective-permute-start.5 = (bf16[128,768]{1,0:T(8,128)(2,1)S(1)}, bf16[128,768]{1,0:T(8,128)(2,1)S(1)}, u32[]{:S(2)}, u32[]{:S(2)}) collective-permute-start(bf16[128,768]{1,0:T(8,128)(2,1)S(1)} %collective-permute-done.3.refs_9_), channel_id=1, source_target_pairs={{0,1},{1,0},{2,3},{3,2},{4,5},{5,4},{6,7},{7,6},{8,9},{9,8},{10,11... | collective-permute-start | bytes 589832 | tf_op jit(solution)/shard_map/ppermute | solution.py:414
  27.3 1.7 %collective-permute-start.4 = (bf16[128,768]{1,0:T(8,128)(2,1)S(1)}, bf16[128,768]{1,0:T(8,128)(2,1)S(1)}, u32[]{:S(2)}, u32[]{:S(2)}) collective-permute-start(bf16[128,768]{1,0:T(8,128)(2,1)S(1)} %collective-permute-done.2.refs_8_), channel_id=1, source_target_pairs={{0,1},{1,0},{2,3},{3,2},{4,5},{5,4},{6,7},{7,6},{8,9},{9,8},{10,11... | collective-permute-start | bytes 589832 | tf_op jit(solution)/shard_map/ppermute | solution.py:414
  29.0 2.4 %copy-start.4 = (s32[1,8]{1,0:T(1,128)S(1)}, s32[1,8]{1,0:T(1,128)}, u32[]{:S(2)}) copy-start(s32[1,8]{1,0:T(1,128)} %param.10) | copy-start | bytes 100
  47.2 9.7 %collective-permute-start.10 = (f32[3,96,128]{2,1,0:T(8,128)S(1)}, f32[3,96,128]{2,1,0:T(8,128)S(1)}, u32[]{:S(2)}, u32[]{:S(2)}) collective-permute-start(f32[3,96,128]{2,1,0:T(8,128)S(1)} %get-tuple-element.70), channel_id=1, source_target_pairs={{0,2},{2,0},{1,3},{3,1},{4,6},{6,4},{5,7},{7,5},{8,10},{10,8},{9,1... | collective-permute-start | bytes 442376 | tf_op jit(solution)/shard_map/ppermute | solution.py:414
  51.3 5.5 %collective-permute-start.9 = (f32[3,96,128]{2,1,0:T(8,128)S(1)}, f32[3,96,128]{2,1,0:T(8,128)S(1)}, u32[]{:S(2)}, u32[]{:S(2)}) collective-permute-start(f32[3,96,128]{2,1,0:T(8,128)S(1)} %get-tuple-element.69), channel_id=1, source_target_pairs={{0,2},{2,0},{1,3},{3,1},{4,6},{6,4},{5,7},{7,5},{8,10},{10,8},{9,1... | collective-permute-start | bytes 442376 | tf_op jit(solution)/shard_map/ppermute | solution.py:414
  55.2 3.5 %collective-permute-start.11 = (f32[256,768]{1,0:T(8,128)S(1)}, f32[256,768]{1,0:T(8,128)S(1)}, u32[]{:S(2)}, u32[]{:S(2)}) collective-permute-start(f32[256,768]{1,0:T(8,128)S(1)} %get-tuple-element.68.mine_ref), channel_id=1, source_target_pairs={{0,1},{1,0},{2,3},{3,2},{4,5},{5,4},{6,7},{7,6},{8,9},{9,8},{10,11... | collective-permute-start | bytes 2359304 | tf_op jit(solution)/shard_map/ppermute | solution.py:414
  55.3 6.3 %collective-permute-start.12 = (f32[3,96,128]{2,1,0:T(8,128)S(1)}, f32[3,96,128]{2,1,0:T(8,128)S(1)}, u32[]{:S(2)}, u32[]{:S(2)}) collective-permute-start(f32[3,96,128]{2,1,0:T(8,128)S(1)} %get-tuple-element.76), channel_id=1, source_target_pairs={{0,2},{2,0},{1,3},{3,1},{4,6},{6,4},{5,7},{7,5},{8,10},{10,8},{9,1... | collective-permute-start | bytes 442376 | tf_op jit(solution)/shard_map/ppermute | solution.py:414
  56.9 1.9 %copy-start.3 = (bf16[1,256,768]{2,1,0:T(8,128)(2,1)S(1)}, bf16[1,256,768]{2,1,0:T(8,128)(2,1)}, u32[]{:S(2)}) copy-start(bf16[1,256,768]{2,1,0:T(8,128)(2,1)} %param.6) | copy-start | bytes 1179652

commit v4 on v3

--- a/solution.py
+++ b/solution.py
@@ -414,12 +414,11 @@
         return lax.ppermute(value, axis, [(0, 1), (1, 0)])
 
     half = lax.dynamic_slice_in_dim(features, lax.axis_index("tp") * (nodes // 2), nodes // 2)
-    steps = list(range(1, shards))
+    steps = [1] + list(range(shards - 1, 1, -1))
     near = {step: trade(half, step) for step in steps}
     far = {1: swap(near[1], "tp")}
-    ready, _ = lax.optimization_barrier((cotangent, near[1]))
     dout = call(
-        prepare_kernel, "prepare", total, (pairs,), (ready,), (shape(BF16, nodes + TAIL, half_width),),
+        prepare_kernel, "prepare", total, (pairs,), (cotangent,), (shape(BF16, nodes + TAIL, half_width),),
         micros=1,
     )[0]
     douts = {0: dout, 1: trade(dout, 1)}
@@ -438,12 +437,11 @@
     for step in steps[1:]:
         near[step], _ = lax.optimization_barrier((near[step], (first[0], second[0])))
         far[step] = swap(near[step], "tp")
-    ready, _ = lax.optimization_barrier((dout, [near[step] for step in steps]))
-    for step in steps[1:]:
+        ready, _ = lax.optimization_barrier((dout, near[step]))
         douts[step] = trade(ready, step)
     q, k, v, left = call(
         functools.partial(project_kernel, shards), "project", total, (),
-        (weights, pick, *first, *second, *[near[i] for i in steps[1:]], *[far[i] for i in steps[1:]]),
+        (weights, pick, *first, *second, *[near[i] for i in range(2, shards)], *[far[i] for i in range(2, shards)]),
         (
             shape(BF16, total, half_width),
             shape(BF16, total + count, half_width),

time: 62.6 us -> 61.5 us (0.982)
  local copies, waits for them, and re-layouts: 4.24 us -> 2.7 us
  waiting for transfers between devices: 12.7 us -> 14 us
  other arithmetic: 0.82 us -> 0.15 us
    ppermute x6, waiting for transfers between devices: 9.71 us -> 10.7 us  [trade(): return lax.ppermute(value, 'seq', [(j, j ^ step) for j in range(shards)])]
    unnamed x14 -> x12, local copies, waits for them, and re-layouts: 2.49 us -> 1.62 us
    add x2, other arithmetic: 0.82 us -> 0.15 us  [local(): ids = (global_ids // nodes ^ me) * nodes + global_ids % nodes]
    squeeze x1, local copies, waits for them, and re-layouts: 0.8 us -> 0.13 us  [local(): global_ids = global_nodes[0]]
  transfers between devices with their start and end apart: 13 -> 13, of which waited for: 6 -> 7; matrix products, arithmetic and copies ran while one was open for 3% -> 0% of each run, Pallas kernels for 40% -> 41%
where the time goes in v4:
time: 61.5 us; the launch traced here: 61.4 us
  Pallas kernels  28.6 us (47%)
  starting transfers between devices  15.1 us (25%)
  waiting for transfers between devices  14 us (23%)
  local copies, waits for them, and re-layouts  2.7 us (4%)
  between operations  0.81 us (1%)
    pallas_call x12, Pallas kernels, call(): pl.pallas_call(kernel, out_shape=outs, in_specs=[SMEM] * len(scalars) + [...  28.6 us
    ppermute x6, starting transfers between devices, trade(): return lax.ppermute(value, 'seq', [(j, j ^ step) for j in range(shards)])  10.8 us
    ppermute x6, waiting for transfers between devices, trade(): return lax.ppermute(value, 'seq', [(j, j ^ step) for j in range(shards)])  10.7 us
    ppermute x7, starting transfers between devices, swap(): return lax.ppermute(value, axis, [(0, 1), (1, 0)])  4.36 us
    ppermute x7, waiting for transfers between devices, swap(): return lax.ppermute(value, axis, [(0, 1), (1, 0)])  3.28 us
    unnamed x12, local copies, waits for them, and re-layouts  1.62 us
  transfers between devices with their start and end apart: 13, of which 7 were waited for; matrix products, arithmetic and copies ran while one was open for 0% of the time, Pallas kernels for 41%

profile of v4, /device:TPU:0, one launch (start us, length us, event | category | flops | bytes accessed | tf_op | source)
XLA Modules:
  0.0 61.4 jit_solution(1589073315177858641)
XLA Ops:
  0.6 0.9 %dynamic-slice_bitcast_fusion = bf16[128,768]{1,0:T(8,128)(2,1)S(1)} fusion(bf16[1,256,768]{2,1,0:T(8,128)(2,1)} %param.6, s32[]{:T(128)S(6)} %select_n.39), kind=kLoop, calls=%fused_computation | loop fusion | bytes 393220 | tf_op jit(solution)/shard_map/dynamic_slice | solution.py:416
  1.6 3.1 %collective-permute-start = (bf16[128,768]{1,0:T(8,128)(2,1)S(1)}, bf16[128,768]{1,0:T(8,128)(2,1)S(1)}, u32[]{:S(2)}, u32[]{:S(2)}) collective-permute-start(bf16[128,768]{1,0:T(8,128)(2,1)S(1)} %dynamic-slice_bitcast_fusion), channel_id=1, source_target_pairs={{0,4},{4,0},{8,12},{12,8},{1,5},{5,1},{9,13},{13,9},{2,6},{6,2},{1... | collective-permute-start | bytes 589832 | tf_op jit(solution)/shard_map/ppermute | solution.py:411
  4.7 2.5 %collective-permute-start.3 = (bf16[128,768]{1,0:T(8,128)(2,1)S(1)}, bf16[128,768]{1,0:T(8,128)(2,1)S(1)}, u32[]{:S(2)}, u32[]{:S(2)}) collective-permute-start(bf16[128,768]{1,0:T(8,128)(2,1)S(1)} %dynamic-slice_bitcast_fusion), channel_id=1, source_target_pairs={{0,12},{4,8},{8,4},{12,0},{1,13},{5,9},{9,5},{13,1},{2,14},{6,10},... | collective-permute-start | bytes 589832 | tf_op jit(solution)/shard_map/ppermute | solution.py:411
  7.3 0.9 %copy-done.3 = bf16[1,256,384]{2,1,0:T(8,128)(2,1)S(1)} copy-done((bf16[1,256,384]{2,1,0:T(8,128)(2,1)S(1)}, bf16[1,256,384]{2,1,0:T(8,128)(2,1)}, u32[]{:S(2)}) %copy-start.3) | copy-done | bytes 196632
  8.2 0.7 %copy-done.4 = s32[1,2,2]{2,1,0:T(2,128)S(1)} copy-done((s32[1,2,2]{2,1,0:T(2,128)S(1)}, s32[1,2,2]{2,1,0:T(2,128)}, u32[]{:S(2)}) %copy-start.4) | copy-done | bytes 40
  9.5 1.9 %collective-permute-start.6 = (bf16[272,384]{1,0:T(8,128)(2,1)S(1)}, bf16[272,384]{1,0:T(8,128)(2,1)S(1)}, u32[]{:S(2)}, u32[]{:S(2)}) collective-permute-start(bf16[272,384]{1,0:T(8,128)(2,1)S(1)} %prepare.1.refs_0_.dout_ref), channel_id=1, source_target_pairs={{0,4},{4,0},{8,12},{12,8},{1,5},{5,1},{9,13},{13,9},{2,6},{6,2},{1... | collective-permute-start | bytes 626696 | tf_op jit(solution)/shard_map/ppermute | solution.py:411
  11.7 1.1 %project_first.1 = (bf16[256,384]{1,0:T(8,128)(2,1)S(1)}, bf16[256,384]{1,0:T(8,128)(2,1)S(1)}, bf16[256,384]{1,0:T(8,128)(2,1)S(1)}, bf16[192,256]{1,0:T(8,128)...) custom-call(s32[1,256]{1,0:T(1,128)S(1)} %fusion.7.row_ref, s32[256,1]{1,0:T(8,128)S(1)} %fusion.2.col_ref, ...), custom_call_target="tpu_custom_call" | custom-call | flops 2000000000 | tf_op jit(solution)/shard_map/project_first/pallas_call | solution.py:38
  13.1 1.0 %project_next.1 = (bf16[256,384]{1,0:T(8,128)(2,1)S(1)}, bf16[256,384]{1,0:T(8,128)(2,1)S(1)}, bf16[256,384]{1,0:T(8,128)(2,1)S(1)}, bf16[192,256]{1,0:T(8,128)(2,1)S(1)}) custom-call(bf16[3,768,384]{2,1,0:T(8,128)(2,1)S(1)} %bitcast.12, bf16[128,768]{1,0:T(8,128)(2,1)S(1)} %collective-permute-done.near_ref, bf16[128,768]{1,0:T(8,128)(2,1)S(1)} %collective-permute-done.1.far_ref), custom_call_target="tpu_custom_call" | custom-call | flops 2000000000 | tf_op jit(solution)/shard_map/project_next/pallas_call | solution.py:38
  14.1 3.1 %collective-permute-done.3.refs_9_ = bf16[128,768]{1,0:T(8,128)(2,1)S(1)} collective-permute-done((bf16[128,768]{1,0:T(8,128)(2,1)S(1)}, bf16[128,768]{1,0:T(8,128)(2,1)S(1)}, u32[]{:S(2)}, u32[]{:S(2)}) %collective-permute-start.3) | collective-permute-done | bytes 196640 | tf_op jit(solution)/shard_map/ppermute | solution.py:411
  17.2 7.3 %collective-permute-done.2.refs_8_ = bf16[128,768]{1,0:T(8,128)(2,1)S(1)} collective-permute-done((bf16[128,768]{1,0:T(8,128)(2,1)S(1)}, bf16[128,768]{1,0:T(8,128)(2,1)S(1)}, u32[]{:S(2)}, u32[]{:S(2)}) %collective-permute-start.2) | collective-permute-done | bytes 196640 | tf_op jit(solution)/shard_map/ppermute | solution.py:411
  24.5 3.2 %collective-permute-start.8 = (bf16[272,384]{1,0:T(8,128)(2,1)S(1)}, bf16[272,384]{1,0:T(8,128)(2,1)S(1)}, u32[]{:S(2)}, u32[]{:S(2)}) collective-permute-start(bf16[272,384]{1,0:T(8,128)(2,1)S(1)} %prepare.1.refs_0_.dout_ref), channel_id=1, source_target_pairs={{0,12},{4,8},{8,4},{12,0},{1,13},{5,9},{9,5},{13,1},{2,14},{6,10},... | collective-permute-start | bytes 626696 | tf_op jit(solution)/shard_map/ppermute | solution.py:411
  28.3 0.9 %collective-permute-done.5.refs_11_ = bf16[128,768]{1,0:T(8,128)(2,1)S(1)} collective-permute-done((bf16[128,768]{1,0:T(8,128)(2,1)S(1)}, bf16[128,768]{1,0:T(8,128)(2,1)S(1)}, u32[]{:S(2)}, u32[]{:S(2)}) %collective-permute-start.5) | collective-permute-done | bytes 196640 | tf_op jit(solution)/shard_map/ppermute | solution.py:414
  29.5 2.4 %project.1 = (bf16[1024,384]{1,0:T(8,128)(2,1)S(1)}, bf16[1280,384]{1,0:T(8,128)(2,1)S(1)}, bf16[1280,384]{1,0:T(8,128)(2,1)S(1)}, bf16[192,1024]{1,0:T(8,128)(2,1)S(1)}) custom-call(bf16[3,768,384]{2,1,0:T(8,128)(2,1)S(1)} %bitcast.13, bf16[256,1024]{1,0:T(8,128)(2,1)S(1)} %get-tuple-element.40.pick_ref, bf16[256,384]{1,0:T(8,128)(2,1)S(1)} %get-tuple-element.41.refs_0_, ...), custom_call_target="tpu_custom_call" | custom-call | tf_op jit(solution)/shard_map/project/pallas_call | solution.py:38
  31.9 7.1 %attend_1.1 = (f32[1280,384]{1,0:T(8,128)S(1)}, f32[1280,384]{1,0:T(8,128)S(1)}, bf16[6,512,256]{2,1,0:T(8,128)(2,1)S(1)}, bf16[256,384]{1,0:T(8,128)(2,1)S(1)}, bf16[256,384]{1,0:T(8,128)(2,1)S(1)}) custom-call(s32[8]{0:T(128)S(1)} %bitcast.17, bf16[1024,384]{1,0:T(8,128)(2,1)S(1)} %get-tuple-element.52.q_ref, ...), custom_call_target="tpu_custom_call" | custom-call | tf_op jit(solution)/shard_map/attend_1/pallas_call | solution.py:38
  39.1 4.2 %attend_3.1 = (f32[1280,384]{1,0:T(8,128)S(1)}, f32[1280,384]{1,0:T(8,128)S(1)}, bf16[256,384]{1,0:T(8,128)(2,1)S(1)}) custom-call(s32[8]{0:T(128)S(1)} %bitcast.18, bf16[1024,384]{1,0:T(8,128)(2,1)S(1)} %get-tuple-element.52.q_ref, bf16[1280,384]{1,0:T(8,128)(2,1)S(1)} %get-tuple-element.53.k_ref, bf16[1280,384]{1,0:T(8,128)(2,1)S(1)} %get-tuple-element.51.v_ref, ...), custom_call_target="tpu_custom_call" | custom-call | tf_op jit(solution)/shard_map/attend_3/pallas_call | solution.py:38
  43.6 2.6 %finish_128.1 = (f32[3,96,128]{2,1,0:T(8,128)S(1)}, f32[3,96,128]{2,1,0:T(8,128)S(1)}, bf16[256,384]{1,0:T(8,128)(2,1)S(1)}) custom-call(s32[8]{0:T(128)S(1)} %bitcast.19, bf16[1024,384]{1,0:T(8,128)(2,1)S(1)} %get-tuple-element.52.q_ref, bf16[272,384]{1,0:T(8,128)(2,1)S(1)} %collective-permute-done.7.dout_ref, ...), custom_call_target="tpu_custom_call" | custom-call | tf_op jit(solution)/shard_map/finish_128/pallas_call | solution.py:38
  46.2 1.6 %collective-permute-start.10 = (f32[3,96,128]{2,1,0:T(8,128)S(1)}, f32[3,96,128]{2,1,0:T(8,128)S(1)}, u32[]{:S(2)}, u32[]{:S(2)}) collective-permute-start(f32[3,96,128]{2,1,0:T(8,128)S(1)} %get-tuple-element.70), channel_id=1, source_target_pairs={{0,2},{2,0},{1,3},{3,1},{4,6},{6,4},{5,7},{7,5},{8,10},{10,8},{9,1... | collective-permute-start | bytes 442376 | tf_op jit(solution)/shard_map/ppermute | solution.py:414
  47.7 2.6 %finish_0.1 = (f32[3,96,128]{2,1,0:T(8,128)S(1)}, f32[3,96,128]{2,1,0:T(8,128)S(1)}, bf16[256,384]{1,0:T(8,128)(2,1)S(1)}) custom-call(s32[8]{0:T(128)S(1)} %bitcast.20, bf16[1024,384]{1,0:T(8,128)(2,1)S(1)} %get-tuple-element.52.q_ref, bf16[272,384]{1,0:T(8,128)(2,1)S(1)} %collective-permute-done.7.dout_ref, bf16[1280,384]{1,0:T(8,128)(2,1)S(1)} %get-tuple-element.53.k_ref, ...), custom_call_target="tpu_custom_call" | custom-call | tf_op jit(solution)/shard_map/finish_0/pallas_call | solution.py:38
  50.9 3.3 %finish_256.1 = (f32[3,96,128]{2,1,0:T(8,128)S(1)}, f32[3,96,128]{2,1,0:T(8,128)S(1)}, f32[256,768]{1,0:T(8,128)S(1)}) custom-call(s32[8]{0:T(128)S(1)} %bitcast.21, bf16[1024,384]{1,0:T(8,128)(2,1)S(1)} %get-tuple-element.52.q_ref, bf16[272,384]{1,0:T(8,128)(2,1)S(1)} %collective-permute-done.7.dout_ref, bf16[1280,384]{1,0:T(8,128)(2,1)S(1)} %get-tuple-element.53.k_ref, ...), custom_call_target="tpu_custom_call" | custom-call | tf_op jit(solution)/shard_map/finish_256/pallas_call | solution.py:38
  54.3 1.5 %collective-permute-start.12 = (f32[3,96,128]{2,1,0:T(8,128)S(1)}, f32[3,96,128]{2,1,0:T(8,128)S(1)}, u32[]{:S(2)}, u32[]{:S(2)}) collective-permute-start(f32[3,96,128]{2,1,0:T(8,128)S(1)} %get-tuple-element.76), channel_id=1, source_target_pairs={{0,2},{2,0},{1,3},{3,1},{4,6},{6,4},{5,7},{7,5},{8,10},{10,8},{9,1... | collective-permute-start | bytes 442376 | tf_op jit(solution)/shard_map/ppermute | solution.py:414
  55.8 1.8 %mix.1 = bf16[256,384]{1,0:T(8,128)(2,1)} custom-call(s32[8]{0:T(128)S(1)} %bitcast.22, bf16[272,384]{1,0:T(8,128)(2,1)S(1)} %prepare.1.refs_0_.dout_ref, bf16[1280,384]{1,0:T(8,128)(2,1)S(1)} %get-tuple-element.51.v_ref, bf16[6,512,256]{2,1,0:T(8,128)(2,1)S(1)} %get-tuple-element.71.probs_ref), custom_call_target="tpu_custom_call" | custom-call | flops 40000000000 | tf_op jit(solution)/shard_map/mix/pallas_call | solution.py:38
  57.7 1.1 %features.1 = bf16[256,768]{1,0:T(8,128)(2,1)} custom-call(bf16[256,768]{1,0:T(8,128)(2,1)S(1)} %bitcast.16, f32[256,768]{1,0:T(8,128)S(1)} %get-tuple-element.68.mine_ref, f32[256,768]{1,0:T(8,128)S(1)} %collective-permute-done.11.other_ref), custom_call_target="tpu_custom_call" | custom-call | flops 5000000000 | tf_op jit(solution)/shard_map/features/pallas_call | solution.py:38
  58.7 1.8 %collective-permute-done.12.refs_5_ = f32[3,96,128]{2,1,0:T(8,128)S(1)} collective-permute-done((f32[3,96,128]{2,1,0:T(8,128)S(1)}, f32[3,96,128]{2,1,0:T(8,128)S(1)}, u32[]{:S(2)}, u32[]{:S(2)}) %collective-permute-start.12) | collective-permute-done | bytes 147488 | tf_op jit(solution)/shard_map/ppermute | solution.py:414
  60.6 0.8 %join.1 = f32[3,96,384]{2,1,0:T(8,128)} custom-call(f32[3,96,128]{2,1,0:T(8,128)S(1)} %get-tuple-element.73.refs_0_, f32[3,96,128]{2,1,0:T(8,128)S(1)} %get-tuple-element.74.refs_1_, f32[3,96,128]{2,1,0:T(8,128)S(1)} %get-tuple-element.75.refs_2_, f32[3,96,128]{2,1,0:T(8,128)S(1)} %collective-permute-done.9.refs_3_, ...), custom_call_target="tpu_custom_call" | custom-call | tf_op jit(solution)/shard_map/join/pallas_call | solution.py:38
  (30 shorter events, 3.1 us)
Async XLA Ops:
  0.6 10.7 %copy-start.5 = (s32[1,256]{1,0:T(1,128)S(1)}, s32[1,256]{1,0:T(1,128)}, u32[]{:S(2)}) copy-start(s32[1,256]{1,0:T(1,128)} %param.11) | copy-start | bytes 3076
  1.6 10.0 %collective-permute-start = (bf16[128,768]{1,0:T(8,128)(2,1)S(1)}, bf16[128,768]{1,0:T(8,128)(2,1)S(1)}, u32[]{:S(2)}, u32[]{:S(2)}) collective-permute-start(bf16[128,768]{1,0:T(8,128)(2,1)S(1)} %dynamic-slice_bitcast_fusion), channel_id=1, source_target_pairs={{0,4},{4,0},{8,12},{12,8},{1,5},{5,1},{9,13},{13,9},{2,6},{6,2},{1... | collective-permute-start | bytes 589832 | tf_op jit(solution)/shard_map/ppermute | solution.py:411
  4.7 12.6 %collective-permute-start.3 = (bf16[128,768]{1,0:T(8,128)(2,1)S(1)}, bf16[128,768]{1,0:T(8,128)(2,1)S(1)}, u32[]{:S(2)}, u32[]{:S(2)}) collective-permute-start(bf16[128,768]{1,0:T(8,128)(2,1)S(1)} %dynamic-slice_bitcast_fusion), channel_id=1, source_target_pairs={{0,12},{4,8},{8,4},{12,0},{1,13},{5,9},{9,5},{13,1},{2,14},{6,10},... | collective-permute-start | bytes 589832 | tf_op jit(solution)/shard_map/ppermute | solution.py:411
  7.2 17.4 %collective-permute-start.2 = (bf16[128,768]{1,0:T(8,128)(2,1)S(1)}, bf16[128,768]{1,0:T(8,128)(2,1)S(1)}, u32[]{:S(2)}, u32[]{:S(2)}) collective-permute-start(bf16[128,768]{1,0:T(8,128)(2,1)S(1)} %dynamic-slice_bitcast_fusion), channel_id=1, source_target_pairs={{0,8},{4,12},{8,0},{12,4},{1,9},{5,13},{9,1},{13,5},{2,10},{6,14},... | collective-permute-start | bytes 589832 | tf_op jit(solution)/shard_map/ppermute | solution.py:411
  7.3 0.9 %copy-start.3 = (bf16[1,256,384]{2,1,0:T(8,128)(2,1)S(1)}, bf16[1,256,384]{2,1,0:T(8,128)(2,1)}, u32[]{:S(2)}) copy-start(bf16[1,256,384]{2,1,0:T(8,128)(2,1)} %param.7) | copy-start | bytes 589828
  8.2 0.7 %copy-start.4 = (s32[1,2,2]{2,1,0:T(2,128)S(1)}, s32[1,2,2]{2,1,0:T(2,128)}, u32[]{:S(2)}) copy-start(s32[1,2,2]{2,1,0:T(2,128)} %param.9) | copy-start | bytes 52
  8.9 2.8 %copy-start = (bf16[768,3,384]{2,0,1:T(8,128)(2,1)S(1)}, bf16[768,3,384]{2,0,1:T(8,128)(2,1)}, u32[]{:S(2)}) copy-start(bf16[768,3,384]{2,0,1:T(8,128)(2,1)} %param.8) | copy-start | bytes 5308420
  8.9 2.8 %copy-start.1 = (bf16[1,256,768]{2,1,0:T(8,128)(2,1)S(1)}, bf16[1,256,768]{2,1,0:T(8,128)(2,1)}, u32[]{:S(2)}) copy-start(bf16[1,256,768]{2,1,0:T(8,128)(2,1)} %param.6) | copy-start | bytes 1179652
  9.5 22.4 %collective-permute-start.6 = (bf16[272,384]{1,0:T(8,128)(2,1)S(1)}, bf16[272,384]{1,0:T(8,128)(2,1)S(1)}, u32[]{:S(2)}, u32[]{:S(2)}) collective-permute-start(bf16[272,384]{1,0:T(8,128)(2,1)S(1)} %prepare.1.refs_0_.dout_ref), channel_id=1, source_target_pairs={{0,4},{4,0},{8,12},{12,8},{1,5},{5,1},{9,13},{13,9},{2,6},{6,2},{1... | collective-permute-start | bytes 626696 | tf_op jit(solution)/shard_map/ppermute | solution.py:411
  11.6 1.5 %collective-permute-start.1 = (bf16[128,768]{1,0:T(8,128)(2,1)S(1)}, bf16[128,768]{1,0:T(8,128)(2,1)S(1)}, u32[]{:S(2)}, u32[]{:S(2)}) collective-permute-start(bf16[128,768]{1,0:T(8,128)(2,1)S(1)} %collective-permute-done.near_ref), channel_id=1, source_target_pairs={{0,1},{1,0},{2,3},{3,2},{4,5},{5,4},{6,7},{7,6},{8,9},{9,8},{10,11... | collective-permute-start | bytes 589832 | tf_op jit(solution)/shard_map/ppermute | solution.py:414
  24.5 14.5 %collective-permute-start.8 = (bf16[272,384]{1,0:T(8,128)(2,1)S(1)}, bf16[272,384]{1,0:T(8,128)(2,1)S(1)}, u32[]{:S(2)}, u32[]{:S(2)}) collective-permute-start(bf16[272,384]{1,0:T(8,128)(2,1)S(1)} %prepare.1.refs_0_.dout_ref), channel_id=1, source_target_pairs={{0,12},{4,8},{8,4},{12,0},{1,13},{5,9},{9,5},{13,1},{2,14},{6,10},... | collective-permute-start | bytes 626696 | tf_op jit(solution)/shard_map/ppermute | solution.py:411
  27.7 15.8 %collective-permute-start.7 = (bf16[272,384]{1,0:T(8,128)(2,1)S(1)}, bf16[272,384]{1,0:T(8,128)(2,1)S(1)}, u32[]{:S(2)}, u32[]{:S(2)}) collective-permute-start(bf16[272,384]{1,0:T(8,128)(2,1)S(1)} %prepare.1.refs_0_.dout_ref), channel_id=1, source_target_pairs={{0,8},{4,12},{8,0},{12,4},{1,9},{5,13},{9,1},{13,5},{2,10},{6,14},... | collective-permute-start | bytes 626696 | tf_op jit(solution)/shard_map/ppermute | solution.py:411
  27.7 1.4 %collective-permute-start.5 = (bf16[128,768]{1,0:T(8,128)(2,1)S(1)}, bf16[128,768]{1,0:T(8,128)(2,1)S(1)}, u32[]{:S(2)}, u32[]{:S(2)}) collective-permute-start(bf16[128,768]{1,0:T(8,128)(2,1)S(1)} %collective-permute-done.3.refs_9_), channel_id=1, source_target_pairs={{0,1},{1,0},{2,3},{3,2},{4,5},{5,4},{6,7},{7,6},{8,9},{9,8},{10,11... | collective-permute-start | bytes 589832 | tf_op jit(solution)/shard_map/ppermute | solution.py:414
  27.8 1.7 %collective-permute-start.4 = (bf16[128,768]{1,0:T(8,128)(2,1)S(1)}, bf16[128,768]{1,0:T(8,128)(2,1)S(1)}, u32[]{:S(2)}, u32[]{:S(2)}) collective-permute-start(bf16[128,768]{1,0:T(8,128)(2,1)S(1)} %collective-permute-done.2.refs_8_), channel_id=1, source_target_pairs={{0,1},{1,0},{2,3},{3,2},{4,5},{5,4},{6,7},{7,6},{8,9},{9,8},{10,11... | collective-permute-start | bytes 589832 | tf_op jit(solution)/shard_map/ppermute | solution.py:414
  29.5 2.4 %copy-start.2 = (s32[1,8]{1,0:T(1,128)S(1)}, s32[1,8]{1,0:T(1,128)}, u32[]{:S(2)}) copy-start(s32[1,8]{1,0:T(1,128)} %param.10) | copy-start | bytes 100
  46.2 9.7 %collective-permute-start.10 = (f32[3,96,128]{2,1,0:T(8,128)S(1)}, f32[3,96,128]{2,1,0:T(8,128)S(1)}, u32[]{:S(2)}, u32[]{:S(2)}) collective-permute-start(f32[3,96,128]{2,1,0:T(8,128)S(1)} %get-tuple-element.70), channel_id=1, source_target_pairs={{0,2},{2,0},{1,3},{3,1},{4,6},{6,4},{5,7},{7,5},{8,10},{10,8},{9,1... | collective-permute-start | bytes 442376 | tf_op jit(solution)/shard_map/ppermute | solution.py:414
  50.3 5.5 %collective-permute-start.9 = (f32[3,96,128]{2,1,0:T(8,128)S(1)}, f32[3,96,128]{2,1,0:T(8,128)S(1)}, u32[]{:S(2)}, u32[]{:S(2)}) collective-permute-start(f32[3,96,128]{2,1,0:T(8,128)S(1)} %get-tuple-element.69), channel_id=1, source_target_pairs={{0,2},{2,0},{1,3},{3,1},{4,6},{6,4},{5,7},{7,5},{8,10},{10,8},{9,1... | collective-permute-start | bytes 442376 | tf_op jit(solution)/shard_map/ppermute | solution.py:414
  54.2 3.5 %collective-permute-start.11 = (f32[256,768]{1,0:T(8,128)S(1)}, f32[256,768]{1,0:T(8,128)S(1)}, u32[]{:S(2)}, u32[]{:S(2)}) collective-permute-start(f32[256,768]{1,0:T(8,128)S(1)} %get-tuple-element.68.mine_ref), channel_id=1, source_target_pairs={{0,1},{1,0},{2,3},{3,2},{4,5},{5,4},{6,7},{7,6},{8,9},{9,8},{10,11... | collective-permute-start | bytes 2359304 | tf_op jit(solution)/shard_map/ppermute | solution.py:414
  54.3 6.3 %collective-permute-start.12 = (f32[3,96,128]{2,1,0:T(8,128)S(1)}, f32[3,96,128]{2,1,0:T(8,128)S(1)}, u32[]{:S(2)}, u32[]{:S(2)}) collective-permute-start(f32[3,96,128]{2,1,0:T(8,128)S(1)} %get-tuple-element.76), channel_id=1, source_target_pairs={{0,2},{2,0},{1,3},{3,1},{4,6},{6,4},{5,7},{7,5},{8,10},{10,8},{9,1... | collective-permute-start | bytes 442376 | tf_op jit(solution)/shard_map/ppermute | solution.py:414

commit v5 on v4

--- a/solution.py
+++ b/solution.py
@@ -137,16 +137,17 @@
 def read_pairs(fill_ref, dout_ref, nodes, clusters, lookups):
     tail = dout_ref[nodes:, :PAIR].astype(F32)
     lane = lax.broadcasted_iota(jnp.int32, tail.shape, 1)
-    base = fill_ref.shape[0]
+    bits = (fill_ref.shape[0] - 1).bit_length()
     weight = jnp.zeros(tail.shape, F32)
     for index in range(clusters * lookups):
-        weight = jnp.where(lane == index, float(base**index), weight)
+        weight = jnp.where(lane == index, float(1 << bits * index), weight)
     code = jnp.sum(tail * weight).astype(jnp.int32)
     me = lax.axis_index("seq")
     entries = []
     for index in range(clusters * lookups):
-        cluster = lax.rem(lax.div(code, base**index), base)
-        block = (lax.div(cluster, clusters) ^ me) * clusters + lax.rem(cluster, clusters)
+        cluster = (code >> (bits * index)) & ((1 << bits) - 1)
+        place = clusters.bit_length() - 1
+        block = ((cluster >> place) ^ me) * clusters + (cluster & (clusters - 1))
         entries.append((pl.multiple_of(block * GROUP_VERTICES, GROUP_VERTICES), fill_ref[cluster]))
     return [entries[i * lookups : (i + 1) * lookups] for i in range(clusters)]
 
@@ -164,8 +165,7 @@
     dk_ref, dv_ref = accs
     size = GROUP_VERTICES
     clusters = (dout_ref.shape[0] - TAIL) // size
-    local_rows = len(entries) * size
-    listed = local_rows + k_ref.shape[0] - total
+    listed = len(entries) * size + k_ref.shape[0] - total
     cols = slice(column, column + PAIR)
     state = {}
     places = [pl.ds(start, size) for start, _ in entries]
@@ -185,27 +185,24 @@
 
     def score_step(index):
         span = slice(index * size, (index + 1) * size)
-        score_ref[span, :] = dot(k_ref[places[index], cols], state["queries"], NT)
+        scores = dot(k_ref[places[index], cols], state["queries"], NT)
+        if index < len(entries):
+            slots = lax.broadcasted_iota(jnp.int32, scores.shape, 0)
+            scores = jnp.where(slots < entries[index][1], scores, -1e30)
+        score_ref[span, :] = scores
 
     def dprob_step(index):
         span = slice(index * size, (index + 1) * size)
         dprob_ref[span, :] = dot(v_ref[places[index], cols], state["douts"], NT)
 
-    def masked(start):
-        block = score_ref[start : start + CHUNK, :]
-        if start >= local_rows:
-            return block
-        slots = lax.broadcasted_iota(jnp.int32, (CHUNK, 2 * size), 0) + start % size
-        return jnp.where(slots < entries[start // size][1], block, -1e30)
-
     def peak_step(start):
-        part = fold(masked(start), jnp.maximum)
+        part = fold(score_ref[start : start + CHUNK, :], jnp.maximum)
         state["peak"] = part if start == 0 else jnp.maximum(state["peak"], part)
 
     def term_step(start):
         if start == 0:
             state["peak"] = jnp.max(state["peak"], 0, keepdims=True)
-        terms = jnp.exp2((masked(start) - state["peak"]) * (LOG2E * SCALE))
+        terms = jnp.exp2((score_ref[start : start + CHUNK, :] - state["peak"]) * (LOG2E * SCALE))
         weighted = fold(terms * dprob_ref[start : start + CHUNK, :], jnp.add)
         score_ref[start : start + CHUNK, :] = terms
         terms = fold(terms, jnp.add)
@@ -299,7 +296,24 @@
     run_units(units)
 
 
-def mix_kernel(total, lookups, fill_ref, dout_ref, v_ref, probs_ref, out_ref):
+def share_product(left_ref, all_ref, begin, end):
+    aligned = begin % TAIL == 0 and end % TAIL == 0
+    total = all_ref.shape[0]
+    sums = None
+    for start in range(0, total, 1024):
+        stop = min(start + 1024, total)
+        left = left_ref[begin:end, start:stop] if aligned else left_ref[:, start:stop]
+        term = dot(left, all_ref[start:stop, :])
+        sums = term if start == 0 else sums + term
+    return sums if aligned else sums[begin:end]
+
+
+def mix_kernel(total, lookups, fill_ref, dout_ref, v_ref, probs_ref, left_ref, *refs):
+    *all_refs, out_ref, mine_ref = refs
+    for index, all_ref in enumerate(all_refs):
+        sums = share_product(left_ref, all_ref, 0, mine_ref.shape[1])
+        for i in range(3):
+            mine_ref[i, :, index * PAIR : (index + 1) * PAIR] = sums[:, i * PAIR : (i + 1) * PAIR]
     size = GROUP_VERTICES
     nodes, width = out_ref.shape
     clusters = nodes // size
@@ -322,7 +336,7 @@
     own_refs = []
     if final:
         w_ref, own_refs, refs = refs[0], list(refs[1 : 1 + column // PAIR]), refs[1 + column // PAIR :]
-    mine_ref, other_ref, own_ref, dk_ref, dv_ref, dq_ref, all_ref = refs
+    other_ref, all_ref, *node_refs, dk_ref, dv_ref, dq_ref = refs
     cols = slice(column, column + PAIR)
     dk_ref[...] = dk_in[:, cols]
     dv_ref[...] = dv_in[:, cols]
@@ -342,7 +356,7 @@
             for cluster in range(clusters)
         ]
     )
-    share = mine_ref.shape[1]
+    share = left_ref.shape[0] - other_ref.shape[1]
     wide = jnp.concatenate([dk_ref[total:, :], dv_ref[total:, :]], 1)
     high = wide.astype(BF16)
     picked = jnp.concatenate([high, (wide - high.astype(F32)).astype(BF16)], 0)
@@ -354,24 +368,18 @@
         all_ref[span, :PAIR] = dq_ref[...] if block == shard else next(order)[:, cols]
         all_ref[span, PAIR : 2 * PAIR] = (dk_ref[span, :] + added[:, :PAIR]).astype(BF16)
         all_ref[span, 2 * PAIR :] = (dv_ref[span, :] + added[:, PAIR:]).astype(BF16)
-    sums = None
-    for start in range(0, total, BATCH * nodes):
-        stop = min(start + BATCH * nodes, total)
-        term = dot(left_ref[:, start:stop], all_ref[start:stop, :])
-        sums = term if start == 0 else sums + term
+    sums = share_product(left_ref, all_ref, share, left_ref.shape[0])
     for i in range(3):
-        mine_ref[i] = sums[:share, i * PAIR : (i + 1) * PAIR]
-        other_ref[i] = sums[share:, i * PAIR : (i + 1) * PAIR]
+        other_ref[i] = sums[:, i * PAIR : (i + 1) * PAIR]
     if not final:
-        own_ref[...] = all_ref[:nodes, :]
         return
     node = None
     for i in range(3):
         part = slice(i * PAIR, (i + 1) * PAIR)
-        grads = [ref[:, part] for ref in own_refs] + [all_ref[:nodes, part]]
+        grads = [ref[:nodes, part] for ref in own_refs] + [all_ref[:nodes, part]]
         term = dot(jnp.concatenate(grads, 1), w_ref[i], NT)
         node = term if node is None else node + term
-    own_ref[...] = node
+    node_refs[0][...] = node
 
 
 def features_kernel(x_ref, mine_ref, other_ref, out_ref):
@@ -382,12 +390,11 @@
     out_ref[...] = (inverse * (grad - normed * jnp.mean(normed * grad, -1, keepdims=True))).astype(BF16)
 
 
-def join_kernel(*refs):
+def join_kernel(mine_ref, *refs):
     out_ref = refs[-1]
-    half = (len(refs) - 1) // 2
-    for index in range(half):
+    for index, back_ref in enumerate(refs[:-1]):
         cols = slice(index * PAIR, (index + 1) * PAIR)
-        out_ref[:, :, cols] = refs[index][...] + refs[half + index][...]
+        out_ref[:, :, cols] = mine_ref[:, :, cols] + back_ref[...]
 
 
 def local(node_features, result_cotangent, proj_weights, cluster_pairs, cluster_fill, global_nodes):
@@ -469,7 +476,7 @@
         kept = got[2] if first else kept
         dqs.update(zip(group, got[-len(group) :]))
     last = steps[-1]
-    mine, other, grads = [], [], []
+    other, grads = [], []
     for column in range(0, half_width, PAIR):
         final = column + PAIR == half_width
         got = call(
@@ -478,38 +485,36 @@
             (q, douts[last], k, v, dk, dv, left, put)
             + tuple(dqs[i] for i in sorted(dqs)) + ((weights, *grads) if final else ()),
             (
-                shape(F32, 3, share, PAIR),
                 shape(F32, 3, (reps - 1) * share, PAIR),
-                shape(F32, nodes, width) if final else shape(BF16, nodes, 3 * PAIR),
-            ),
+                shape(BF16, total, 3 * PAIR),
+            ) + ((shape(F32, nodes, width),) if final else ()),
             (
                 pltpu.VMEM((total + count, PAIR), F32),
                 pltpu.VMEM((total + count, PAIR), F32),
                 pltpu.VMEM((nodes, PAIR), BF16),
-                pltpu.VMEM((total, 3 * PAIR), BF16),
             ) + scratch,
         )
-        mine.append(got[0])
-        other.append(got[1])
-        grads.append(got[2])
-    node_part = grads.pop()
+        other.append(got[0])
+        grads.append(got[1])
+    node_part = got[2]
     back = [swap(block, "rep") for block in other] if reps == 2 else [block for block in other]
     later, _ = lax.optimization_barrier((kept, (node_part, back[:-1])))
-    mixed = call(
-        functools.partial(mix_kernel, total, lookups), "mix", total, (fill,), (dout, v, later), (flat,), micros=40,
-    )[0]
+    mixed, mine = call(
+        functools.partial(mix_kernel, total, lookups), "mix", total, (fill,), (dout, v, later, left, *grads),
+        (flat, shape(F32, 3, share, half_width)), micros=40,
+    )
 
     grad_x = call(
         features_kernel, "features", total, (), (features, node_part, swap(node_part, "tp")),
         (shape(BF16, nodes, width),), micros=5,
     )[0]
     if reps == 2:
-        ready, _ = lax.optimization_barrier((mine[0], grad_x))
+        ready, _ = lax.optimization_barrier((mine, grad_x))
         grad_w = call(
-            join_kernel, "join", total, (), (ready, *mine[1:], *back), (shape(F32, 3, share, half_width),),
+            join_kernel, "join", total, (), (ready, *back), (shape(F32, 3, share, half_width),),
         )[0]
     else:
-        whole = jnp.concatenate([jnp.concatenate(mine, 2), jnp.concatenate(other, 2)], 1)
+        whole = jnp.concatenate([mine, jnp.concatenate(other, 2)], 1)
         whole = jnp.roll(whole, lax.axis_index("rep") * share, 1)
         grad_w = lax.psum_scatter(whole, "rep", scatter_dimension=1, tiled=True)
     return mixed[None], grad_x[None], jnp.transpose(grad_w, (1, 0, 2))

time: 61.5 us -> 61.3 us (level)
  no operation moved by 1% of the time
where the time goes in v5:
time: 61.3 us; the launch traced here: 61.1 us
  Pallas kernels  28.6 us (47%)
  starting transfers between devices  15.1 us (25%)
  waiting for transfers between devices  13.8 us (23%)
  local copies, waits for them, and re-layouts  2.7 us (4%)
  between operations  0.81 us (1%)
    pallas_call x12, Pallas kernels, call(): pl.pallas_call(kernel, out_shape=outs, in_specs=[SMEM] * len(scalars) + [...  28.6 us
    ppermute x6, waiting for transfers between devices, trade(): return lax.ppermute(value, 'seq', [(j, j ^ step) for j in range(shards)])  10.8 us
    ppermute x6, starting transfers between devices, trade(): return lax.ppermute(value, 'seq', [(j, j ^ step) for j in range(shards)])  10.8 us
    ppermute x7, starting transfers between devices, swap(): return lax.ppermute(value, axis, [(0, 1), (1, 0)])  4.37 us
    ppermute x7, waiting for transfers between devices, swap(): return lax.ppermute(value, axis, [(0, 1), (1, 0)])  3.01 us
    unnamed x12, local copies, waits for them, and re-layouts  1.62 us
  transfers between devices with their start and end apart: 13, of which 7 were waited for; matrix products, arithmetic and copies ran while one was open for 0% of the time, Pallas kernels for 41%

profile of v5, /device:TPU:0, one launch (start us, length us, event | category | flops | bytes accessed | tf_op | source)
XLA Modules:
  0.0 61.1 jit_solution(15286385559240748818)
XLA Ops:
  0.6 0.9 %dynamic-slice_bitcast_fusion = bf16[128,768]{1,0:T(8,128)(2,1)S(1)} fusion(bf16[1,256,768]{2,1,0:T(8,128)(2,1)} %param.6, s32[]{:T(128)S(6)} %select_n.39), kind=kLoop, calls=%fused_computation | loop fusion | bytes 393220 | tf_op jit(solution)/shard_map/dynamic_slice | solution.py:423
  1.6 3.1 %collective-permute-start = (bf16[128,768]{1,0:T(8,128)(2,1)S(1)}, bf16[128,768]{1,0:T(8,128)(2,1)S(1)}, u32[]{:S(2)}, u32[]{:S(2)}) collective-permute-start(bf16[128,768]{1,0:T(8,128)(2,1)S(1)} %dynamic-slice_bitcast_fusion), channel_id=1, source_target_pairs={{0,4},{4,0},{8,12},{12,8},{1,5},{5,1},{9,13},{13,9},{2,6},{6,2},{1... | collective-permute-start | bytes 589832 | tf_op jit(solution)/shard_map/ppermute | solution.py:418
  4.7 2.5 %collective-permute-start.3 = (bf16[128,768]{1,0:T(8,128)(2,1)S(1)}, bf16[128,768]{1,0:T(8,128)(2,1)S(1)}, u32[]{:S(2)}, u32[]{:S(2)}) collective-permute-start(bf16[128,768]{1,0:T(8,128)(2,1)S(1)} %dynamic-slice_bitcast_fusion), channel_id=1, source_target_pairs={{0,12},{4,8},{8,4},{12,0},{1,13},{5,9},{9,5},{13,1},{2,14},{6,10},... | collective-permute-start | bytes 589832 | tf_op jit(solution)/shard_map/ppermute | solution.py:418
  7.3 0.9 %copy-done.3 = bf16[1,256,384]{2,1,0:T(8,128)(2,1)S(1)} copy-done((bf16[1,256,384]{2,1,0:T(8,128)(2,1)S(1)}, bf16[1,256,384]{2,1,0:T(8,128)(2,1)}, u32[]{:S(2)}) %copy-start.3) | copy-done | bytes 196632
  8.2 0.7 %copy-done.4 = s32[1,2,2]{2,1,0:T(2,128)S(1)} copy-done((s32[1,2,2]{2,1,0:T(2,128)S(1)}, s32[1,2,2]{2,1,0:T(2,128)}, u32[]{:S(2)}) %copy-start.4) | copy-done | bytes 40
  9.5 1.9 %collective-permute-start.6 = (bf16[272,384]{1,0:T(8,128)(2,1)S(1)}, bf16[272,384]{1,0:T(8,128)(2,1)S(1)}, u32[]{:S(2)}, u32[]{:S(2)}) collective-permute-start(bf16[272,384]{1,0:T(8,128)(2,1)S(1)} %prepare.1.refs_0_.dout_ref), channel_id=1, source_target_pairs={{0,4},{4,0},{8,12},{12,8},{1,5},{5,1},{9,13},{13,9},{2,6},{6,2},{1... | collective-permute-start | bytes 626696 | tf_op jit(solution)/shard_map/ppermute | solution.py:418
  11.7 1.1 %project_first.1 = (bf16[256,384]{1,0:T(8,128)(2,1)S(1)}, bf16[256,384]{1,0:T(8,128)(2,1)S(1)}, bf16[256,384]{1,0:T(8,128)(2,1)S(1)}, bf16[192,256]{1,0:T(8,128)...) custom-call(s32[1,256]{1,0:T(1,128)S(1)} %fusion.7.row_ref, s32[256,1]{1,0:T(8,128)S(1)} %fusion.2.col_ref, ...), custom_call_target="tpu_custom_call" | custom-call | flops 2000000000 | tf_op jit(solution)/shard_map/project_first/pallas_call | solution.py:38
  13.1 1.0 %project_next.1 = (bf16[256,384]{1,0:T(8,128)(2,1)S(1)}, bf16[256,384]{1,0:T(8,128)(2,1)S(1)}, bf16[256,384]{1,0:T(8,128)(2,1)S(1)}, bf16[192,256]{1,0:T(8,128)(2,1)S(1)}) custom-call(bf16[3,768,384]{2,1,0:T(8,128)(2,1)S(1)} %bitcast.12, bf16[128,768]{1,0:T(8,128)(2,1)S(1)} %collective-permute-done.near_ref, bf16[128,768]{1,0:T(8,128)(2,1)S(1)} %collective-permute-done.1.far_ref), custom_call_target="tpu_custom_call" | custom-call | flops 2000000000 | tf_op jit(solution)/shard_map/project_next/pallas_call | solution.py:38
  14.1 3.1 %collective-permute-done.3.refs_9_ = bf16[128,768]{1,0:T(8,128)(2,1)S(1)} collective-permute-done((bf16[128,768]{1,0:T(8,128)(2,1)S(1)}, bf16[128,768]{1,0:T(8,128)(2,1)S(1)}, u32[]{:S(2)}, u32[]{:S(2)}) %collective-permute-start.3) | collective-permute-done | bytes 196640 | tf_op jit(solution)/shard_map/ppermute | solution.py:418
  17.2 7.3 %collective-permute-done.2.refs_8_ = bf16[128,768]{1,0:T(8,128)(2,1)S(1)} collective-permute-done((bf16[128,768]{1,0:T(8,128)(2,1)S(1)}, bf16[128,768]{1,0:T(8,128)(2,1)S(1)}, u32[]{:S(2)}, u32[]{:S(2)}) %collective-permute-start.2) | collective-permute-done | bytes 196640 | tf_op jit(solution)/shard_map/ppermute | solution.py:418
  24.5 3.2 %collective-permute-start.8 = (bf16[272,384]{1,0:T(8,128)(2,1)S(1)}, bf16[272,384]{1,0:T(8,128)(2,1)S(1)}, u32[]{:S(2)}, u32[]{:S(2)}) collective-permute-start(bf16[272,384]{1,0:T(8,128)(2,1)S(1)} %prepare.1.refs_0_.dout_ref), channel_id=1, source_target_pairs={{0,12},{4,8},{8,4},{12,0},{1,13},{5,9},{9,5},{13,1},{2,14},{6,10},... | collective-permute-start | bytes 626696 | tf_op jit(solution)/shard_map/ppermute | solution.py:418
  28.3 0.9 %collective-permute-done.5.refs_11_ = bf16[128,768]{1,0:T(8,128)(2,1)S(1)} collective-permute-done((bf16[128,768]{1,0:T(8,128)(2,1)S(1)}, bf16[128,768]{1,0:T(8,128)(2,1)S(1)}, u32[]{:S(2)}, u32[]{:S(2)}) %collective-permute-start.5) | collective-permute-done | bytes 196640 | tf_op jit(solution)/shard_map/ppermute | solution.py:421
  29.5 2.4 %project.1 = (bf16[1024,384]{1,0:T(8,128)(2,1)S(1)}, bf16[1280,384]{1,0:T(8,128)(2,1)S(1)}, bf16[1280,384]{1,0:T(8,128)(2,1)S(1)}, bf16[192,1024]{1,0:T(8,128)(2,1)S(1)}) custom-call(bf16[3,768,384]{2,1,0:T(8,128)(2,1)S(1)} %bitcast.13, bf16[256,1024]{1,0:T(8,128)(2,1)S(1)} %get-tuple-element.40.pick_ref, bf16[256,384]{1,0:T(8,128)(2,1)S(1)} %get-tuple-element.41.refs_0_, ...), custom_call_target="tpu_custom_call" | custom-call | tf_op jit(solution)/shard_map/project/pallas_call | solution.py:38
  31.9 7.1 %attend_1.1 = (f32[1280,384]{1,0:T(8,128)S(1)}, f32[1280,384]{1,0:T(8,128)S(1)}, bf16[6,512,256]{2,1,0:T(8,128)(2,1)S(1)}, bf16[256,384]{1,0:T(8,128)(2,1)S(1)}, bf16[256,384]{1,0:T(8,128)(2,1)S(1)}) custom-call(s32[8]{0:T(128)S(1)} %bitcast.17, bf16[1024,384]{1,0:T(8,128)(2,1)S(1)} %get-tuple-element.52.q_ref, ...), custom_call_target="tpu_custom_call" | custom-call | tf_op jit(solution)/shard_map/attend_1/pallas_call | solution.py:38
  39.0 4.2 %attend_3.1 = (f32[1280,384]{1,0:T(8,128)S(1)}, f32[1280,384]{1,0:T(8,128)S(1)}, bf16[256,384]{1,0:T(8,128)(2,1)S(1)}) custom-call(s32[8]{0:T(128)S(1)} %bitcast.18, bf16[1024,384]{1,0:T(8,128)(2,1)S(1)} %get-tuple-element.52.q_ref, bf16[1280,384]{1,0:T(8,128)(2,1)S(1)} %get-tuple-element.53.k_ref, bf16[1280,384]{1,0:T(8,128)(2,1)S(1)} %get-tuple-element.51.v_ref, ...), custom_call_target="tpu_custom_call" | custom-call | tf_op jit(solution)/shard_map/attend_3/pallas_call | solution.py:38
  43.6 2.5 %finish_128.1 = (f32[3,96,128]{2,1,0:T(8,128)S(1)}, bf16[1024,384]{1,0:T(8,128)(2,1)S(1)}) custom-call(s32[8]{0:T(128)S(1)} %bitcast.19, bf16[1024,384]{1,0:T(8,128)(2,1)S(1)} %get-tuple-element.52.q_ref, bf16[272,384]{1,0:T(8,128)(2,1)S(1)} %collective-permute-done.7.dout_ref, bf16[1280,384]{1,0:T(8,128)(2,1)S(1)} %get-tuple-element.53.k_ref, ...), custom_call_target="tpu_custom_call" | custom-call | tf_op jit(solution)/shard_map/finish_128/pallas_call | solution.py:38
  46.0 1.6 %collective-permute-start.10 = (f32[3,96,128]{2,1,0:T(8,128)S(1)}, f32[3,96,128]{2,1,0:T(8,128)S(1)}, u32[]{:S(2)}, u32[]{:S(2)}) collective-permute-start(f32[3,96,128]{2,1,0:T(8,128)S(1)} %get-tuple-element.70), channel_id=1, source_target_pairs={{0,2},{2,0},{1,3},{3,1},{4,6},{6,4},{5,7},{7,5},{8,10},{10,8},{9,1... | collective-permute-start | bytes 442376 | tf_op jit(solution)/shard_map/ppermute | solution.py:421
  47.6 2.5 %finish_0.1 = (f32[3,96,128]{2,1,0:T(8,128)S(1)}, bf16[1024,384]{1,0:T(8,128)(2,1)S(1)}) custom-call(s32[8]{0:T(128)S(1)} %bitcast.20, bf16[1024,384]{1,0:T(8,128)(2,1)S(1)} %get-tuple-element.52.q_ref, bf16[272,384]{1,0:T(8,128)(2,1)S(1)} %collective-permute-done.7.dout_ref, bf16[1280,384]{1,0:T(8,128)(2,1)S(1)} %get-tuple-element.53.k_ref, ...), custom_call_target="tpu_custom_call" | custom-call | tf_op jit(solution)/shard_map/finish_0/pallas_call | solution.py:38
  50.7 3.3 %finish_256.1 = (f32[3,96,128]{2,1,0:T(8,128)S(1)}, bf16[1024,384]{1,0:T(8,128)(2,1)S(1)}, f32[256,768]{1,0:T(8,128)S(1)}) custom-call(s32[8]{0:T(128)S(1)} %bitcast.21, bf16[1024,384]{1,0:T(8,128)(2,1)S(1)} %get-tuple-element.52.q_ref, bf16[272,384]{1,0:T(8,128)(2,1)S(1)} %collective-permute-done.7.dout_ref, bf16[1280,384]{1,0:T(8,128)(2,1)S(1)} %get-tuple-element.53.k_ref, ...), custom_call_target="tpu_custom_call" | custom-call | tf_op jit(solution)/shard_map/finish_256/pallas_call | solution.py:38
  54.0 1.6 %collective-permute-start.12 = (f32[3,96,128]{2,1,0:T(8,128)S(1)}, f32[3,96,128]{2,1,0:T(8,128)S(1)}, u32[]{:S(2)}, u32[]{:S(2)}) collective-permute-start(f32[3,96,128]{2,1,0:T(8,128)S(1)} %get-tuple-element.76), channel_id=1, source_target_pairs={{0,2},{2,0},{1,3},{3,1},{4,6},{6,4},{5,7},{7,5},{8,10},{10,8},{9,1... | collective-permute-start | bytes 442376 | tf_op jit(solution)/shard_map/ppermute | solution.py:421
  55.6 2.1 %mix.1 = (bf16[256,384]{1,0:T(8,128)(2,1)}, f32[3,96,384]{2,1,0:T(8,128)S(1)}) custom-call(s32[8]{0:T(128)S(1)} %bitcast.22, bf16[272,384]{1,0:T(8,128)(2,1)S(1)} %prepare.1.refs_0_.dout_ref, bf16[1280,384]{1,0:T(8,128)(2,1)S(1)} %get-tuple-element.51.v_ref, bf16[6,512,256]{2,1,0:T(8,128)(2,1)S(1)} %get-tuple-element.71.probs_ref, ...), custom_call_target="tpu_custom_call" | custom-call | flops 40000000000 | tf_op jit(solution)/shard_map/mix/pallas_call | solution.py:38
  57.7 1.1 %features.1 = bf16[256,768]{1,0:T(8,128)(2,1)} custom-call(bf16[256,768]{1,0:T(8,128)(2,1)S(1)} %bitcast.16, f32[256,768]{1,0:T(8,128)S(1)} %get-tuple-element.68.mine_ref, f32[256,768]{1,0:T(8,128)S(1)} %collective-permute-done.11.other_ref), custom_call_target="tpu_custom_call" | custom-call | flops 5000000000 | tf_op jit(solution)/shard_map/features/pallas_call | solution.py:38
  58.7 1.5 %collective-permute-done.12.refs_2_ = f32[3,96,128]{2,1,0:T(8,128)S(1)} collective-permute-done((f32[3,96,128]{2,1,0:T(8,128)S(1)}, f32[3,96,128]{2,1,0:T(8,128)S(1)}, u32[]{:S(2)}, u32[]{:S(2)}) %collective-permute-start.12) | collective-permute-done | bytes 147488 | tf_op jit(solution)/shard_map/ppermute | solution.py:421
  60.3 0.8 %join.1 = f32[3,96,384]{2,1,0:T(8,128)} custom-call(f32[3,96,384]{2,1,0:T(8,128)S(1)} %get-tuple-element.75.mine_ref, f32[3,96,128]{2,1,0:T(8,128)S(1)} %collective-permute-done.9.refs_0_, f32[3,96,128]{2,1,0:T(8,128)S(1)} %collective-permute-done.10.refs_1_, f32[3,96,128]{2,1,0:T(8,128)S(1)} %collective-permute-done.12.refs_2_), custom_call_target="tpu_custom_call" | custom-call | tf_op jit(solution)/shard_map/join/pallas_call | solution.py:38
  (30 shorter events, 3.1 us)
Async XLA Ops:
  0.6 10.7 %copy-start.5 = (s32[1,256]{1,0:T(1,128)S(1)}, s32[1,256]{1,0:T(1,128)}, u32[]{:S(2)}) copy-start(s32[1,256]{1,0:T(1,128)} %param.11) | copy-start | bytes 3076
  1.6 10.0 %collective-permute-start = (bf16[128,768]{1,0:T(8,128)(2,1)S(1)}, bf16[128,768]{1,0:T(8,128)(2,1)S(1)}, u32[]{:S(2)}, u32[]{:S(2)}) collective-permute-start(bf16[128,768]{1,0:T(8,128)(2,1)S(1)} %dynamic-slice_bitcast_fusion), channel_id=1, source_target_pairs={{0,4},{4,0},{8,12},{12,8},{1,5},{5,1},{9,13},{13,9},{2,6},{6,2},{1... | collective-permute-start | bytes 589832 | tf_op jit(solution)/shard_map/ppermute | solution.py:418
  4.7 12.6 %collective-permute-start.3 = (bf16[128,768]{1,0:T(8,128)(2,1)S(1)}, bf16[128,768]{1,0:T(8,128)(2,1)S(1)}, u32[]{:S(2)}, u32[]{:S(2)}) collective-permute-start(bf16[128,768]{1,0:T(8,128)(2,1)S(1)} %dynamic-slice_bitcast_fusion), channel_id=1, source_target_pairs={{0,12},{4,8},{8,4},{12,0},{1,13},{5,9},{9,5},{13,1},{2,14},{6,10},... | collective-permute-start | bytes 589832 | tf_op jit(solution)/shard_map/ppermute | solution.py:418
  7.2 17.4 %collective-permute-start.2 = (bf16[128,768]{1,0:T(8,128)(2,1)S(1)}, bf16[128,768]{1,0:T(8,128)(2,1)S(1)}, u32[]{:S(2)}, u32[]{:S(2)}) collective-permute-start(bf16[128,768]{1,0:T(8,128)(2,1)S(1)} %dynamic-slice_bitcast_fusion), channel_id=1, source_target_pairs={{0,8},{4,12},{8,0},{12,4},{1,9},{5,13},{9,1},{13,5},{2,10},{6,14},... | collective-permute-start | bytes 589832 | tf_op jit(solution)/shard_map/ppermute | solution.py:418
  7.3 0.9 %copy-start.3 = (bf16[1,256,384]{2,1,0:T(8,128)(2,1)S(1)}, bf16[1,256,384]{2,1,0:T(8,128)(2,1)}, u32[]{:S(2)}) copy-start(bf16[1,256,384]{2,1,0:T(8,128)(2,1)} %param.7) | copy-start | bytes 589828
  8.2 0.7 %copy-start.4 = (s32[1,2,2]{2,1,0:T(2,128)S(1)}, s32[1,2,2]{2,1,0:T(2,128)}, u32[]{:S(2)}) copy-start(s32[1,2,2]{2,1,0:T(2,128)} %param.9) | copy-start | bytes 52
  8.9 2.8 %copy-start = (bf16[768,3,384]{2,0,1:T(8,128)(2,1)S(1)}, bf16[768,3,384]{2,0,1:T(8,128)(2,1)}, u32[]{:S(2)}) copy-start(bf16[768,3,384]{2,0,1:T(8,128)(2,1)} %param.8) | copy-start | bytes 5308420
  8.9 2.8 %copy-start.1 = (bf16[1,256,768]{2,1,0:T(8,128)(2,1)S(1)}, bf16[1,256,768]{2,1,0:T(8,128)(2,1)}, u32[]{:S(2)}) copy-start(bf16[1,256,768]{2,1,0:T(8,128)(2,1)} %param.6) | copy-start | bytes 1179652
  9.5 22.4 %collective-permute-start.6 = (bf16[272,384]{1,0:T(8,128)(2,1)S(1)}, bf16[272,384]{1,0:T(8,128)(2,1)S(1)}, u32[]{:S(2)}, u32[]{:S(2)}) collective-permute-start(bf16[272,384]{1,0:T(8,128)(2,1)S(1)} %prepare.1.refs_0_.dout_ref), channel_id=1, source_target_pairs={{0,4},{4,0},{8,12},{12,8},{1,5},{5,1},{9,13},{13,9},{2,6},{6,2},{1... | collective-permute-start | bytes 626696 | tf_op jit(solution)/shard_map/ppermute | solution.py:418
  11.6 1.5 %collective-permute-start.1 = (bf16[128,768]{1,0:T(8,128)(2,1)S(1)}, bf16[128,768]{1,0:T(8,128)(2,1)S(1)}, u32[]{:S(2)}, u32[]{:S(2)}) collective-permute-start(bf16[128,768]{1,0:T(8,128)(2,1)S(1)} %collective-permute-done.near_ref), channel_id=1, source_target_pairs={{0,1},{1,0},{2,3},{3,2},{4,5},{5,4},{6,7},{7,6},{8,9},{9,8},{10,11... | collective-permute-start | bytes 589832 | tf_op jit(solution)/shard_map/ppermute | solution.py:421
  24.5 14.5 %collective-permute-start.8 = (bf16[272,384]{1,0:T(8,128)(2,1)S(1)}, bf16[272,384]{1,0:T(8,128)(2,1)S(1)}, u32[]{:S(2)}, u32[]{:S(2)}) collective-permute-start(bf16[272,384]{1,0:T(8,128)(2,1)S(1)} %prepare.1.refs_0_.dout_ref), channel_id=1, source_target_pairs={{0,12},{4,8},{8,4},{12,0},{1,13},{5,9},{9,5},{13,1},{2,14},{6,10},... | collective-permute-start | bytes 626696 | tf_op jit(solution)/shard_map/ppermute | solution.py:418
  27.7 15.8 %collective-permute-start.7 = (bf16[272,384]{1,0:T(8,128)(2,1)S(1)}, bf16[272,384]{1,0:T(8,128)(2,1)S(1)}, u32[]{:S(2)}, u32[]{:S(2)}) collective-permute-start(bf16[272,384]{1,0:T(8,128)(2,1)S(1)} %prepare.1.refs_0_.dout_ref), channel_id=1, source_target_pairs={{0,8},{4,12},{8,0},{12,4},{1,9},{5,13},{9,1},{13,5},{2,10},{6,14},... | collective-permute-start | bytes 626696 | tf_op jit(solution)/shard_map/ppermute | solution.py:418
  27.7 1.4 %collective-permute-start.5 = (bf16[128,768]{1,0:T(8,128)(2,1)S(1)}, bf16[128,768]{1,0:T(8,128)(2,1)S(1)}, u32[]{:S(2)}, u32[]{:S(2)}) collective-permute-start(bf16[128,768]{1,0:T(8,128)(2,1)S(1)} %collective-permute-done.3.refs_9_), channel_id=1, source_target_pairs={{0,1},{1,0},{2,3},{3,2},{4,5},{5,4},{6,7},{7,6},{8,9},{9,8},{10,11... | collective-permute-start | bytes 589832 | tf_op jit(solution)/shard_map/ppermute | solution.py:421
  27.8 1.7 %collective-permute-start.4 = (bf16[128,768]{1,0:T(8,128)(2,1)S(1)}, bf16[128,768]{1,0:T(8,128)(2,1)S(1)}, u32[]{:S(2)}, u32[]{:S(2)}) collective-permute-start(bf16[128,768]{1,0:T(8,128)(2,1)S(1)} %collective-permute-done.2.refs_8_), channel_id=1, source_target_pairs={{0,1},{1,0},{2,3},{3,2},{4,5},{5,4},{6,7},{7,6},{8,9},{9,8},{10,11... | collective-permute-start | bytes 589832 | tf_op jit(solution)/shard_map/ppermute | solution.py:421
  29.5 2.4 %copy-start.2 = (s32[1,8]{1,0:T(1,128)S(1)}, s32[1,8]{1,0:T(1,128)}, u32[]{:S(2)}) copy-start(s32[1,8]{1,0:T(1,128)} %param.10) | copy-start | bytes 100
  46.0 9.5 %collective-permute-start.10 = (f32[3,96,128]{2,1,0:T(8,128)S(1)}, f32[3,96,128]{2,1,0:T(8,128)S(1)}, u32[]{:S(2)}, u32[]{:S(2)}) collective-permute-start(f32[3,96,128]{2,1,0:T(8,128)S(1)} %get-tuple-element.70), channel_id=1, source_target_pairs={{0,2},{2,0},{1,3},{3,1},{4,6},{6,4},{5,7},{7,5},{8,10},{10,8},{9,1... | collective-permute-start | bytes 442376 | tf_op jit(solution)/shard_map/ppermute | solution.py:421
  50.1 5.5 %collective-permute-start.9 = (f32[3,96,128]{2,1,0:T(8,128)S(1)}, f32[3,96,128]{2,1,0:T(8,128)S(1)}, u32[]{:S(2)}, u32[]{:S(2)}) collective-permute-start(f32[3,96,128]{2,1,0:T(8,128)S(1)} %get-tuple-element.69), channel_id=1, source_target_pairs={{0,2},{2,0},{1,3},{3,1},{4,6},{6,4},{5,7},{7,5},{8,10},{10,8},{9,1... | collective-permute-start | bytes 442376 | tf_op jit(solution)/shard_map/ppermute | solution.py:421
  53.9 3.7 %collective-permute-start.11 = (f32[256,768]{1,0:T(8,128)S(1)}, f32[256,768]{1,0:T(8,128)S(1)}, u32[]{:S(2)}, u32[]{:S(2)}) collective-permute-start(f32[256,768]{1,0:T(8,128)S(1)} %get-tuple-element.68.mine_ref), channel_id=1, source_target_pairs={{0,1},{1,0},{2,3},{3,2},{4,5},{5,4},{6,7},{7,6},{8,9},{9,8},{10,11... | collective-permute-start | bytes 2359304 | tf_op jit(solution)/shard_map/ppermute | solution.py:421
  54.0 6.3 %collective-permute-start.12 = (f32[3,96,128]{2,1,0:T(8,128)S(1)}, f32[3,96,128]{2,1,0:T(8,128)S(1)}, u32[]{:S(2)}, u32[]{:S(2)}) collective-permute-start(f32[3,96,128]{2,1,0:T(8,128)S(1)} %get-tuple-element.76), channel_id=1, source_target_pairs={{0,2},{2,0},{1,3},{3,1},{4,6},{6,4},{5,7},{7,5},{8,10},{10,8},{9,1... | collective-permute-start | bytes 442376 | tf_op jit(solution)/shard_map/ppermute | solution.py:421
